TPU v7x, 128 devices: a whole 4x4x4 slice. The times are simulated.
128 devices in a mesh: bx: 8 (over y, z_hi), by: 16 (over x, z_lo, core).
Axes of the slice: x: 4, y: 4, z: 4 (z_hi: 2, z_lo: 2; z = z_hi * 2 + z_lo), core: 2. Of those that a mesh axis runs over, the one named last changes fastest.
Arguments:
- populations: float32 [27, 128, 256, 128], P(None, 'bx', 'by'), as said below
- block_level: int32 [1024], replicated, may hold values 0 or 1
- new_slot: int32 [1024], P(('bx', 'by')), may hold values from 0 to 1023, as said below
Outputs:
- density: float32 [1024, 4096], P(('bx', 'by'))
- velocity: float32 [3, 1024, 4096], P(None, ('bx', 'by'))
Inputs may be any that keep to these rules, and one draw needn't show every extreme that they name: `populations`: every population is positive. new_slot is a permutation; slot s belongs to device s // 8 in the curve order, which is the order of bx+by. Every block stays at its slot or moves to the next or the previous device in that order; at most one block of a device goes to each of those two devices, and it takes the slot of the block that crosses the same cut the other way. Some cut is crossed in every draw.
All inputs are finite; a program needn't handle non-finite values.
Results may differ from a plain program's by a relative error of at most 0.0003.
Values sent between devices are 32-bit elements; how exact they have to be, the bound alone decides.
No kernel may reach another device: no remote copies, remote signals or barrier semaphores. Data moves between devices by JAX's collectives and lax.ppermute only.
A program may use at most 192 MiB of HBM per device.

v0:
```python
import math

import jax
import jax.numpy as jnp
import numpy as np
from jax import lax
from jax.sharding import PartitionSpec as P

lattice_vel = np.array(
    [
        [first, second, third]
        for first in (-1, 0, 1)
        for second in (-1, 0, 1)
        for third in (-1, 0, 1)
    ],
    dtype=np.float32,
)
lattice_sq = np.sum(lattice_vel * lattice_vel, axis=1)
lattice_wts = np.where(
    lattice_sq == 0,
    8.0 / 27,
    np.where(lattice_sq == 1, 2.0 / 27, np.where(lattice_sq == 2, 1.0 / 54, 1.0 / 216)),
).astype(np.float32)
stress_table = np.stack(
    [lattice_vel[:, first] * lattice_vel[:, second] for first in range(3) for second in range(3)]
).astype(np.float32)
tau_coarse = 0.56
tau_fine = 0.62
scale_to_fine = tau_fine / (2.0 * tau_coarse)
scale_to_coarse = 2.0 * tau_coarse / tau_fine
smagorinsky = 18.0 * math.sqrt(2.0) * 0.17 * 0.17


def extended(cells, sides, width):
    for axis, dim in sides:
        count = lax.axis_size(axis)
        head = lax.slice_in_dim(cells, 0, width, axis=dim)
        tail = lax.slice_in_dim(cells, cells.shape[dim] - width, cells.shape[dim], axis=dim)
        cells = jnp.concatenate(
            [
                lax.ppermute(tail, axis, [(i, (i + 1) % count) for i in range(count)]),
                cells,
                lax.ppermute(head, axis, [((i + 1) % count, i) for i in range(count)]),
            ],
            axis=dim,
        )
    return cells


def shifted(value, axis, by):
    devices = lax.axis_size(axis)
    pairs = [(i, i + by) for i in range(devices) if 0 <= i + by < devices]
    return lax.ppermute(value, axis, pairs)


def cell_moments(states):
    density = jnp.sum(states, axis=0)
    momentum = jnp.einsum(
        "ia,i...->a...", jnp.asarray(lattice_vel), states, precision=lax.Precision.HIGHEST
    )
    return (density, momentum / density)


def equilibrium(density, velocity):
    projected = jnp.einsum(
        "ia,a...->i...", jnp.asarray(lattice_vel), velocity, precision=lax.Precision.HIGHEST
    )
    speed_sq = jnp.sum(velocity * velocity, axis=0)
    weights = jnp.asarray(lattice_wts).reshape((27,) + (1,) * density.ndim)
    return (
        weights * density * (1.0 + 3.0 * projected + 4.5 * projected * projected - 1.5 * speed_sq)
    )


def relax_cells(states, fine_cells, active_cells):
    density, velocity = cell_moments(states)
    balance = equilibrium(density, velocity)
    departure = states - balance
    stress = jnp.einsum(
        "ki,i...->k...", jnp.asarray(stress_table), departure, precision=lax.Precision.HIGHEST
    )
    stress_norm = jnp.sqrt(jnp.sum(stress * stress, axis=0))
    base_time = jnp.where(fine_cells, tau_fine, tau_coarse)
    relax_time = 0.5 * (
        base_time + jnp.sqrt(base_time * base_time + smagorinsky * stress_norm / density)
    )
    relaxed = jnp.where(active_cells, states - departure / relax_time, states)
    factor = jnp.where(fine_cells, scale_to_coarse, scale_to_fine)
    rescaled = balance + factor * (relaxed - balance)
    return (relaxed, rescaled)


def coarse_only(states):
    density, velocity = cell_moments(states)
    balance = equilibrium(density, velocity)
    factor = jnp.full(density.shape, scale_to_fine, states.dtype)
    rescaled = balance + factor * (states - balance)
    return (states, rescaled)


def exchange_faces(outgoing):
    return extended(outgoing, (("bx", 1), ("by", 2)), 1)


def stream_cells(padded, size_x, size_y):
    moved = []
    for direction in range(27):
        shift_x, shift_y, shift_z = (int(value) for value in lattice_vel[direction])
        window = padded[
            direction, 1 - shift_x : 1 - shift_x + size_x, 1 - shift_y : 1 - shift_y + size_y
        ]
        moved.append(jnp.roll(window, shift_z, axis=2))
    return jnp.stack(moved)


def block_fields(fields, blocks):
    channels, size_x, size_y, size_z = fields.shape
    edge = size_z // blocks
    split = fields.reshape(channels, size_x, size_y, blocks, edge)
    return split.transpose(3, 0, 1, 2, 4).reshape(blocks, channels, size_x * size_y * edge)


def on_device(populations, block_level, new_slot):
    count_x = lax.axis_size("bx")
    count_y = lax.axis_size("by")
    index_x = lax.axis_index("bx")
    index_y = lax.axis_index("by")
    blocks = new_slot.shape[0]
    size_x = populations.shape[1]
    size_y = populations.shape[2]
    size_z = populations.shape[3]
    edge = size_z // blocks
    levels = block_level.reshape(count_x, count_y, blocks)
    offsets = jnp.array([-1, 0, 1], jnp.int32)
    rows_x = (index_x + offsets) % count_x
    rows_y = (index_y + offsets) % count_y
    nearby = jnp.take(jnp.take(levels, rows_x, axis=0), rows_y, axis=1)
    pick_x = np.array([0] + [1] * size_x + [2])
    pick_y = np.array([0] + [1] * size_y + [2])
    pick_z = np.arange(size_z) // edge
    level_pad = nearby[pick_x][:, pick_y][:, :, pick_z]
    own_level = level_pad[1 : size_x + 1, 1 : size_y + 1]
    fine_cells = own_level == 1
    crossing = jnp.stack(
        [
            jnp.roll(
                level_pad[
                    1 + int(offset[0]) : 1 + int(offset[0]) + size_x,
                    1 + int(offset[1]) : 1 + int(offset[1]) + size_y,
                ],
                -int(offset[2]),
                axis=2,
            )
            != own_level
            for offset in lattice_vel
        ]
    )
    any_fine = jnp.any(fine_cells)
    every = jnp.ones_like(fine_cells)

    def relax_fine(states):
        return relax_cells(states, fine_cells, fine_cells)

    state = populations
    for substep in range(2):
        if substep == 0:
            relaxed, rescaled = lax.cond(any_fine, relax_fine, coarse_only, state)
        else:
            relaxed, rescaled = relax_cells(state, fine_cells, every)
        outgoing = jnp.where(crossing, rescaled, relaxed)
        padded = exchange_faces(outgoing)
        if substep == 0:

            def advance(current):
                return jnp.where(fine_cells, stream_cells(padded, size_x, size_y), current)

            def keep(current):
                return current

            state = lax.cond(any_fine, advance, keep, state)
        else:
            state = stream_cells(padded, size_x, size_y)
    curve = index_x * count_y + index_y
    target = new_slot // blocks
    to_next = target == curve + 1
    to_prev = target == curve - 1
    payload = block_fields(state, blocks)
    send_next = jnp.sum(jnp.where(to_next[:, None, None], payload, 0.0), axis=0)
    send_prev = jnp.sum(jnp.where(to_prev[:, None, None], payload, 0.0), axis=0)
    from_prev = shifted(send_next, ("bx", "by"), 1)
    from_next = shifted(send_prev, ("bx", "by"), -1)
    arrived = jnp.where(
        to_prev[:, None, None],
        from_prev[None],
        jnp.where(to_next[:, None, None], from_next[None], payload),
    )
    density, velocity = cell_moments(arrived.transpose(1, 0, 2))
    return (density, velocity)


def solution(mesh):
    in_specs = (P(None, "bx", "by", None), P(), P(("bx", "by")))
    out_specs = (P(("bx", "by"), None), P(None, ("bx", "by"), None))
    return jax.shard_map(
        on_device, mesh=mesh, in_specs=in_specs, out_specs=out_specs, check_vma=False
    )
```

profile of v0, /device:TPU:16, one launch (start us, length us, event | category | flops | bytes accessed | tf_op | source)
XLA Modules:
  0.0 378.3 jit_solution(10822315842688208113)
XLA Ops:
  51.9 32.1 %conditional.2 = (f32[27,16,16,128]{3,0,2,1:T(8,128)}, f32[27,16,16,128]{3,0,2,1:T(8,128)}) conditional(s32[]{:T(128)} %convert_element_type.4, (f32[27]{0:T(128)S(1)}, f32[27,16,16,128]{3,2,1,0:T(8,128)S(1)}, f32[27,3]{0,1:T(4,128)S(1)}) %tuple.275, (pred[16,16,128]{2,1,0:T(8,128)(4,1)}, f32[27]{0:T(128)S(1)}, f32[27,16,16,128]{3,2,1,0:T(8,128)S(1)}, ...), branch_computations={%region_1.4_spmd, %region_4.8_spmd} | conditional | flops 175374336 | bytes 35194636 | solution.py:167
  61.6 5.2 %multiply_reduce_fusion.2 = (f32[16,16,128]{2,1,0:T(8,128)S(1)}, f32[3,16,16,128]{3,0,2,1:T(4,128)S(1)}) fusion(f32[16,16,128]{2,1,0:T(8,128)} %reduce_sum.98, f32[27,16,16,128]{3,2,1,0:T(8,128)S(1)} %get-tuple-element.495, f32[27,3]{0,1:T(4,128)S(1)} %get-tuple-element.42), kind=kOutput, calls=%fused_computation.31 | convolution fusion | flops 32112640 | bytes 4194628 | tf_op jit(solution)/shard_map/cond/branch_1_fun/ia,i...->a.../dot_general | solution.py:58
  71.2 5.8 %multiply_reduce_fusion.1 = f32[16,16,128]{2,1,0:T(8,128)S(1)} fusion(f32[27,16,16,128]{3,0,2,1:T(8,128)S(1)} %fusion.10, f32[27,16,16,128]{3,2,1,0:T(8,128)S(1)} %get-tuple-element.495, f32[9,27]{1,0:T(8,128)S(1)} %get-tuple-element.43), kind=kOutput, calls=%fused_computation.28 | convolution fusion | flops 96993280 | bytes 7209932 | tf_op jit(solution)/shard_map/cond/branch_1_fun/ki,i...->k.../dot_general | solution.py:79
  77.1 6.3 %multiply_add_fusion.1 = (f32[27,16,16,128]{3,0,2,1:T(8,128)}, f32[27,16,16,128]{3,0,2,1:T(8,128)}) fusion(f32[27,16,16,128]{3,0,2,1:T(8,128)S(1)} %fusion.10, f32[16,16,128]{2,1,0:T(8,128)S(1)} %get-tuple-element.555, f32[16,16,128]{2,1,0:T(8,128)S(1)} %get-tuple-element.554, f32[27,16,16,128]{3,2,1,0:T(8,128)S(1)} %get-tuple-element.495, ...), kind=kLoop, calls=%fused_computation.27 | loop fusion | flops 6193152 | bytes 14450688 | tf_op jit(solution)/shard_map/cond/branch_1_fun/add | solution.py:89
  84.7 14.6 %stack.261 = pred[27,16,16,128]{3,0,2,1:T(8,128)(4,1)} concatenate(pred[1,16,16,128]{3,0,2,1:T(4,128)(4,1)} %copy.2107, pred[1,16,16,128]{3,0,2,1:T(4,128)(4,1)} %copy.2108, pred[1,16,16,128]{3,0,2,1:T(4,128)(4,1)} %copy.2109, pred[1,16,16,128]{3,0,2,1:T(4,128)(4,1)} %copy.2110, pred[1,16,16,128]{3,0,2,1:T(4,128)(4,1)} %copy.2111, pred[1,16,16,128]{3,0,2,1:T(4,128)(4,1)} %copy.2112, ...), dimensions={0} | concatenate | bytes 1769472 | tf_op jit(solution)/shard_map/stack | solution.py:144
  99.3 5.0 %select_n.96 = f32[27,16,16,128]{3,0,2,1:T(8,128)S(1)} select(pred[27,16,16,128]{3,0,2,1:T(8,128)(4,1)} %stack.261, f32[27,16,16,128]{3,0,2,1:T(8,128)} %get-tuple-element.53, f32[27,16,16,128]{3,0,2,1:T(8,128)} %get-tuple-element.54) | non-fusion elementwise | flops 884736 | bytes 11501568 | tf_op jit(solution)/shard_map/jit(_where)/select_n | solution.py:170
  108.8 10.6 %collective-permute-done = f32[27,1,16,128]{3,0,2,1:T(8,128)S(1)} collective-permute-done((f32[27,1,16,128]{3,0,2,1:T(8,128)S(1)}, f32[27,1,16,128]{3,0,2,1:T(8,128)S(1)}, u32[]{:S(2)}, u32[]{:S(2)}) %collective-permute-start) | collective-permute-done | bytes 221216 | tf_op jit(solution)/shard_map/ppermute | solution.py:41
  128.2 4.5 %collective-permute-done.2 = f32[27,18,1,128]{3,0,2,1:T(8,128)S(1)} collective-permute-done((f32[27,18,1,128]{3,0,2,1:T(8,128)S(1)}, f32[27,18,1,128]{3,0,2,1:T(8,128)S(1)}, u32[]{:S(2)}, u32[]{:S(2)}) %collective-permute-start.2) | collective-permute-done | bytes 248864 | tf_op jit(solution)/shard_map/ppermute | solution.py:41
  135.4 17.4 %conditional.3 = (f32[27,16,16,128]{3,2,1,0:T(8,128)S(1)}) conditional(s32[]{:T(128)} %convert_element_type.4, f32[27,16,16,128]{3,2,1,0:T(8,128)S(1)} %copy.2296, (pred[16,16,128]{2,1,0:T(8,128)(4,1)}, f32[27,18,18,128]{3,0,2,1:T(8,128)}, f32[27,18,16,128]{3,0,2,1:T(8,128)}, f32[27,16,16,128]{3,0,2,1:T(8,128)S(1)}, ...), branch_computations={%region_8.9_spmd, %region_9.10_spmd} | conditional | flops 1474559 | bytes 51163172 | solution.py:180
  135.6 5.2 %copy.2135 = f32[27,18,18,128]{3,2,1,0:T(8,128)S(1)} copy(f32[27,18,18,128]{3,0,2,1:T(8,128)} %get-tuple-element.499) | data formatting | bytes 8957952 | tf_op jit(solution)/shard_map
  141.3 4.6 %copy.2136 = f32[27,18,16,128]{3,2,1,0:T(8,128)S(1)} copy(f32[27,18,16,128]{3,0,2,1:T(8,128)} %get-tuple-element.500) | data formatting | bytes 7962624 | tf_op jit(solution)/shard_map
  153.7 6.2 %multiply_reduce_fusion.4 = (f32[16,16,128]{2,1,0:T(8,128)S(1)}, f32[3,16,16,128]{3,0,2,1:T(4,128)S(1)}) fusion(f32[16,16,128]{2,1,0:T(8,128)} %reduce_sum.109, f32[27,3,1,1]{0,1,3,2:T(4,128)S(1)} %copy-done.53, f32[27,16,16,128]{3,2,1,0:T(8,128)S(1)} %get-tuple-element.658), kind=kOutput, calls=%fused_computation.160 | convolution fusion | flops 32112640 | bytes 4194628 | tf_op jit(solution)/shard_map/ia,i...->a.../dot_general | solution.py:58
  163.5 6.3 %multiply_reduce_fusion.3 = f32[16,16,128]{2,1,0:T(8,128)S(1)} fusion(f32[9,27,1,1]{1,0,3,2:T(8,128)S(1)} %copy-done.60, f32[27,16,16,128]{3,2,1,0:T(8,128)S(1)} %get-tuple-element.658, f32[27,16,16,128]{3,0,2,1:T(8,128)S(1)} %fusion.100, f32[16,16,128]{2,1,0:T(8,128)S(1)} %broadcast_multiply_fusion.2, f32[16,16,128]{2,1,0:T(8,128)S(1)} %copy-done.24, ...), kind=kOutput, calls=%fused_computation.124 | convolution fusion | flops 104071168 | bytes 7472184 | tf_op jit(solution)/shard_map/ki,i...->k.../dot_general | solution.py:79
  170.0 5.2 %add_select_fusion = f32[27,16,16,128]{3,0,2,1:T(8,128)S(1)} fusion(pred[27,16,16,128]{3,0,2,1:T(8,128)(4,1)S(1)} %copy-done.2, f32[27,16,16,128]{3,2,1,0:T(8,128)S(1)} %get-tuple-element.658, f32[27,16,16,128]{3,0,2,1:T(8,128)S(1)} %fusion.100, f32[16,16,128]{2,1,0:T(8,128)S(1)} %fusion.62, f32[16,16,128]{2,1,0:T(8,128)S(1)} %copy-done.43, ...), kind=kLoop, calls=%fused_computation.121 | loop fusion | flops 13271040 | bytes 12025964 | tf_op jit(solution)/shard_map/jit(_where)/select_n | solution.py:170
  181.7 9.1 %collective-permute-done.4 = f32[27,1,16,128]{3,0,2,1:T(8,128)S(1)} collective-permute-done((f32[27,1,16,128]{3,0,2,1:T(8,128)S(1)}, f32[27,1,16,128]{3,0,2,1:T(8,128)S(1)}, u32[]{:S(2)}, u32[]{:S(2)}) %collective-permute-start.4) | collective-permute-done | bytes 221216 | tf_op jit(solution)/shard_map/ppermute | solution.py:41
  204.6 5.1 %pad_maximum_fusion.5 = (f32[1,16,16,128]{3,0,2,1:T(1,128)S(1)}, f32[1,16,16,128]{3,0,2,1:T(1,128)}, f32[1,16,16,128]{3,0,2,1:T(1,128)}, f32[1,16,16,128]{3,0,2,...) fusion(f32[27,18,1,128]{3,0,2,1:T(8,128)S(1)} %collective-permute-done.7, ...), kind=kLoop, calls=%fused_computation.169 | loop fusion | flops 425984 | bytes 5803008 | tf_op jit(solution)/shard_map/concatenate | solution.py:39
  210.2 6.7 %maximum_reduce_fusion = (f32[16,16,128]{2,1,0:T(8,128)}, f32[16,16,128]{2,1,0:T(8,128)}, f32[16,16,128]{2,1,0:T(8,128)}, f32[16,16,128]{2,1,0:T(8,128)}, f32[16,16,128]{2,1,0:T(8,128)}, /*index=5*/f32[16,16,128]{2,1,0:T(8,128)}) fusion(f32[27,18,1,128]{3,0,2,1:T(8,128)S(1)} %collective-permute-done.7, f32[27,1,16,128]{3,0,2,1:T(8,128)S(1)} %collective-permute-done.5, ...), kind=kLoop, calls=%fused_computation.172 | loop fusion | flops 360448 | bytes 5803008 | tf_op jit(solution)/shard_map/slice | solution.py:109
  225.1 4.4 %maximum_reduce_fusion.2 = (f32[16,16,128]{2,1,0:T(8,128)}, f32[16,16,128]{2,1,0:T(8,128)}, f32[16,16,128]{2,1,0:T(8,128)}, f32[1,16,16,128]{3,0,2,1:T(1,128)}) fusion(f32[27,18,1,128]{3,0,2,1:T(8,128)S(1)} %collective-permute-done.6, f32[27,1,16,128]{3,0,2,1:T(8,128)S(1)} %collective-permute-done.5, f32[27,16,16,128]{3,0,2,1:T(8,128)} %copy-done, ...), kind=kLoop, calls=%fused_computation.180 | loop fusion | flops 393216 | bytes 4754432 | tf_op jit(solution)/shard_map/slice | solution.py:109
  231.7 6.2 %pad_maximum_fusion.8 = (f32[1,16,16,128]{3,0,2,1:T(1,128)}, f32[1,16,16,128]{3,0,2,1:T(1,128)}, f32[1,16,16,128]{3,0,2,1:T(1,128)S(1)}, f32[1,16,16,128]{3,0,2,...) fusion(f32[27,18,1,128]{3,0,2,1:T(8,128)S(1)} %collective-permute-done.7, ...), kind=kLoop, calls=%fused_computation.173 | loop fusion | flops 393216 | bytes 6182912 | tf_op jit(solution)/shard_map/slice | solution.py:109
  309.6 15.8 %select_reduce_fusion.1 = (f32[27,16,16,16]{3,2,1,0:T(8,128)}, f32[27,16,16,16]{3,2,1,0:T(8,128)S(1)}) fusion(pred[8]{0:T(512)(128)(4,1)S(1)} %broadcast_compare_fusion.1, f32[27,16,16,8,16]{4,2,1,3,0:T(8,128)} %copy_dynamic-update-slice_fusion, pred[8]{0:T(512)(128)(4,1)S(1)} %get-tuple-element.520), kind=kLoop, calls=%fused_computation.107 | loop fusion | flops 3317760 | bytes 4423696 | tf_op jit(solution)/shard_map/reduce_sum | solution.py:188
  325.4 5.4 %reduce_sum.113 = f32[27,4096]{1,0:T(8,128)} reshape(f32[27,16,16,16]{3,2,1,0:T(8,128)} %get-tuple-element.505) | data formatting | bytes 884736 | tf_op jit(solution)/shard_map/reduce_sum | solution.py:188
  336.6 7.8 %collective-permute-start.9 = (f32[27,4096]{1,0:T(8,128)}, f32[27,4096]{1,0:T(8,128)}, u32[]{:S(2)}, u32[]{:S(2)}) collective-permute-start(f32[27,4096]{1,0:T(8,128)} %reduce_sum.115), channel_id=1, source_target_pairs={{1,0},{2,1},{3,2},{4,3},{5,4},{6,5},{7,6},{8,7},{9,8},{10,9},{11,1... | collective-permute-start | bytes 1327112 | tf_op jit(solution)/shard_map/ppermute | solution.py:53
  344.5 24.0 %reshape.96 = f32[8,27,4096]{2,0,1:T(8,128)} reshape(f32[8,27,16,16,16]{4,3,2,0,1:T(8,128)} %bitcast.297) | data formatting | bytes 7077888 | tf_op jit(solution)/shard_map/reshape | solution.py:120
  371.6 5.3 %fusion.40 = f32[3,8,4096]{2,0,1:T(4,128)S(1)} fusion(f32[27,3,1]{0,1,2:T(4,128)S(1)} %copy-done.56, f32[27,8,4096]{2,1,0:T(8,128)S(1)} %get-tuple-element.519, f32[8,4096]{1,0:T(8,128)S(1)} %get-tuple-element.518), kind=kOutput, calls=%fused_computation.112 | convolution fusion | flops 31948800 | bytes 4063556 | tf_op jit(solution)/shard_map/ia,i...->a.../dot_general | solution.py:58
  (349 shorter events, 196.4 us)
Async XLA Ops:
  33.6 17.7 %copy-start.52 = (f32[9,27]{1,0:T(8,128)S(1)}, f32[9,27]{1,0:T(8,128)}, u32[]{:S(2)}) copy-start(f32[9,27]{1,0:T(8,128)} %constant.160.clone) | copy-start | bytes 2920
  33.6 17.7 %copy-start.54 = (f32[27,3]{0,1:T(4,128)S(1)}, f32[27,3]{0,1:T(4,128)}, u32[]{:S(2)}) copy-start(f32[27,3]{0,1:T(4,128)} %constant.158.clone) | copy-start | bytes 976
  33.6 17.7 %copy-start.59 = (f32[27]{0:T(128)S(1)}, f32[27]{0:T(128)}, u32[]{:S(2)}) copy-start(f32[27]{0:T(128)} %constant.159.clone) | copy-start | bytes 328
  104.3 15.1 %collective-permute-start = (f32[27,1,16,128]{3,0,2,1:T(8,128)S(1)}, f32[27,1,16,128]{3,0,2,1:T(8,128)S(1)}, u32[]{:S(2)}, u32[]{:S(2)}) collective-permute-start(f32[27,1,16,128]{3,0,2,1:T(8,128)S(1)} %get-tuple-element.582), channel_id=1, source_target_pairs={{0,16},{16,32},{32,48},{48,64},{64,80},{80,96},{96,112},{112,0},{1... | collective-permute-start | bytes 663560 | tf_op jit(solution)/shard_map/ppermute | solution.py:41
  108.2 12.2 %collective-permute-start.1 = (f32[27,1,16,128]{3,0,2,1:T(8,128)S(1)}, f32[27,1,16,128]{3,0,2,1:T(8,128)S(1)}, u32[]{:S(2)}, u32[]{:S(2)}) collective-permute-start(f32[27,1,16,128]{3,0,2,1:T(8,128)S(1)} %get-tuple-element.583), channel_id=1, source_target_pairs={{16,0},{32,16},{48,32},{64,48},{80,64},{96,80},{112,96},{0,112},{1... | collective-permute-start | bytes 663560 | tf_op jit(solution)/shard_map/ppermute | solution.py:43
  124.3 8.4 %collective-permute-start.2 = (f32[27,18,1,128]{3,0,2,1:T(8,128)S(1)}, f32[27,18,1,128]{3,0,2,1:T(8,128)S(1)}, u32[]{:S(2)}, u32[]{:S(2)}) collective-permute-start(f32[27,18,1,128]{3,0,2,1:T(8,128)S(1)} %get-tuple-element.572), channel_id=1, source_target_pairs={{0,1},{1,2},{2,3},{3,4},{4,5},{5,6},{6,7},{7,8},{8,9},{9,10},{10,1... | collective-permute-start | bytes 746504 | tf_op jit(solution)/shard_map/ppermute | solution.py:41
  124.4 8.3 %collective-permute-start.3 = (f32[27,18,1,128]{3,0,2,1:T(8,128)S(1)}, f32[27,18,1,128]{3,0,2,1:T(8,128)S(1)}, u32[]{:S(2)}, u32[]{:S(2)}) collective-permute-start(f32[27,18,1,128]{3,0,2,1:T(8,128)S(1)} %get-tuple-element.573), channel_id=1, source_target_pairs={{1,0},{2,1},{3,2},{4,3},{5,4},{6,5},{7,6},{8,7},{9,8},{10,9},{11,1... | collective-permute-start | bytes 746504 | tf_op jit(solution)/shard_map/ppermute | solution.py:43
  135.4 18.2 %copy-start.53 = (f32[27,3,1,1]{0,1,3,2:T(4,128)S(1)}, f32[27,3,1,1]{0,1,3,2:T(4,128)}, u32[]{:S(2)}) copy-start(f32[27,3,1,1]{0,1,3,2:T(4,128)} %constant.167) | copy-start | bytes 976
  153.7 9.8 %copy-start.24 = (f32[16,16,128]{2,1,0:T(8,128)S(1)}, f32[16,16,128]{2,1,0:T(8,128)}, u32[]{:S(2)}) copy-start(f32[16,16,128]{2,1,0:T(8,128)} %reduce_sum.109) | copy-start | bytes 393220
  153.7 9.8 %copy-start.60 = (f32[9,27,1,1]{1,0,3,2:T(8,128)S(1)}, f32[9,27,1,1]{1,0,3,2:T(8,128)}, u32[]{:S(2)}) copy-start(f32[9,27,1,1]{1,0,3,2:T(8,128)} %constant.168) | copy-start | bytes 2920
  177.2 19.1 %copy-start.58 = (s32[8]{0:T(128)S(1)}, s32[8]{0:T(128)}, u32[]{:S(2)}) copy-start(s32[8]{0:T(128)} %param.19) | copy-start | bytes 100
  177.2 13.6 %collective-permute-start.4 = (f32[27,1,16,128]{3,0,2,1:T(8,128)S(1)}, f32[27,1,16,128]{3,0,2,1:T(8,128)S(1)}, u32[]{:S(2)}, u32[]{:S(2)}) collective-permute-start(f32[27,1,16,128]{3,0,2,1:T(8,128)S(1)} %get-tuple-element.580), channel_id=1, source_target_pairs={{0,16},{16,32},{32,48},{48,64},{64,80},{80,96},{96,112},{112,0},{1... | collective-permute-start | bytes 663560 | tf_op jit(solution)/shard_map/ppermute | solution.py:41
  180.3 14.1 %collective-permute-start.5 = (f32[27,1,16,128]{3,0,2,1:T(8,128)S(1)}, f32[27,1,16,128]{3,0,2,1:T(8,128)S(1)}, u32[]{:S(2)}, u32[]{:S(2)}) collective-permute-start(f32[27,1,16,128]{3,0,2,1:T(8,128)S(1)} %get-tuple-element.581), channel_id=1, source_target_pairs={{16,0},{32,16},{48,32},{64,48},{80,64},{96,80},{112,96},{0,112},{1... | collective-permute-start | bytes 663560 | tf_op jit(solution)/shard_map/ppermute | solution.py:43
  196.2 8.4 %collective-permute-start.7 = (f32[27,18,1,128]{3,0,2,1:T(8,128)S(1)}, f32[27,18,1,128]{3,0,2,1:T(8,128)S(1)}, u32[]{:S(2)}, u32[]{:S(2)}) collective-permute-start(f32[27,18,1,128]{3,0,2,1:T(8,128)S(1)} %get-tuple-element.570), channel_id=1, source_target_pairs={{0,1},{1,2},{2,3},{3,4},{4,5},{5,6},{6,7},{7,8},{8,9},{9,10},{10,1... | collective-permute-start | bytes 746504 | tf_op jit(solution)/shard_map/ppermute | solution.py:41
  196.3 21.8 %collective-permute-start.6 = (f32[27,18,1,128]{3,0,2,1:T(8,128)}, f32[27,18,1,128]{3,0,2,1:T(8,128)S(1)}, u32[]{:S(2)}, u32[]{:S(2)}) collective-permute-start(f32[27,18,1,128]{3,0,2,1:T(8,128)} %get-tuple-element.571), channel_id=1, source_target_pairs={{1,0},{2,1},{3,2},{4,3},{5,4},{6,5},{7,6},{8,7},{9,8},{10,9},{11,1... | collective-permute-start | bytes 746504 | tf_op jit(solution)/shard_map/ppermute | solution.py:43
  237.9 7.9 %copy-start.39 = (f32[1,16,16,128]{3,0,2,1:T(1,128)S(1)}, f32[1,16,16,128]{3,0,2,1:T(1,128)}, u32[]{:S(2)}) copy-start(f32[1,16,16,128]{3,0,2,1:T(1,128)} %get-tuple-element.563) | copy-start | bytes 393220
  238.1 9.2 %copy-start.49 = (f32[16,16,128]{2,1,0:T(8,128)S(1)}, f32[16,16,128]{2,1,0:T(8,128)}, u32[]{:S(2)}) copy-start(f32[16,16,128]{2,1,0:T(8,128)} %get-tuple-element.509) | copy-start | bytes 393220
  239.4 9.2 %copy-start.37 = (f32[1,16,16,128]{3,0,2,1:T(1,128)S(1)}, f32[1,16,16,128]{3,0,2,1:T(1,128)}, u32[]{:S(2)}) copy-start(f32[1,16,16,128]{3,0,2,1:T(1,128)} %get-tuple-element.566) | copy-start | bytes 393220
  257.4 7.4 %copy-start.31 = (f32[1,16,16,128]{3,0,2,1:T(1,128)S(1)}, f32[1,16,16,128]{3,0,2,1:T(1,128)}, u32[]{:S(2)}) copy-start(f32[1,16,16,128]{3,0,2,1:T(1,128)} %get-tuple-element.564) | copy-start | bytes 393220
  260.3 7.4 %copy-start.45 = (f32[16,16,128]{2,1,0:T(8,128)S(1)}, f32[16,16,128]{2,1,0:T(8,128)}, u32[]{:S(2)}) copy-start(f32[16,16,128]{2,1,0:T(8,128)} %get-tuple-element.513) | copy-start | bytes 393220
  263.2 7.4 %copy-start.32 = (f32[1,16,16,128]{3,0,2,1:T(1,128)S(1)}, f32[1,16,16,128]{3,0,2,1:T(1,128)}, u32[]{:S(2)}) copy-start(f32[1,16,16,128]{3,0,2,1:T(1,128)} %get-tuple-element.562) | copy-start | bytes 393220
  275.0 8.7 %copy-start.3 = (f32[1,16,16,8,16]{4,3,2,1,0:T(8,128)S(1)}, f32[1,16,16,8,16]{4,3,2,1,0:T(8,128)}, u32[]{:S(2)}) copy-start(f32[1,16,16,8,16]{4,3,2,1,0:T(8,128)} %stack.267) | copy-start | bytes 393220
  330.8 37.7 %collective-permute-start.8 = (f32[27,4096]{1,0:T(8,128)}, f32[27,4096]{1,0:T(8,128)}, u32[]{:S(2)}, u32[]{:S(2)}) collective-permute-start(f32[27,4096]{1,0:T(8,128)} %reduce_sum.113), channel_id=1, source_target_pairs={{0,1},{1,2},{2,3},{3,4},{4,5},{5,6},{6,7},{7,8},{8,9},{9,10},{10,1... | collective-permute-start | bytes 1327112 | tf_op jit(solution)/shard_map/ppermute | solution.py:53
  336.6 31.9 %collective-permute-start.9 = (f32[27,4096]{1,0:T(8,128)}, f32[27,4096]{1,0:T(8,128)}, u32[]{:S(2)}, u32[]{:S(2)}) collective-permute-start(f32[27,4096]{1,0:T(8,128)} %reduce_sum.115), channel_id=1, source_target_pairs={{1,0},{2,1},{3,2},{4,3},{5,4},{6,5},{7,6},{8,7},{9,8},{10,9},{11,1... | collective-permute-start | bytes 1327112 | tf_op jit(solution)/shard_map/ppermute | solution.py:53
  (46 other events, 250.5 us)
where the time goes:
time: 386 us; the launch traced here: 378 us
  local copies, waits for them, and re-layouts  185 us (48%)
  other arithmetic  84.1 us (22%)
  matrix products  36.6 us (9%)
  waiting for transfers between devices  33.1 us (9%)
  starting transfers between devices  27 us (7%)
  loops' own time  10.1 us (3%)
    unnamed x142, local copies, waits for them, and re-layouts  41 us
    another operation x28, local copies, waits for them, and re-layouts, stream_cells(): return jnp.stack(moved)  37.3 us
    another operation x28, local copies, waits for them, and re-layouts, on_device(): jnp.stack([jnp.roll(level_pad[1 + int(offset[0]):1 + int(offset[0]) + siz...  35.5 us
    ppermute x4, waiting for transfers between devices, extended(): lax.ppermute(tail, axis, [(i, (i + 1) % count) for i in range(count)])  28.5 us
    reshape x1, local copies, waits for them, and re-layouts, block_fields(): split.transpose(3, 0, 1, 2, 4)  24 us
    slice x3, other arithmetic, stream_cells(): padded[direction, 1 - shift_x:1 - shift_x + size_x, 1 - shift_y:1 - shift...  17.3 us
    dot_general x3, matrix products, cell_moments(): jnp.einsum('ia,i...->a...', jnp.asarray(lattice_vel), states, precision=l...  16.6 us
    concatenate x5, other arithmetic, extended(): jnp.concatenate([lax.ppermute(tail, axis, [(i, (i + 1) % count) for i in...  16.3 us
  transfers between devices with their start and end apart: 10, of which 6 were waited for; matrix products, arithmetic and copies ran while one was open for 11% of the time, Pallas kernels for 0%

commit v1 on v0

v1 whole, which is shorter than its diff:
```python
import math

import jax
import jax.numpy as jnp
import numpy as np
from jax import lax
from jax.experimental import pallas as pl
from jax.experimental.pallas import tpu as pltpu
from jax.sharding import PartitionSpec as P

tau_coarse = 0.56
tau_fine = 0.62
scale_to_fine = tau_fine / (2.0 * tau_coarse)
scale_to_coarse = 2.0 * tau_coarse / tau_fine
smagorinsky = 18.0 * math.sqrt(2.0) * 0.17 * 0.17
weights = (8.0 / 27, 2.0 / 27, 1.0 / 54, 1.0 / 216)
ROWS = 8
LANES = 128
VMEM_BYTES = 56 * 1024 * 1024


def comp(a, b, e):
    return 9 * (a + 1) + 3 * (b + 1) + (e + 1)


def face(b, e):
    return 3 * (b + 1) + (e + 1)


DIRS = [(a, b, e) for a in (-1, 0, 1) for b in (-1, 0, 1) for e in (-1, 0, 1)]
HALF = [c for c in DIRS if c > (0, 0, 0)]


def lane_block(edge):
    return lax.broadcasted_iota(jnp.int32, (ROWS, LANES), 1) // edge


def sublane():
    return lax.broadcasted_iota(jnp.int32, (ROWS, LANES), 0)


def column_level(levels, shape, blocks, dx, dy):
    count_x, count_y = shape
    ix = lax.rem(lax.axis_index("bx") + (dx + count_x), count_x)
    iy = lax.rem(lax.axis_index("by") + (dy + count_y), count_y)
    base = (ix * count_y + iy) * blocks
    block = lane_block(LANES // blocks)
    value = jnp.full((ROWS, LANES), levels[base], jnp.int32)
    for k in range(1, blocks):
        value = jnp.where(block == k, levels[base + k], value)
    return value


def lane_roll(tile, by):
    return tile if by == 0 else pltpu.roll(tile, by % LANES, 1)


def collide(get, fine, everywhere, factor, put, dirs=None):
    total, diff, quad = {}, {}, {}
    for a in (-1, 0, 1):
        for b in (-1, 0, 1):
            low, mid, high = (get((a, b, e)) for e in (-1, 0, 1))
            both = low + high
            total[a, b] = both + mid
            diff[a, b] = high - low
            quad[a, b] = both
    ta, tb, tbb, da, db, qa = {}, {}, {}, {}, {}, {}
    for a in (-1, 0, 1):
        both = total[a, -1] + total[a, 1]
        tbb[a] = both
        ta[a] = both + total[a, 0]
        tb[a] = total[a, 1] - total[a, -1]
        da[a] = diff[a, -1] + diff[a, 0] + diff[a, 1]
        db[a] = diff[a, 1] - diff[a, -1]
        qa[a] = quad[a, -1] + quad[a, 0] + quad[a, 1]
    pxx = ta[-1] + ta[1]
    rho = pxx + ta[0]
    jx = ta[1] - ta[-1]
    jy = tb[-1] + tb[0] + tb[1]
    jz = da[-1] + da[0] + da[1]
    pyy = tbb[-1] + tbb[0] + tbb[1]
    pzz = qa[-1] + qa[0] + qa[1]
    pxy = tb[1] - tb[-1]
    pxz = da[1] - da[-1]
    pyz = db[-1] + db[0] + db[1]
    inv = 1.0 / rho
    ux, uy, uz = jx * inv, jy * inv, jz * inv
    third = rho * (1.0 / 3.0)
    pxx = pxx - third - jx * ux
    pyy = pyy - third - jy * uy
    pzz = pzz - third - jz * uz
    pxy = pxy - jx * uy
    pxz = pxz - jx * uz
    pyz = pyz - jy * uz
    norm = jnp.sqrt(
        pxx * pxx + pyy * pyy + pzz * pzz + 2.0 * (pxy * pxy + pxz * pxz + pyz * pyz)
    )
    base_time = jnp.where(fine, tau_fine, tau_coarse)
    tau = 0.5 * (base_time + jnp.sqrt(base_time * base_time + smagorinsky * norm * inv))
    keep = 1.0 - 1.0 / tau
    if not everywhere:
        keep = jnp.where(fine, keep, 1.0)
    base = 1.0 - 1.5 * (ux * ux + uy * uy + uz * uz)
    scaled = [rho * w for w in weights]
    rest = [s * base for s in scaled]
    vx, vy, vz = 3.0 * ux, 3.0 * uy, 3.0 * uz
    vel = {(0, 0, 1): vz, (0, 1, 0): vy, (1, 0, 0): vx}
    vel[0, 1, 1], vel[0, 1, -1] = vy + vz, vy - vz
    vel[1, 0, 1], vel[1, 0, -1] = vx + vz, vx - vz
    vel[1, 1, 0], vel[1, -1, 0] = vx + vy, vx - vy
    for b in (-1, 1):
        for e in (-1, 1):
            vel[1, b, e] = vel[1, b, 0] + (vz if e > 0 else -vz)

    def emit(c, balance):
        if dirs is not None and c not in dirs:
            return
        gain = keep if c == (0, 0, 0) else keep * factor(c)
        put(c, balance + gain * (get(c) - balance))

    emit((0, 0, 0), rest[0])
    for c in HALF:
        n = sum(abs(k) for k in c)
        odd = scaled[n] * vel[c]
        even = rest[n] + 0.5 * odd * vel[c]
        emit(c, even + odd)
        emit(tuple(-k for k in c), even - odd)


def level_factor(here, there_rows, e):
    scale = jnp.where(here == 1, scale_to_coarse, scale_to_fine)
    return jnp.where(lane_roll(there_rows, -e) != here, scale, 1.0)


def fill_factors(levels, shape, blocks, table):
    lev = {
        (dx, dy): column_level(levels, shape, blocks, dx, dy)
        for dx in (-1, 0, 1)
        for dy in (-1, 0, 1)
    }
    row = sublane()
    for k, (own, dx) in enumerate(((0, -1), (0, 0), (0, 1), (-1, 0), (1, 0))):
        here = lev[own, 0]
        for e in (-1, 0, 1):
            plain = level_factor(here, lev[dx, 0], e)
            for b in (-1, 0, 1):
                low, high = plain, plain
                if b == -1:
                    low = jnp.where(row == 0, level_factor(here, lev[dx, -1], e), plain)
                if b == 1:
                    high = jnp.where(row == ROWS - 1, level_factor(here, lev[dx, 1], e), plain)
                table[k, b + 1, e + 1, 0:8, :] = low
                table[k, b + 1, e + 1, 8:16, :] = high


def x_side(a, x, last):
    if a == 0:
        return 1
    return jnp.where(x == (0 if a < 0 else last), 1 + a, 1)


def store_by_parity(odd, first, second, up, down):
    @pl.when(odd == 0)
    def _():
        first[...] = up[...]
        second[...] = down[...]

    @pl.when(odd == 1)
    def _():
        first[...] = down[...]
        second[...] = up[...]


def start_kernel(shape, blocks, levels, f, out, table, pay_a, pay_b, up, down):
    fill_factors(levels, shape, blocks, table)
    fine = column_level(levels, shape, blocks, 0, 0) == 1
    last = f.shape[1] - 1

    def layer(x, carry):
        for h in (0, 1):
            rows = slice(8 * h, 8 * h + 8)

            def put(c, value):
                a, b, e = c
                out[comp(*c), x, rows, :] = value
                if b == 1 and h == 1:
                    up[face(a, e), pl.ds(x, 1), :] = value[7:8]
                if b == -1 and h == 0:
                    down[face(a, e), pl.ds(x, 1), :] = value[0:1]

            collide(
                lambda c: f[comp(*c), x, rows, :],
                fine,
                False,
                lambda c: table[x_side(c[0], x, last), c[1] + 1, c[2] + 1, rows, :],
                put,
            )
        return carry

    lax.fori_loop(0, f.shape[1], layer, 0)
    store_by_parity(lax.rem(lax.axis_index("by"), 2), pay_a, pay_b, up, down)


def shifted_read(g, above, below, row, c, x, h):
    a, b, e = c
    i = comp(a, b, e)
    if b == 0:
        tile = g[i, x, 8 * h : 8 * h + 8, :]
    elif b == 1:
        if h == 1:
            tile = g[i, x, 7:15, :]
        else:
            tile = pltpu.roll(g[i, x, 0:8, :], 1, 0)
            tile = jnp.where(row == 0, below[face(a, e), pl.ds(x, 1), :], tile)
    else:
        if h == 0:
            tile = g[i, x, 1:9, :]
        else:
            tile = pltpu.roll(g[i, x, 8:16, :], 7, 0)
            tile = jnp.where(row == 7, above[face(a, e), pl.ds(x, 1), :], tile)
    return lane_roll(tile, e)


def load_by_parity(odd, first, second, above, below):
    @pl.when(odd == 0)
    def _():
        above[...] = first[...]
        below[...] = second[...]

    @pl.when(odd == 1)
    def _():
        above[...] = second[...]
        below[...] = first[...]


def side_kernel(shape, blocks, levels, f, g, got_a, got_b, pay_a, pay_b, above, below, up, down):
    load_by_parity(lax.rem(lax.axis_index("by"), 2), got_a, got_b, above, below)
    fine = column_level(levels, shape, blocks, 0, 0) == 1
    row = sublane()
    last = f.shape[1] - 1
    for ad, edge, inner, pay in ((1, last, last - 1, up), (-1, 0, 1, down)):
        for h in (0, 1):
            rows = slice(8 * h, 8 * h + 8)
            for b in (-1, 0, 1):
                for e in (-1, 0, 1):
                    j = face(b, e)
                    same, flat, back = (ad, b, e), (0, b, e), (-ad, b, e)
                    pay[j, rows, :] = shifted_read(g, above, below, row, same, edge, h)
                    pay[9 + j, rows, :] = jnp.where(
                        fine,
                        shifted_read(g, above, below, row, same, inner, h),
                        f[comp(*same), edge, rows, :],
                    )
                    pay[18 + j, rows, :] = jnp.where(
                        fine,
                        shifted_read(g, above, below, row, flat, edge, h),
                        f[comp(*flat), edge, rows, :],
                    )
                    pay[27 + j, rows, :] = f[comp(*back), edge, rows, :]
    store_by_parity(lax.rem(lax.axis_index("bx"), 2), pay_a, pay_b, up, down)


def body_kernel(
    shape, blocks, levels, f, g, table, ya, yb, xa, xb, out, pay_a, pay_b,
    above, below, right, left, state, sums, up, down,
):
    odd_x = lax.rem(lax.axis_index("bx"), 2)
    odd_y = lax.rem(lax.axis_index("by"), 2)
    load_by_parity(odd_y, ya, yb, above, below)
    load_by_parity(odd_x, xa, xb, right, left)
    fine = {dx: column_level(levels, shape, blocks, dx, 0) == 1 for dx in (-1, 0, 1)}
    row = sublane()
    last = f.shape[1] - 1

    def read(c, x, h):
        return shifted_read(g, above, below, row, c, x, h)

    def finish(x, h, mask, factor, dirs, slot):
        rows = slice(8 * h, 8 * h + 8)
        made = {}

        def put(c, value):
            made[c] = value

        collide(lambda c: state[comp(*c), rows, :], mask, True, factor, put, dirs)
        for a in (-1, 0, 1):
            if dirs is not None and (a, 0, 0) not in dirs:
                continue
            for b in (-1, 0, 1):
                plus = lane_roll(made[a, b, 1], 1)
                minus = lane_roll(made[a, b, -1], -1)
                sums[a + 1, b + 1, 0, slot, rows, :] = made[a, b, 0] + (plus + minus)
                sums[a + 1, b + 1, 1, slot, rows, :] = plus - minus

    def own(x, skip):
        for h in (0, 1):
            rows = slice(8 * h, 8 * h + 8)
            for c in DIRS:
                a, b, e = c
                if a == skip == 1:
                    tile = left[face(b, e), rows, :]
                elif a == skip == -1:
                    tile = right[face(b, e), rows, :]
                else:
                    tile = read(c, x - a, h)
                state[comp(*c), rows, :] = jnp.where(fine[0], tile, f[comp(*c), x, rows, :])
            dirs = None if skip == 0 else [c for c in DIRS if c[0] != -skip]
            finish(
                x, h, fine[0],
                lambda c: table[
                    1 + (c[0] if skip == -c[0] else 0), c[1] + 1, c[2] + 1, rows, :
                ],
                dirs, x + 1,
            )

    def halo(side, slot, pay, edge, k):
        for h in (0, 1):
            rows = slice(8 * h, 8 * h + 8)
            for b in (-1, 0, 1):
                for e in (-1, 0, 1):
                    j = face(b, e)
                    state[comp(-side, b, e), rows, :] = pay[9 + j, rows, :]
                    state[comp(0, b, e), rows, :] = pay[18 + j, rows, :]
                    state[comp(side, b, e), rows, :] = jnp.where(
                        fine[side], read((side, b, e), edge, h), pay[27 + j, rows, :]
                    )
            finish(
                0, h, fine[side],
                lambda c: table[k, c[1] + 1, c[2] + 1, rows, :],
                [c for c in DIRS if c[0] == -side], slot,
            )

    def layer(x, carry):
        own(x, 0)
        return carry

    lax.fori_loop(1, last, layer, 0)
    own(0, 1)
    own(last, -1)
    halo(-1, 0, left, 0, 3)
    halo(1, last + 2, right, last, 4)

    def gather(x, carry):
        for h in (0, 1):
            rows = slice(8 * h, 8 * h + 8)
        total, cross, along = {}, {}, {}
        for b in (-1, 0, 1):
            for h in (0, 1):
                rows = slice(8 * h, 8 * h + 8)
                low = sums[2, b + 1, 0, x, rows, :]
                mid = sums[1, b + 1, 0, x + 1, rows, :]
                high = sums[0, b + 1, 0, x + 2, rows, :]
                total[b, h] = low + mid + high
                cross[b, h] = low - high
                along[b, h] = (
                    sums[2, b + 1, 1, x, rows, :]
                    + sums[1, b + 1, 1, x + 1, rows, :]
                    + sums[0, b + 1, 1, x + 2, rows, :]
                )
        for n, part in enumerate((total, cross, along)):
            up[n, pl.ds(x, 1), :] = part[1, 1][7:8]
            down[n, pl.ds(x, 1), :] = part[-1, 0][0:1]
            rise = [pltpu.roll(part[1, h], 1, 0) for h in (0, 1)]
            fall = [pltpu.roll(part[-1, h], 7, 0) for h in (0, 1)]
            rise = [jnp.where(row == 0, 0.0, rise[0]), jnp.where(row == 0, rise[0], rise[1])]
            fall = [jnp.where(row == 7, fall[1], fall[0]), jnp.where(row == 7, 0.0, fall[1])]
            for h in (0, 1):
                rows = slice(8 * h, 8 * h + 8)
                out[(0, 1, 3)[n], x, rows, :] = part[0, h] + rise[h] + fall[h]
                if n == 0:
                    out[2, x, rows, :] = rise[h] - fall[h]
        return carry

    lax.fori_loop(0, last + 1, gather, 0)
    store_by_parity(odd_y, pay_a, pay_b, up, down)


def block_rows(tile, reflect, turn):
    tile = pltpu.roll(tile, 0, 1, stride=LANES // 8, stride_axis=0)
    tile = jnp.take_along_axis(tile, reflect, axis=0)
    return jnp.take_along_axis(tile, turn, axis=1)


def leaving(slots, blocks, step):
    here = lax.axis_index("bx") * lax.axis_size("by") + lax.axis_index("by")
    which = jnp.int32(-1)
    for k in range(blocks):
        which = jnp.where(slots[k] // blocks == here + step, k, which)
    return which


def moments_kernel(
    blocks, slots, part, got_a, got_b, rho_out, vel_out, pay_a, pay_b,
    above, below, made, up, down,
):
    odd = lax.rem(lax.axis_index("by"), 2)
    load_by_parity(odd, got_a, got_b, above, below)
    row = sublane()
    group = lane_block(LANES // 8)
    reflect = (group - row) & 7
    turn = (lane_block(1) + row * (LANES // 8)) & (LANES - 1)

    def layer(x, carry):
        for h in (0, 1):
            rows = slice(8 * h, 8 * h + 8)
            edge, halo, sign = (0, below, 1.0) if h == 0 else (7, above, -1.0)
            total, cross, along = (halo[n, pl.ds(x, 1), :] for n in range(3))
            values = []
            for n, extra in enumerate((total, cross, sign * total, along)):
                values.append(part[n, x, rows, :] + jnp.where(row == edge, extra, 0.0))
            inv = 1.0 / values[0]
            for n in range(4):
                tile = values[0] if n == 0 else values[n] * inv
                tile = block_rows(tile, reflect, turn)
                made[2 * n + h, pl.ds(x * 8, 8), :] = tile
        return carry

    lax.fori_loop(0, part.shape[1], layer, 0)
    for x in range(part.shape[1]):
        for h in (0, 1):
            lanes = slice((2 * x + h) * LANES, (2 * x + h + 1) * LANES)
            rho_out[:, lanes] = made[h, 8 * x : 8 * x + 8, :]
            for n in range(3):
                vel_out[n, :, lanes] = made[2 * n + 2 + h, 8 * x : 8 * x + 8, :]
    for step, pay in ((1, up), (-1, down)):
        which = jnp.maximum(leaving(slots, blocks, step), 0)
        for n in range(8):
            pay[n, :, :] = made[n, pl.ds(which, part.shape[1], stride=8), :]
    store_by_parity(odd, pay_a, pay_b, up, down)


def place_kernel(blocks, slots, rho, vel, got_a, got_b, rho_out, vel_out, after, before):
    odd = lax.rem(lax.axis_index("by"), 2)
    load_by_parity(odd, got_a, got_b, after, before)
    row = sublane()
    to_next = row == leaving(slots, blocks, 1)
    to_prev = row == leaving(slots, blocks, -1)
    for x in range(after.shape[1]):
        for h in (0, 1):
            lanes = slice((2 * x + h) * LANES, (2 * x + h + 1) * LANES)
            for n in range(4):
                k = 2 * n + h
                tile = rho[:, lanes] if n == 0 else vel[n - 1, :, lanes]
                tile = jnp.where(to_next, after[k, x : x + 1, :], tile)
                tile = jnp.where(to_prev, before[k, x : x + 1, :], tile)
                if n == 0:
                    rho_out[:, lanes] = tile
                else:
                    vel_out[n - 1, :, lanes] = tile


def swap(value, axis, odd, curve=False):
    count_x, count_y = lax.axis_size("bx"), lax.axis_size("by")
    pairs = []
    if curve:
        pairs = [(j, j + 1) for j in range(odd, count_x * count_y - 1, 2)]
    elif axis == "by":
        for x in range(count_x):
            for y in range(odd, count_y, 2):
                pairs.append((x * count_y + y, x * count_y + (y + 1) % count_y))
    else:
        for y in range(count_y):
            for x in range(odd, count_x, 2):
                pairs.append((x * count_y + y, (x + 1) % count_x * count_y + y))
    pairs = pairs + [(b, a) for a, b in pairs]
    return lax.ppermute(value, ("bx", "by"), pairs)


def call(kernel, outs, specs, scratch, name):
    space = {"v": pltpu.VMEM, "s": pltpu.SMEM}
    return pl.pallas_call(
        kernel,
        out_shape=[jax.ShapeDtypeStruct(s, jnp.float32) for s in outs],
        in_specs=[pl.BlockSpec(memory_space=space[k]) for k in specs],
        out_specs=[pl.BlockSpec(memory_space=pltpu.VMEM)] * len(outs),
        scratch_shapes=[pltpu.VMEM(s, jnp.float32) for s in scratch],
        compiler_params=pltpu.CompilerParams(vmem_limit_bytes=VMEM_BYTES),
        name=name,
    )


def on_device(populations, block_level, new_slot):
    shape = (lax.axis_size("bx"), lax.axis_size("by"))
    blocks = new_slot.shape[0]
    _, nx, ny, nz = populations.shape
    yface, xface, yedge, block = (9, nx, nz), (36, ny, nz), (3, nx, nz), (8, nx, nz)

    def start(*refs):
        start_kernel(shape, blocks, *refs)

    out, table, pay_a, pay_b = call(
        start,
        [populations.shape, (5, 3, 3, ny, nz), yface, yface],
        "sv",
        [yface, yface],
        "start",
    )(block_level, populations)
    ya, yb = swap(pay_a, "by", 0), swap(pay_b, "by", 1)

    def side(*refs):
        side_kernel(shape, blocks, *refs)

    pay_a, pay_b = call(
        side, [xface, xface], "svvvv", [yface, yface, xface, xface], "side"
    )(block_level, populations, out, ya, yb)
    xa, xb = swap(pay_a, "bx", 0), swap(pay_b, "bx", 1)

    def body(*refs):
        body_kernel(shape, blocks, *refs)

    part, pay_a, pay_b = call(
        body,
        [(4, nx, ny, nz), yedge, yedge],
        "svvvvvvv",
        [yface, yface, xface, xface, (27, ny, nz), (3, 3, 2, nx + 2, ny, nz), yedge, yedge],
        "body",
    )(block_level, populations, out, table, ya, yb, xa, xb)
    ya, yb = swap(pay_a, "by", 0), swap(pay_b, "by", 1)

    def moments(*refs):
        moments_kernel(blocks, *refs)

    cells = nx * ny * nz // blocks
    rho, vel, pay_a, pay_b = call(
        moments,
        [(blocks, cells), (3, blocks, cells), block, block],
        "svvv",
        [yedge, yedge, (8, nx * 8, nz), block, block],
        "moments",
    )(new_slot, part, ya, yb)
    ma, mb = swap(pay_a, "by", 0, True), swap(pay_b, "by", 1, True)

    def place(*refs):
        place_kernel(blocks, *refs)

    return tuple(
        call(place, [(blocks, cells), (3, blocks, cells)], "svvvv", [block, block], "place")(
            new_slot, rho, vel, ma, mb
        )
    )


def solution(mesh):
    in_specs = (P(None, "bx", "by", None), P(), P(("bx", "by")))
    out_specs = (P(("bx", "by"), None), P(None, ("bx", "by"), None))
    return jax.shard_map(
        on_device, mesh=mesh, in_specs=in_specs, out_specs=out_specs, check_vma=False
    )
```

time: 386 us -> 66.7 us (0.17); the launches traced: 378 us -> 66.5 us
  local copies, waits for them, and re-layouts: 185 us -> 2.67 us
  other arithmetic: 84.1 us -> 0 us
  matrix products: 36.6 us -> 0 us
  Pallas kernels: 0 us -> 25.5 us
  waiting for transfers between devices: 33.1 us -> 19.2 us
  loops' own time: 10.1 us -> 0 us
  starting transfers between devices: 27 us -> 18.5 us
    another operation x59 -> x0, local copies, waits for them, and re-layouts: 84.7 us -> none  [the longest x28 37.3 us: stream_cells(): return jnp.stack(moved)]
    unnamed x142 -> x16, local copies, waits for them, and re-layouts: 41 us -> 2.67 us
    dot_general x7 -> x0, matrix products: 36.6 us -> none  [the longest x3 16.6 us: cell_moments(): jnp.einsum('ia,i...->a...', jnp.asarray(lattice_vel), states, precision=l...]
    reshape x3 -> x0, local copies, waits for them, and re-layouts: 26.3 us -> none  [the longest x1 24 us: block_fields(): split.transpose(3, 0, 1, 2, 4)]
    pallas_call x0 -> x5, Pallas kernels: none -> 25.5 us  [the longest x1 8.69 us: on_device(): call(body, [(4, nx, ny, nz), yedge, yedge], 'svvvvvvv', [yface, yface, xf...]
    reduce_sum x4 -> x0, other arithmetic: 20.6 us -> none  [the longest x1 15.8 us: on_device(): send_next = jnp.sum(jnp.where(to_next[:, None, None], payload, 0.0), axis=0)]
    concatenate x23 -> x0, other arithmetic: 18.9 us -> none  [the longest x5 16.3 us: extended(): jnp.concatenate([lax.ppermute(tail, axis, [(i, (i + 1) % count) for i in...]
    slice x3 -> x0, other arithmetic: 17.3 us -> none  [stream_cells(): padded[direction, 1 - shift_x:1 - shift_x + size_x, 1 - shift_y:1 - shift...]
  transfers between devices with their start and end apart: 10 -> 8, of which waited for: 6 -> 4; matrix products, arithmetic and copies ran while one was open for 11% -> 0% of each run, Pallas kernels for 0% -> 0%
where the time goes in v1:
time: 66.7 us; the launch traced here: 66.5 us
  Pallas kernels  25.5 us (38%)
  waiting for transfers between devices  19.2 us (29%)
  starting transfers between devices  18.5 us (28%)
  local copies, waits for them, and re-layouts  2.67 us (4%)
  between operations  0.67 us (1%)
    ppermute x8, waiting for transfers between devices, swap(): return lax.ppermute(value, ('bx', 'by'), pairs)  19.2 us
    ppermute x8, starting transfers between devices, swap(): return lax.ppermute(value, ('bx', 'by'), pairs)  18.5 us
    pallas_call x1, Pallas kernels, on_device(): call(body, [(4, nx, ny, nz), yedge, yedge], 'svvvvvvv', [yface, yface, xf...  8.69 us
    pallas_call x1, Pallas kernels, on_device(): call(start, [populations.shape, (5, 3, 3, ny, nz), yface, yface], 'sv', [...  6.31 us
    pallas_call x1, Pallas kernels, on_device(): call(moments, [(blocks, cells), (3, blocks, cells), block, block], 'svvv'...  4.46 us
    pallas_call x1, Pallas kernels, on_device(): call(side, [xface, xface], 'svvvv', [yface, yface, xface, xface], 'side')  4.1 us
    unnamed x16, local copies, waits for them, and re-layouts  2.67 us
    pallas_call x1, Pallas kernels, on_device(): call(place, [(blocks, cells), (3, blocks, cells)], 'svvvv', [block, block...  1.98 us
  transfers between devices with their start and end apart: 8, of which 4 were waited for; matrix products, arithmetic and copies ran while one was open for 0% of the time, Pallas kernels for 0%

profile of v1, /device:TPU:16, one launch (start us, length us, event | category | flops | bytes accessed | tf_op | source)
XLA Modules:
  0.0 66.5 jit_solution(10141617819731036691)
XLA Ops:
  0.6 6.3 %start.1 = (f32[27,16,16,128]{3,2,1,0:T(8,128)}, f32[5,3,3,16,128]{4,3,2,1,0:T(8,128)}, f32[9,16,128]{2,1,0:T(8,128)}, f32[9,16,128]{2,1,0:T(8,128)}) custom-call(s32[1024]{0:T(1024)} %refs_0_.7, f32[27,16,16,128]{3,2,1,0:T(8,128)} %refs_1_.5), custom_call_target="tpu_custom_call" | custom-call | tf_op jit(solution)/shard_map/start/pallas_call | solution.py:491
  6.9 0.0 collective-permute-start
  6.9 4.2 %collective-permute-start.1 = (f32[9,16,128]{2,1,0:T(8,128)}, f32[9,16,128]{2,1,0:T(8,128)S(1)}, u32[]{:S(2)}, u32[]{:S(2)}) collective-permute-start(f32[9,16,128]{2,1,0:T(8,128)} %get-tuple-element.18), channel_id=1, source_target_pairs={{1,2},{3,4},{5,6},{7,8},{9,10},{11,12},{13,14},{15,0},{17,18},{19,... | collective-permute-start | bytes 221192 | tf_op jit(solution)/shard_map/ppermute | solution.py:466
  11.2 0.0 collective-permute-done.refs_3_.refs_4_
  11.2 2.3 %collective-permute-done.1.refs_4_.refs_5_ = f32[9,16,128]{2,1,0:T(8,128)S(1)} collective-permute-done((f32[9,16,128]{2,1,0:T(8,128)}, f32[9,16,128]{2,1,0:T(8,128)S(1)}, u32[]{:S(2)}, u32[]{:S(2)}) %collective-permute-start.1) | collective-permute-done | bytes 73760 | tf_op jit(solution)/shard_map/ppermute | solution.py:466
  13.5 0.6 copy-done.3
  14.1 4.1 %side.1 = (f32[36,16,128]{2,1,0:T(8,128)}, f32[36,16,128]{2,1,0:T(8,128)}) custom-call(s32[1024]{0:T(1024)} %refs_0_.7, f32[27,16,16,128]{3,2,1,0:T(8,128)} %refs_1_.5, f32[27,16,16,128]{3,2,1,0:T(8,128)} %get-tuple-element.15.refs_2_, f32[9,16,128]{2,1,0:T(8,128)} %copy-done.2, f32[9,16,128]{2,1,0:T(8,128)} %copy-done.3), custom_call_target="tpu_custom_call" | custom-call | tf_op jit(solution)/shard_map/side/pallas_call | solution.py:503
  18.2 3.6 %collective-permute-start.2 = (f32[36,16,128]{2,1,0:T(8,128)}, f32[36,16,128]{2,1,0:T(8,128)S(1)}, u32[]{:S(2)}, u32[]{:S(2)}) collective-permute-start(f32[36,16,128]{2,1,0:T(8,128)} %get-tuple-element.19), channel_id=1, source_target_pairs={{0,16},{32,48},{64,80},{96,112},{1,17},{33,49},{65,81},{97,113},{2... | collective-permute-start | bytes 884744 | tf_op jit(solution)/shard_map/ppermute | solution.py:466
  21.8 0.0 collective-permute-start.3
  21.8 12.0 %collective-permute-done.2.refs_6_ = f32[36,16,128]{2,1,0:T(8,128)S(1)} collective-permute-done((f32[36,16,128]{2,1,0:T(8,128)}, f32[36,16,128]{2,1,0:T(8,128)S(1)}, u32[]{:S(2)}, u32[]{:S(2)}) %collective-permute-start.2) | collective-permute-done | bytes 294944 | tf_op jit(solution)/shard_map/ppermute | solution.py:466
  33.8 0.0 collective-permute-done.3.refs_7_
  33.8 0.7 %copy-done = f32[36,16,128]{2,1,0:T(8,128)} copy-done((f32[36,16,128]{2,1,0:T(8,128)}, f32[36,16,128]{2,1,0:T(8,128)S(1)}, u32[]{:S(2)}) %copy-start) | copy-done | bytes 294936
  34.5 0.1 copy-done.1
  34.6 8.7 %body.1 = (f32[4,16,16,128]{3,2,1,0:T(8,128)}, f32[3,16,128]{2,1,0:T(8,128)}, f32[3,16,128]{2,1,0:T(8,128)}) custom-call(s32[1024]{0:T(1024)} %refs_0_.7, f32[27,16,16,128]{3,2,1,0:T(8,128)} %refs_1_.5, f32[27,16,16,128]{3,2,1,0:T(8,128)} %get-tuple-element.15.refs_2_, f32[5,3,3,16,128]{4,3,2,1,0:T(8,128)} %get-tuple-element.16.refs_3_, ...), custom_call_target="tpu_custom_call" | custom-call | tf_op jit(solution)/shard_map/body/pallas_call | solution.py:511
  43.3 0.0 collective-permute-start.4
  43.3 3.4 %collective-permute-start.5 = (f32[3,16,128]{2,1,0:T(8,128)}, f32[3,16,128]{2,1,0:T(8,128)S(1)}, u32[]{:S(2)}, u32[]{:S(2)}) collective-permute-start(f32[3,16,128]{2,1,0:T(8,128)} %get-tuple-element.23), channel_id=1, source_target_pairs={{1,2},{3,4},{5,6},{7,8},{9,10},{11,12},{13,14},{15,0},{17,18},{19,... | collective-permute-start | bytes 73736 | tf_op jit(solution)/shard_map/ppermute | solution.py:466
  46.6 2.2 %collective-permute-done.5.refs_3_ = f32[3,16,128]{2,1,0:T(8,128)S(1)} collective-permute-done((f32[3,16,128]{2,1,0:T(8,128)}, f32[3,16,128]{2,1,0:T(8,128)S(1)}, u32[]{:S(2)}, u32[]{:S(2)}) %collective-permute-start.5) | collective-permute-done | bytes 24608 | tf_op jit(solution)/shard_map/ppermute | solution.py:466
  48.9 0.6 copy-done.7
  49.5 4.5 %moments.1 = (f32[8,4096]{1,0:T(8,128)}, f32[3,8,4096]{2,1,0:T(8,128)}, f32[8,16,128]{2,1,0:T(8,128)}, f32[8,16,128]{2,1,0:T(8,128)}) custom-call(s32[8]{0:T(128)} %refs_0_.9, f32[4,16,16,128]{3,2,1,0:T(8,128)} %get-tuple-element.21.refs_1_, f32[3,16,128]{2,1,0:T(8,128)} %copy-done.6, f32[3,16,128]{2,1,0:T(8,128)} %copy-done.7), custom_call_target="tpu_custom_call" | custom-call | tf_op jit(solution)/shard_map/moments/pallas_call | solution.py:524
  53.9 7.3 %collective-permute-start.7 = (f32[8,16,128]{2,1,0:T(8,128)}, f32[8,16,128]{2,1,0:T(8,128)S(1)}, u32[]{:S(2)}, u32[]{:S(2)}) collective-permute-start(f32[8,16,128]{2,1,0:T(8,128)} %get-tuple-element.27), channel_id=1, source_target_pairs={{1,2},{3,4},{5,6},{7,8},{9,10},{11,12},{13,14},{15,16},{17,18},{19... | collective-permute-start | bytes 196616 | tf_op jit(solution)/shard_map/ppermute | solution.py:466
  61.2 0.0 collective-permute-done.6.refs_3_
  61.2 2.7 %collective-permute-done.7.refs_4_ = f32[8,16,128]{2,1,0:T(8,128)S(1)} collective-permute-done((f32[8,16,128]{2,1,0:T(8,128)}, f32[8,16,128]{2,1,0:T(8,128)S(1)}, u32[]{:S(2)}, u32[]{:S(2)}) %collective-permute-start.7) | collective-permute-done | bytes 65568 | tf_op jit(solution)/shard_map/ppermute | solution.py:466
  63.9 0.6 copy-done.5
  64.5 2.0 %place.1 = (f32[8,4096]{1,0:T(8,128)}, f32[3,8,4096]{2,1,0:T(8,128)}) custom-call(s32[8]{0:T(128)} %refs_0_.9, f32[8,4096]{1,0:T(8,128)} %get-tuple-element.24.refs_1_, f32[3,8,4096]{2,1,0:T(8,128)} %get-tuple-element.25.refs_2_, f32[8,16,128]{2,1,0:T(8,128)} %copy-done.4, f32[8,16,128]{2,1,0:T(8,128)} %copy-done.5), custom_call_target="tpu_custom_call" | custom-call | tf_op jit(solution)/shard_map/place/pallas_call | solution.py:537
  (13 shorter events, 0.0 us)
Async XLA Ops:
  6.9 4.2 %collective-permute-start = (f32[9,16,128]{2,1,0:T(8,128)}, f32[9,16,128]{2,1,0:T(8,128)S(1)}, u32[]{:S(2)}, u32[]{:S(2)}) collective-permute-start(f32[9,16,128]{2,1,0:T(8,128)} %get-tuple-element.17), channel_id=1, source_target_pairs={{0,1},{2,3},{4,5},{6,7},{8,9},{10,11},{12,13},{14,15},{16,17},{18,... | collective-permute-start | bytes 221192 | tf_op jit(solution)/shard_map/ppermute | solution.py:466
  6.9 6.5 %collective-permute-start.1 = (f32[9,16,128]{2,1,0:T(8,128)}, f32[9,16,128]{2,1,0:T(8,128)S(1)}, u32[]{:S(2)}, u32[]{:S(2)}) collective-permute-start(f32[9,16,128]{2,1,0:T(8,128)} %get-tuple-element.18), channel_id=1, source_target_pairs={{1,2},{3,4},{5,6},{7,8},{9,10},{11,12},{13,14},{15,0},{17,18},{19,... | collective-permute-start | bytes 221192 | tf_op jit(solution)/shard_map/ppermute | solution.py:466
  11.2 2.3 %copy-start.2 = (f32[9,16,128]{2,1,0:T(8,128)}, f32[9,16,128]{2,1,0:T(8,128)S(1)}, u32[]{:S(2)}) copy-start(f32[9,16,128]{2,1,0:T(8,128)S(1)} %collective-permute-done.refs_3_.refs_4_) | copy-start | bytes 221188
  13.5 0.6 copy-start.3
  18.2 15.6 %collective-permute-start.2 = (f32[36,16,128]{2,1,0:T(8,128)}, f32[36,16,128]{2,1,0:T(8,128)S(1)}, u32[]{:S(2)}, u32[]{:S(2)}) collective-permute-start(f32[36,16,128]{2,1,0:T(8,128)} %get-tuple-element.19), channel_id=1, source_target_pairs={{0,16},{32,48},{64,80},{96,112},{1,17},{33,49},{65,81},{97,113},{2... | collective-permute-start | bytes 884744 | tf_op jit(solution)/shard_map/ppermute | solution.py:466
  21.8 12.0 %collective-permute-start.3 = (f32[36,16,128]{2,1,0:T(8,128)}, f32[36,16,128]{2,1,0:T(8,128)S(1)}, u32[]{:S(2)}, u32[]{:S(2)}) collective-permute-start(f32[36,16,128]{2,1,0:T(8,128)} %get-tuple-element.20), channel_id=1, source_target_pairs={{16,32},{48,64},{80,96},{112,0},{17,33},{49,65},{81,97},{113,1},{1... | collective-permute-start | bytes 884744 | tf_op jit(solution)/shard_map/ppermute | solution.py:466
  33.8 0.7 %copy-start = (f32[36,16,128]{2,1,0:T(8,128)}, f32[36,16,128]{2,1,0:T(8,128)S(1)}, u32[]{:S(2)}) copy-start(f32[36,16,128]{2,1,0:T(8,128)S(1)} %collective-permute-done.2.refs_6_) | copy-start | bytes 884740
  33.8 0.8 %copy-start.1 = (f32[36,16,128]{2,1,0:T(8,128)}, f32[36,16,128]{2,1,0:T(8,128)S(1)}, u32[]{:S(2)}) copy-start(f32[36,16,128]{2,1,0:T(8,128)S(1)} %collective-permute-done.3.refs_7_) | copy-start | bytes 884740
  43.3 3.4 %collective-permute-start.4 = (f32[3,16,128]{2,1,0:T(8,128)}, f32[3,16,128]{2,1,0:T(8,128)S(1)}, u32[]{:S(2)}, u32[]{:S(2)}) collective-permute-start(f32[3,16,128]{2,1,0:T(8,128)} %get-tuple-element.22), channel_id=1, source_target_pairs={{0,1},{2,3},{4,5},{6,7},{8,9},{10,11},{12,13},{14,15},{16,17},{18,... | collective-permute-start | bytes 73736 | tf_op jit(solution)/shard_map/ppermute | solution.py:466
  43.3 5.6 %collective-permute-start.5 = (f32[3,16,128]{2,1,0:T(8,128)}, f32[3,16,128]{2,1,0:T(8,128)S(1)}, u32[]{:S(2)}, u32[]{:S(2)}) collective-permute-start(f32[3,16,128]{2,1,0:T(8,128)} %get-tuple-element.23), channel_id=1, source_target_pairs={{1,2},{3,4},{5,6},{7,8},{9,10},{11,12},{13,14},{15,0},{17,18},{19,... | collective-permute-start | bytes 73736 | tf_op jit(solution)/shard_map/ppermute | solution.py:466
  46.6 2.2 %copy-start.6 = (f32[3,16,128]{2,1,0:T(8,128)}, f32[3,16,128]{2,1,0:T(8,128)S(1)}, u32[]{:S(2)}) copy-start(f32[3,16,128]{2,1,0:T(8,128)S(1)} %collective-permute-done.4.refs_2_) | copy-start | bytes 73732
  48.9 0.6 copy-start.7
  53.9 7.3 %collective-permute-start.6 = (f32[8,16,128]{2,1,0:T(8,128)}, f32[8,16,128]{2,1,0:T(8,128)S(1)}, u32[]{:S(2)}, u32[]{:S(2)}) collective-permute-start(f32[8,16,128]{2,1,0:T(8,128)} %get-tuple-element.26), channel_id=1, source_target_pairs={{0,1},{2,3},{4,5},{6,7},{8,9},{10,11},{12,13},{14,15},{16,17},{18,... | collective-permute-start | bytes 196616 | tf_op jit(solution)/shard_map/ppermute | solution.py:466
  53.9 10.0 %collective-permute-start.7 = (f32[8,16,128]{2,1,0:T(8,128)}, f32[8,16,128]{2,1,0:T(8,128)S(1)}, u32[]{:S(2)}, u32[]{:S(2)}) collective-permute-start(f32[8,16,128]{2,1,0:T(8,128)} %get-tuple-element.27), channel_id=1, source_target_pairs={{1,2},{3,4},{5,6},{7,8},{9,10},{11,12},{13,14},{15,16},{17,18},{19... | collective-permute-start | bytes 196616 | tf_op jit(solution)/shard_map/ppermute | solution.py:466
  61.2 2.7 %copy-start.4 = (f32[8,16,128]{2,1,0:T(8,128)}, f32[8,16,128]{2,1,0:T(8,128)S(1)}, u32[]{:S(2)}) copy-start(f32[8,16,128]{2,1,0:T(8,128)S(1)} %collective-permute-done.6.refs_3_) | copy-start | bytes 196612
  63.9 0.6 copy-start.5

commit v2 on v1

--- a/solution.py
+++ b/solution.py
@@ -16,7 +16,7 @@
 weights = (8.0 / 27, 2.0 / 27, 1.0 / 54, 1.0 / 216)
 ROWS = 8
 LANES = 128
-VMEM_BYTES = 56 * 1024 * 1024
+VMEM_BYTES = 16 * 1024 * 1024
 
 
 def comp(a, b, e):

time: 66.7 us -> 54.4 us (0.82)
  Pallas kernels: 25.5 us -> 13.6 us
  waiting for transfers between devices: 19.2 us -> 18.2 us
    pallas_call x1, Pallas kernels: 8.69 us -> 5.22 us  [on_device(): call(body, [(4, nx, ny, nz), yedge, yedge], 'svvvvvvv', [yface, yface, xf...]
    pallas_call x1, Pallas kernels: 6.31 us -> 2.95 us  [on_device(): call(start, [populations.shape, (5, 3, 3, ny, nz), yface, yface], 'sv', [...]
    pallas_call x1, Pallas kernels: 4.1 us -> 0.8 us  [on_device(): call(side, [xface, xface], 'svvvv', [yface, yface, xface, xface], 'side')]
    pallas_call x1, Pallas kernels: 4.46 us -> 3.12 us  [on_device(): call(moments, [(blocks, cells), (3, blocks, cells), block, block], 'svvv'...]
    ppermute x8, waiting for transfers between devices: 19.2 us -> 18.2 us  [swap(): return lax.ppermute(value, ('bx', 'by'), pairs)]
    unnamed x16 -> x6, local copies, waits for them, and re-layouts: 2.67 us -> 2.68 us
where the time goes in v2:
time: 54.4 us; the launch traced here: 54.2 us
  starting transfers between devices  19 us (35%)
  waiting for transfers between devices  18.2 us (33%)
  Pallas kernels  13.6 us (25%)
  local copies, waits for them, and re-layouts  2.68 us (5%)
  between operations  0.72 us (1%)
    ppermute x8, starting transfers between devices, swap(): return lax.ppermute(value, ('bx', 'by'), pairs)  19 us
    ppermute x8, waiting for transfers between devices, swap(): return lax.ppermute(value, ('bx', 'by'), pairs)  18.2 us
    pallas_call x1, Pallas kernels, on_device(): call(body, [(4, nx, ny, nz), yedge, yedge], 'svvvvvvv', [yface, yface, xf...  5.22 us
    pallas_call x1, Pallas kernels, on_device(): call(moments, [(blocks, cells), (3, blocks, cells), block, block], 'svvv'...  3.12 us
    pallas_call x1, Pallas kernels, on_device(): call(start, [populations.shape, (5, 3, 3, ny, nz), yface, yface], 'sv', [...  2.95 us
    unnamed x6, local copies, waits for them, and re-layouts  2.68 us
    pallas_call x1, Pallas kernels, on_device(): call(place, [(blocks, cells), (3, blocks, cells)], 'svvvv', [block, block...  1.49 us
  transfers between devices with their start and end apart: 8, of which 4 were waited for; matrix products, arithmetic and copies ran while one was open for 0% of the time, Pallas kernels for 0%

profile of v2, /device:TPU:16, one launch (start us, length us, event | category | flops | bytes accessed | tf_op | source)
XLA Modules:
  0.0 54.2 jit_solution(14131007650969318749)
XLA Ops:
  0.6 2.0 %copy-done = f32[27,16,16,128]{3,2,1,0:T(8,128)S(1)} copy-done((f32[27,16,16,128]{3,2,1,0:T(8,128)S(1)}, f32[27,16,16,128]{3,2,1,0:T(8,128)}, u32[]{:S(2)}) %copy-start) | copy-done | bytes 3538968
  2.6 0.7 %copy-done.1 = s32[1024]{0:T(1024)S(1)} copy-done((s32[1024]{0:T(1024)S(1)}, s32[1024]{0:T(1024)}, u32[]{:S(2)}) %copy-start.1) | copy-done | bytes 4120
  3.3 2.9 %start.1 = (f32[27,16,16,128]{3,2,1,0:T(8,128)S(1)}, f32[5,3,3,16,128]{4,3,2,1,0:T(8,128)S(1)}, f32[9,16,128]{2,1,0:T(8,128)S(1)}, f32[9,16,128]{2,1,0:T(8,128)S(1)}) custom-call(s32[1024]{0:T(1024)S(1)} %copy-done.1, f32[27,16,16,128]{3,2,1,0:T(8,128)S(1)} %copy-done), custom_call_target="tpu_custom_call" | custom-call | tf_op jit(solution)/shard_map/start/pallas_call | solution.py:491
  6.3 0.1 collective-permute-start
  6.4 4.2 %collective-permute-start.1 = (f32[9,16,128]{2,1,0:T(8,128)S(1)}, f32[9,16,128]{2,1,0:T(8,128)S(1)}, u32[]{:S(2)}, u32[]{:S(2)}) collective-permute-start(f32[9,16,128]{2,1,0:T(8,128)S(1)} %get-tuple-element.18), channel_id=1, source_target_pairs={{1,2},{3,4},{5,6},{7,8},{9,10},{11,12},{13,14},{15,0},{17,18},{19,... | collective-permute-start | bytes 221192 | tf_op jit(solution)/shard_map/ppermute | solution.py:466
  10.6 0.0 collective-permute-done.refs_3_.refs_4_
  10.6 2.0 %collective-permute-done.1.refs_4_.refs_5_ = f32[9,16,128]{2,1,0:T(8,128)S(1)} collective-permute-done((f32[9,16,128]{2,1,0:T(8,128)S(1)}, f32[9,16,128]{2,1,0:T(8,128)S(1)}, u32[]{:S(2)}, u32[]{:S(2)}) %collective-permute-start.1) | collective-permute-done | bytes 73760 | tf_op jit(solution)/shard_map/ppermute | solution.py:466
  12.6 0.8 %side.1 = (f32[36,16,128]{2,1,0:T(8,128)S(1)}, f32[36,16,128]{2,1,0:T(8,128)S(1)}) custom-call(s32[1024]{0:T(1024)S(1)} %copy-done.1, f32[27,16,16,128]{3,2,1,0:T(8,128)S(1)} %copy-done, f32[27,16,16,128]{3,2,1,0:T(8,128)S(1)} %get-tuple-element.15.refs_2_, f32[9,16,128]{2,1,0:T(8,128)S(1)} %collective-permute-done.refs_3_.refs_4_, ...), custom_call_target="tpu_custom_call" | custom-call | tf_op jit(solution)/shard_map/side/pallas_call | solution.py:503
  13.4 3.7 %collective-permute-start.2 = (f32[36,16,128]{2,1,0:T(8,128)S(1)}, f32[36,16,128]{2,1,0:T(8,128)S(1)}, u32[]{:S(2)}, u32[]{:S(2)}) collective-permute-start(f32[36,16,128]{2,1,0:T(8,128)S(1)} %get-tuple-element.19), channel_id=1, source_target_pairs={{0,16},{32,48},{64,80},{96,112},{1,17},{33,49},{65,81},{97,113},{2... | collective-permute-start | bytes 884744 | tf_op jit(solution)/shard_map/ppermute | solution.py:466
  17.1 0.0 collective-permute-start.3
  17.1 11.8 %collective-permute-done.2.refs_6_ = f32[36,16,128]{2,1,0:T(8,128)S(1)} collective-permute-done((f32[36,16,128]{2,1,0:T(8,128)S(1)}, f32[36,16,128]{2,1,0:T(8,128)S(1)}, u32[]{:S(2)}, u32[]{:S(2)}) %collective-permute-start.2) | collective-permute-done | bytes 294944 | tf_op jit(solution)/shard_map/ppermute | solution.py:466
  28.9 0.0 collective-permute-done.3.refs_7_
  28.9 5.2 %body.1 = (f32[4,16,16,128]{3,2,1,0:T(8,128)S(1)}, f32[3,16,128]{2,1,0:T(8,128)S(1)}, f32[3,16,128]{2,1,0:T(8,128)S(1)}) custom-call(s32[1024]{0:T(1024)S(1)} %copy-done.1, f32[27,16,16,128]{3,2,1,0:T(8,128)S(1)} %copy-done, f32[27,16,16,128]{3,2,1,0:T(8,128)S(1)} %get-tuple-element.15.refs_2_, f32[5,3,3,16,128]{4,3,2,1,0:T(8,128)S(1)} %get-tuple-element.16.refs_3_, ...), custom_call_target="tpu_custom_call" | custom-call | tf_op jit(solution)/shard_map/body/pallas_call | solution.py:511
  34.2 0.1 collective-permute-start.4
  34.2 3.5 %collective-permute-start.5 = (f32[3,16,128]{2,1,0:T(8,128)S(1)}, f32[3,16,128]{2,1,0:T(8,128)S(1)}, u32[]{:S(2)}, u32[]{:S(2)}) collective-permute-start(f32[3,16,128]{2,1,0:T(8,128)S(1)} %get-tuple-element.23), channel_id=1, source_target_pairs={{1,2},{3,4},{5,6},{7,8},{9,10},{11,12},{13,14},{15,0},{17,18},{19,... | collective-permute-start | bytes 73736 | tf_op jit(solution)/shard_map/ppermute | solution.py:466
  37.8 0.0 collective-permute-done.4.refs_2_
  37.8 1.9 %collective-permute-done.5.refs_3_ = f32[3,16,128]{2,1,0:T(8,128)S(1)} collective-permute-done((f32[3,16,128]{2,1,0:T(8,128)S(1)}, f32[3,16,128]{2,1,0:T(8,128)S(1)}, u32[]{:S(2)}, u32[]{:S(2)}) %collective-permute-start.5) | collective-permute-done | bytes 24608 | tf_op jit(solution)/shard_map/ppermute | solution.py:466
  39.7 0.0 copy-done.2
  39.7 3.1 %moments.1 = (f32[8,4096]{1,0:T(8,128)S(1)}, f32[3,8,4096]{2,1,0:T(8,128)S(1)}, f32[8,16,128]{2,1,0:T(8,128)S(1)}, f32[8,16,128]{2,1,0:T(8,128)S(1)}) custom-call(s32[8]{0:T(128)S(1)} %copy-done.2, f32[4,16,16,128]{3,2,1,0:T(8,128)S(1)} %get-tuple-element.21.refs_1_, f32[3,16,128]{2,1,0:T(8,128)S(1)} %collective-permute-done.4.refs_2_, ...), custom_call_target="tpu_custom_call" | custom-call | tf_op jit(solution)/shard_map/moments/pallas_call | solution.py:524
  42.8 0.1 collective-permute-start.6
  42.9 7.4 %collective-permute-start.7 = (f32[8,16,128]{2,1,0:T(8,128)S(1)}, f32[8,16,128]{2,1,0:T(8,128)S(1)}, u32[]{:S(2)}, u32[]{:S(2)}) collective-permute-start(f32[8,16,128]{2,1,0:T(8,128)S(1)} %get-tuple-element.27), channel_id=1, source_target_pairs={{1,2},{3,4},{5,6},{7,8},{9,10},{11,12},{13,14},{15,16},{17,18},{19... | collective-permute-start | bytes 196616 | tf_op jit(solution)/shard_map/ppermute | solution.py:466
  50.3 0.0 collective-permute-done.6.refs_3_
  50.3 2.4 %collective-permute-done.7.refs_4_ = f32[8,16,128]{2,1,0:T(8,128)S(1)} collective-permute-done((f32[8,16,128]{2,1,0:T(8,128)S(1)}, f32[8,16,128]{2,1,0:T(8,128)S(1)}, u32[]{:S(2)}, u32[]{:S(2)}) %collective-permute-start.7) | collective-permute-done | bytes 65568 | tf_op jit(solution)/shard_map/ppermute | solution.py:466
  52.7 1.5 %place.1 = (f32[8,4096]{1,0:T(8,128)}, f32[3,8,4096]{2,1,0:T(8,128)}) custom-call(s32[8]{0:T(128)S(1)} %copy-done.2, f32[8,4096]{1,0:T(8,128)S(1)} %get-tuple-element.24.refs_1_, f32[3,8,4096]{2,1,0:T(8,128)S(1)} %get-tuple-element.25.refs_2_, f32[8,16,128]{2,1,0:T(8,128)S(1)} %collective-permute-done.6.refs_3_, f32[8,16,128]{2,1,0:T(8,128)S(1)} %collective-permute-done.7.refs_4_), custom_call_target="tpu_custom_call" | custom-call | tf_op jit(solution)/shard_map/place/pallas_call | solution.py:537
  (3 shorter events, 0.0 us)
Async XLA Ops:
  0.6 2.0 %copy-start = (f32[27,16,16,128]{3,2,1,0:T(8,128)S(1)}, f32[27,16,16,128]{3,2,1,0:T(8,128)}, u32[]{:S(2)}) copy-start(f32[27,16,16,128]{3,2,1,0:T(8,128)} %refs_1_.5) | copy-start | bytes 10616836
  2.6 0.7 %copy-start.1 = (s32[1024]{0:T(1024)S(1)}, s32[1024]{0:T(1024)}, u32[]{:S(2)}) copy-start(s32[1024]{0:T(1024)} %refs_0_.7) | copy-start | bytes 12292
  6.3 4.3 %collective-permute-start = (f32[9,16,128]{2,1,0:T(8,128)S(1)}, f32[9,16,128]{2,1,0:T(8,128)S(1)}, u32[]{:S(2)}, u32[]{:S(2)}) collective-permute-start(f32[9,16,128]{2,1,0:T(8,128)S(1)} %get-tuple-element.17), channel_id=1, source_target_pairs={{0,1},{2,3},{4,5},{6,7},{8,9},{10,11},{12,13},{14,15},{16,17},{18,... | collective-permute-start | bytes 221192 | tf_op jit(solution)/shard_map/ppermute | solution.py:466
  6.4 6.2 %collective-permute-start.1 = (f32[9,16,128]{2,1,0:T(8,128)S(1)}, f32[9,16,128]{2,1,0:T(8,128)S(1)}, u32[]{:S(2)}, u32[]{:S(2)}) collective-permute-start(f32[9,16,128]{2,1,0:T(8,128)S(1)} %get-tuple-element.18), channel_id=1, source_target_pairs={{1,2},{3,4},{5,6},{7,8},{9,10},{11,12},{13,14},{15,0},{17,18},{19,... | collective-permute-start | bytes 221192 | tf_op jit(solution)/shard_map/ppermute | solution.py:466
  13.4 15.5 %collective-permute-start.2 = (f32[36,16,128]{2,1,0:T(8,128)S(1)}, f32[36,16,128]{2,1,0:T(8,128)S(1)}, u32[]{:S(2)}, u32[]{:S(2)}) collective-permute-start(f32[36,16,128]{2,1,0:T(8,128)S(1)} %get-tuple-element.19), channel_id=1, source_target_pairs={{0,16},{32,48},{64,80},{96,112},{1,17},{33,49},{65,81},{97,113},{2... | collective-permute-start | bytes 884744 | tf_op jit(solution)/shard_map/ppermute | solution.py:466
  17.1 11.8 %collective-permute-start.3 = (f32[36,16,128]{2,1,0:T(8,128)S(1)}, f32[36,16,128]{2,1,0:T(8,128)S(1)}, u32[]{:S(2)}, u32[]{:S(2)}) collective-permute-start(f32[36,16,128]{2,1,0:T(8,128)S(1)} %get-tuple-element.20), channel_id=1, source_target_pairs={{16,32},{48,64},{80,96},{112,0},{17,33},{49,65},{81,97},{113,1},{1... | collective-permute-start | bytes 884744 | tf_op jit(solution)/shard_map/ppermute | solution.py:466
  28.9 10.8 %copy-start.2 = (s32[8]{0:T(128)S(1)}, s32[8]{0:T(128)}, u32[]{:S(2)}) copy-start(s32[8]{0:T(128)} %refs_0_.9) | copy-start | bytes 100
  34.2 3.6 %collective-permute-start.4 = (f32[3,16,128]{2,1,0:T(8,128)S(1)}, f32[3,16,128]{2,1,0:T(8,128)S(1)}, u32[]{:S(2)}, u32[]{:S(2)}) collective-permute-start(f32[3,16,128]{2,1,0:T(8,128)S(1)} %get-tuple-element.22), channel_id=1, source_target_pairs={{0,1},{2,3},{4,5},{6,7},{8,9},{10,11},{12,13},{14,15},{16,17},{18,... | collective-permute-start | bytes 73736 | tf_op jit(solution)/shard_map/ppermute | solution.py:466
  34.2 5.4 %collective-permute-start.5 = (f32[3,16,128]{2,1,0:T(8,128)S(1)}, f32[3,16,128]{2,1,0:T(8,128)S(1)}, u32[]{:S(2)}, u32[]{:S(2)}) collective-permute-start(f32[3,16,128]{2,1,0:T(8,128)S(1)} %get-tuple-element.23), channel_id=1, source_target_pairs={{1,2},{3,4},{5,6},{7,8},{9,10},{11,12},{13,14},{15,0},{17,18},{19,... | collective-permute-start | bytes 73736 | tf_op jit(solution)/shard_map/ppermute | solution.py:466
  42.8 7.5 %collective-permute-start.6 = (f32[8,16,128]{2,1,0:T(8,128)S(1)}, f32[8,16,128]{2,1,0:T(8,128)S(1)}, u32[]{:S(2)}, u32[]{:S(2)}) collective-permute-start(f32[8,16,128]{2,1,0:T(8,128)S(1)} %get-tuple-element.26), channel_id=1, source_target_pairs={{0,1},{2,3},{4,5},{6,7},{8,9},{10,11},{12,13},{14,15},{16,17},{18,... | collective-permute-start | bytes 196616 | tf_op jit(solution)/shard_map/ppermute | solution.py:466
  42.9 9.8 %collective-permute-start.7 = (f32[8,16,128]{2,1,0:T(8,128)S(1)}, f32[8,16,128]{2,1,0:T(8,128)S(1)}, u32[]{:S(2)}, u32[]{:S(2)}) collective-permute-start(f32[8,16,128]{2,1,0:T(8,128)S(1)} %get-tuple-element.27), channel_id=1, source_target_pairs={{1,2},{3,4},{5,6},{7,8},{9,10},{11,12},{13,14},{15,16},{17,18},{19... | collective-permute-start | bytes 196616 | tf_op jit(solution)/shard_map/ppermute | solution.py:466

commit v3 on v2

v3 whole, which is shorter than its diff:
```python
import functools
import math

import jax
import jax.numpy as jnp
import numpy as np
from jax import lax
from jax.experimental import pallas as pl
from jax.experimental.pallas import tpu as pltpu
from jax.sharding import PartitionSpec as P

tau_coarse = 0.56
tau_fine = 0.62
scale_to_fine = tau_fine / (2.0 * tau_coarse)
scale_to_coarse = 2.0 * tau_coarse / tau_fine
smagorinsky = 18.0 * math.sqrt(2.0) * 0.17 * 0.17
weights = (8.0 / 27, 2.0 / 27, 1.0 / 54, 1.0 / 216)
ROWS = 8
LANES = 128
VMEM_BYTES = 16 * 1024 * 1024


def comp(a, b, e):
    return 9 * (a + 1) + 3 * (b + 1) + (e + 1)


def face(b, e):
    return 3 * (b + 1) + (e + 1)


DIRS = [(a, b, e) for a in (-1, 0, 1) for b in (-1, 0, 1) for e in (-1, 0, 1)]
HALF = [c for c in DIRS if c > (0, 0, 0)]


def lane_block(edge):
    return lax.broadcasted_iota(jnp.int32, (ROWS, LANES), 1) // edge


def sublane():
    return lax.broadcasted_iota(jnp.int32, (ROWS, LANES), 0)


def column_level(levels, shape, blocks, dx, dy):
    count_x, count_y = shape
    ix = lax.rem(lax.axis_index("bx") + (dx + count_x), count_x)
    iy = lax.rem(lax.axis_index("by") + (dy + count_y), count_y)
    base = (ix * count_y + iy) * blocks
    block = lane_block(LANES // blocks)
    value = jnp.full((ROWS, LANES), levels[base], jnp.int32)
    for k in range(1, blocks):
        value = jnp.where(block == k, levels[base + k], value)
    return value


def lane_roll(tile, by):
    return tile if by == 0 else pltpu.roll(tile, by % LANES, 1)


def group_sums(get):
    total, diff, quad = {}, {}, {}
    for b in (-1, 0, 1):
        low, mid, high = (get(b, e) for e in (-1, 0, 1))
        quad[b] = low + high
        total[b] = quad[b] + mid
        diff[b] = high - low
    both = total[-1] + total[1]
    return (
        both + total[0],
        total[1] - total[-1],
        both,
        diff[-1] + diff[0] + diff[1],
        diff[1] - diff[-1],
        quad[-1] + quad[0] + quad[1],
    )


def add_sums(first, second):
    return tuple(p + q for p, q in zip(first, second))


def collide(groups, get, fine, everywhere, factor, put, dirs=None):
    low, mid, high = (groups[a] for a in (-1, 0, 1))
    ends = add_sums(low, high)
    rho, jy, pyy, jz, pyz, pzz = add_sums(ends, mid)
    pxx = ends[0]
    jx, pxy, pxz = high[0] - low[0], high[1] - low[1], high[3] - low[3]
    inv = 1.0 / rho
    ux, uy, uz = jx * inv, jy * inv, jz * inv
    third = rho * (1.0 / 3.0)
    pxx = pxx - third - jx * ux
    pyy = pyy - third - jy * uy
    pzz = pzz - third - jz * uz
    pxy = pxy - jx * uy
    pxz = pxz - jx * uz
    pyz = pyz - jy * uz
    norm = jnp.sqrt(
        pxx * pxx + pyy * pyy + pzz * pzz + 2.0 * (pxy * pxy + pxz * pxz + pyz * pyz)
    )
    base_time = jnp.where(fine, tau_fine, tau_coarse)
    tau = 0.5 * (base_time + jnp.sqrt(base_time * base_time + smagorinsky * norm * inv))
    keep = 1.0 - 1.0 / tau
    if not everywhere:
        keep = jnp.where(fine, keep, 1.0)
    base = 1.0 - 1.5 * (ux * ux + uy * uy + uz * uz)
    scaled = [rho * w for w in weights]
    rest = [s * base for s in scaled]
    vx, vy, vz = 3.0 * ux, 3.0 * uy, 3.0 * uz
    vel = {(0, 0, 1): vz, (0, 1, 0): vy, (1, 0, 0): vx}
    vel[0, 1, 1], vel[0, 1, -1] = vy + vz, vy - vz
    vel[1, 0, 1], vel[1, 0, -1] = vx + vz, vx - vz
    vel[1, 1, 0], vel[1, -1, 0] = vx + vy, vx - vy
    for b in (-1, 1):
        for e in (-1, 1):
            vel[1, b, e] = vel[1, b, 0] + (vz if e > 0 else -vz)

    def emit(c, balance):
        if dirs is not None and c not in dirs:
            return
        gain = keep if c == (0, 0, 0) else keep * factor(c)
        put(c, balance + gain * (get(c) - balance))

    emit((0, 0, 0), rest[0])
    for c in HALF:
        n = sum(abs(k) for k in c)
        odd = scaled[n] * vel[c]
        even = rest[n] + 0.5 * odd * vel[c]
        emit(c, even + odd)
        emit(tuple(-k for k in c), even - odd)


def sums_of(get):
    return {a: group_sums(lambda b, e, a=a: get((a, b, e))) for a in (-1, 0, 1)}


def level_factor(here, there_rows, e):
    scale = jnp.where(here == 1, scale_to_coarse, scale_to_fine)
    return jnp.where(lane_roll(there_rows, -e) != here, scale, 1.0)


def fill_factors(levels, shape, blocks, table):
    lev = {
        (dx, dy): column_level(levels, shape, blocks, dx, dy)
        for dx in (-1, 0, 1)
        for dy in (-1, 0, 1)
    }
    row = sublane()
    for k, (own, dx) in enumerate(((0, -1), (0, 0), (0, 1), (-1, 0), (1, 0))):
        here = lev[own, 0]
        for e in (-1, 0, 1):
            plain = level_factor(here, lev[dx, 0], e)
            for b in (-1, 0, 1):
                low, high = plain, plain
                if b == -1:
                    low = jnp.where(row == 0, level_factor(here, lev[dx, -1], e), plain)
                if b == 1:
                    high = jnp.where(row == ROWS - 1, level_factor(here, lev[dx, 1], e), plain)
                table[k, b + 1, e + 1, 0:8, :] = low
                table[k, b + 1, e + 1, 8:16, :] = high


def x_side(a, x, last):
    if a == 0:
        return 1
    return jnp.where(x == (0 if a < 0 else last), 1 + a, 1)


def store_by_parity(odd, first, second, up, down):
    @pl.when(odd == 0)
    def _():
        first[...] = up[...]
        second[...] = down[...]

    @pl.when(odd == 1)
    def _():
        first[...] = down[...]
        second[...] = up[...]


def face_kernel(shape, blocks, levels, f, pay_a, pay_b, up, down):
    _, nx, ny, nz = f.shape
    flat = f.reshape(27 * nx * ny, nz)
    here = column_level(levels, shape, blocks, 0, 0)
    row = sublane()
    for b, y, pay in ((1, ny - 1, up), (-1, 0, down)):
        near = [column_level(levels, shape, blocks, dx, b) for dx in (-1, 0, 1)]
        plain = {e: level_factor(here, near[1], e) for e in (-1, 0, 1)}
        for x in range(0, nx, ROWS):

            def get(c):
                return flat[pl.ds((comp(*c) * nx + x) * ny + y, ROWS, stride=ny), :]

            def factor(c):
                if c[0] == -1 and x == 0:
                    return jnp.where(row == 0, level_factor(here, near[0], c[2]), plain[c[2]])
                if c[0] == 1 and x + ROWS == nx:
                    return jnp.where(
                        row == ROWS - 1, level_factor(here, near[2], c[2]), plain[c[2]]
                    )
                return plain[c[2]]

            def put(c, value):
                pay[face(c[0], c[2]), x : x + ROWS, :] = value

            collide(
                sums_of(get), get, here == 1, False, factor, put, [c for c in DIRS if c[1] == b]
            )
    store_by_parity(lax.rem(lax.axis_index("by"), 2), pay_a, pay_b, up, down)


def first_collide(f, table, fine, x, near, put):
    for h in (0, 1):
        rows = slice(8 * h, 8 * h + 8)

        def get(c):
            return f[comp(*c), x, rows, :]

        def factor(c):
            return table[near(c[0]), c[1] + 1, c[2] + 1, rows, :]

        collide(sums_of(get), get, fine, False, factor, lambda c, value: put(c, rows, value))


def edge_kernel(shape, blocks, levels, f, table, out):
    fill_factors(levels, shape, blocks, table)
    fine = column_level(levels, shape, blocks, 0, 0) == 1
    nx = f.shape[1]
    for k, x in enumerate((0, 1, nx - 2, nx - 1)):

        def near(a):
            return 1 + a if (x, a) in ((0, -1), (nx - 1, 1)) else 1

        def put(c, rows, value):
            out[comp(*c), k, rows, :] = value

        first_collide(f, table, fine, x, near, put)


def shifted_read(g, above, below, row, c, k, x, h):
    a, b, e = c
    i = comp(a, b, e)
    if b == 0:
        tile = g[i, k, 8 * h : 8 * h + 8, :]
    elif b == 1:
        if h == 1:
            tile = g[i, k, 7:15, :]
        else:
            tile = pltpu.roll(g[i, k, 0:8, :], 1, 0)
            tile = jnp.where(row == 0, below[face(a, e), pl.ds(x, 1), :], tile)
    else:
        if h == 0:
            tile = g[i, k, 1:9, :]
        else:
            tile = pltpu.roll(g[i, k, 8:16, :], 7, 0)
            tile = jnp.where(row == 7, above[face(a, e), pl.ds(x, 1), :], tile)
    return lane_roll(tile, e)


def load_by_parity(odd, first, second, above, below):
    @pl.when(odd == 0)
    def _():
        above[...] = first[...]
        below[...] = second[...]

    @pl.when(odd == 1)
    def _():
        above[...] = second[...]
        below[...] = first[...]


def side_kernel(
    shape, blocks, levels, f, g, got_a, got_b, pay_a, pay_b, above, below, up, down
):
    load_by_parity(lax.rem(lax.axis_index("by"), 2), got_a, got_b, above, below)
    fine = column_level(levels, shape, blocks, 0, 0) == 1
    row = sublane()
    nx = f.shape[1]
    for ad, x, inner, k, near, pay in ((1, nx - 1, nx - 2, 3, 2, up), (-1, 0, 1, 0, 1, down)):
        for h in (0, 1):
            rows = slice(8 * h, 8 * h + 8)

            def old(c):
                return f[comp(*c), x, rows, :]

            def flat(b, e):
                moved = shifted_read(g, above, below, row, (0, b, e), k, x, h)
                return jnp.where(fine, moved, old((0, b, e)))

            for b in (-1, 0, 1):
                for e in (-1, 0, 1):
                    c = (ad, b, e)
                    pay[face(b, e), rows, :] = shifted_read(g, above, below, row, c, k, x, h)
                    moved = shifted_read(g, above, below, row, c, near, inner, h)
                    pay[9 + face(b, e), rows, :] = jnp.where(fine, moved, old(c))
            middle = group_sums(flat)
            back = group_sums(lambda b, e: old((-ad, b, e)))
            back = [jnp.where(fine, 0.0, s) for s in back]
            parts = [middle[0], middle[1], middle[2] + back[2], middle[3]]
            parts += [middle[4] + back[4], middle[5] + back[5], back[0], back[1], back[3]]
            for n, part in enumerate(parts):
                pay[18 + n, rows, :] = part
    store_by_parity(lax.rem(lax.axis_index("bx"), 2), pay_a, pay_b, up, down)


def second_collide(groups, get, fine, factor, put, dirs):
    made = {}

    def keep(c, value):
        made[c] = value

    collide(groups, get, fine, True, factor, keep, dirs)
    for a in (-1, 0, 1):
        if dirs is not None and (a, 0, 0) not in dirs:
            continue
        for b in (-1, 0, 1):
            plus = lane_roll(made[a, b, 1], 1)
            minus = lane_roll(made[a, b, -1], -1)
            put(a, b, made[a, b, 0] + (plus + minus), plus - minus)


def gather_layer(sums, row, put, up, down):
    total, cross, along = {}, {}, {}
    for b in (-1, 0, 1):
        for h in (0, 1):
            low, mid, high = (sums(a, b, 0, h) for a in (1, 0, -1))
            total[b, h] = low + mid + high
            cross[b, h] = low - high
            along[b, h] = sums(1, b, 1, h) + sums(0, b, 1, h) + sums(-1, b, 1, h)
    for n, part in enumerate((total, cross, along)):
        up(n, part[1, 1][7:8])
        down(n, part[-1, 0][0:1])
        rise = [pltpu.roll(part[1, h], 1, 0) for h in (0, 1)]
        fall = [pltpu.roll(part[-1, h], 7, 0) for h in (0, 1)]
        rise = [jnp.where(row == 0, 0.0, rise[0]), jnp.where(row == 0, rise[0], rise[1])]
        fall = [jnp.where(row == 7, fall[1], fall[0]), jnp.where(row == 7, 0.0, fall[1])]
        for h in (0, 1):
            put((0, 1, 3)[n], h, part[0, h] + rise[h] + fall[h])
            if n == 0:
                put(2, h, rise[h] - fall[h])


def turns():
    row = sublane()
    reflect = (lane_block(LANES // ROWS) - row) & (ROWS - 1)
    turn = (lane_block(1) + row * (LANES // ROWS)) & (LANES - 1)
    return reflect, turn


def block_rows(tile, reflect, turn):
    tile = pltpu.roll(tile, 0, 1, stride=LANES // ROWS, stride_axis=0)
    tile = jnp.take_along_axis(tile, reflect, axis=0)
    return jnp.take_along_axis(tile, turn, axis=1)


def inner_kernel(
    shape, blocks, levels, f, edges, table, ya, yb, tie, sums, made, up, down,
    above, below, g, state,
):
    load_by_parity(lax.rem(lax.axis_index("by"), 2), ya, yb, above, below)
    fine = column_level(levels, shape, blocks, 0, 0) == 1
    row = sublane()
    reflect, turn = turns()
    nx = f.shape[1]
    for k, x in enumerate((0, 1, nx - 2, nx - 1)):
        g[:, x, :, :] = edges[:, k, :, :]

    def first(x, carry):
        def put(c, rows, value):
            g[comp(*c), x, rows, :] = value

        first_collide(f, table, fine, x, lambda a: 1, put)
        return carry

    lax.fori_loop(2, nx - 2, first, 0)

    def second(x, carry):
        for h in (0, 1):
            rows = slice(8 * h, 8 * h + 8)

            def moved(c):
                tile = shifted_read(g, above, below, row, c, x - c[0], x - c[0], h)
                tile = jnp.where(fine, tile, f[comp(*c), x, rows, :])
                state[comp(*c), rows, :] = tile
                return tile

            def put(a, b, total, along):
                sums[a + 1, b + 1, 0, x, rows, :] = total
                sums[a + 1, b + 1, 1, x, rows, :] = along

            second_collide(
                sums_of(moved),
                lambda c: state[comp(*c), rows, :],
                fine,
                lambda c: table[1, c[1] + 1, c[2] + 1, rows, :],
                put,
                None,
            )
        return carry

    lax.fori_loop(1, nx - 1, second, 0)

    def gather(x, carry):
        def put(n, h, tile):
            made[2 * n + h, pl.ds(x * ROWS, ROWS), :] = block_rows(tile, reflect, turn)

        def put_up(n, value):
            up[n, pl.ds(x, 1), :] = value

        def put_down(n, value):
            down[n, pl.ds(x, 1), :] = value

        gather_layer(
            lambda a, b, q, h: sums[a + 1, b + 1, q, x - a, 8 * h : 8 * h + 8, :],
            row, put, put_up, put_down,
        )
        return carry

    lax.fori_loop(2, nx - 2, gather, 0)


def outer_kernel(
    shape, blocks, levels, f, g, table, ya, yb, xa, xb, sums, in_up, in_down,
    part, pay_a, pay_b, above, below, right, left, state, ends, up, down,
):
    load_by_parity(lax.rem(lax.axis_index("by"), 2), ya, yb, above, below)
    load_by_parity(lax.rem(lax.axis_index("bx"), 2), xa, xb, right, left)
    fine = {dx: column_level(levels, shape, blocks, dx, 0) == 1 for dx in (-1, 0, 1)}
    row = sublane()
    reflect, turn = turns()
    nx = f.shape[1]
    hold = {-1: 0, 0: 1, nx - 1: 2, nx: 3}
    at = {0: 0, 1: 1, nx - 2: 2, nx - 1: 3}
    for side, x, k, pay in ((-1, 0, 3, left), (1, nx - 1, 4, right)):
        for h in (0, 1):
            rows = slice(8 * h, 8 * h + 8)

            def keep(slot):
                def put(a, b, total, along):
                    ends[a + 1, b + 1, 0, slot, rows, :] = total
                    ends[a + 1, b + 1, 1, slot, rows, :] = along

                return put

            def read(c, x):
                return shifted_read(g, above, below, row, c, at[x], x, h)

            def moved(c):
                a, b, e = c
                if a == -side:
                    tile = pay[face(b, e), rows, :]
                else:
                    tile = read(c, x - a)
                tile = jnp.where(fine[0], tile, f[comp(*c), x, rows, :])
                state[comp(*c), rows, :] = tile
                return tile

            second_collide(
                sums_of(moved),
                lambda c: state[comp(*c), rows, :],
                fine[0],
                lambda c: table[1, c[1] + 1, c[2] + 1, rows, :],
                keep(hold[x]),
                [c for c in DIRS if c[0] != side],
            )
            got = [pay[18 + n, rows, :] for n in range(9)]
            own = group_sums(lambda b, e: read((side, b, e), x))
            own = [jnp.where(fine[side], s, 0.0) for s in own]
            outer = (own[0] + got[6], own[1] + got[7], own[2], own[3] + got[8], own[4], own[5])

            def toward(c):
                return pay[9 + face(c[1], c[2]), rows, :]

            second_collide(
                {
                    side: outer,
                    0: tuple(got[:6]),
                    -side: group_sums(lambda b, e: toward((-side, b, e))),
                },
                toward,
                fine[side],
                lambda c: table[k, c[1] + 1, c[2] + 1, rows, :],
                keep(hold[x + side]),
                [c for c in DIRS if c[0] == -side],
            )
    up[...] = in_up[...]
    down[...] = in_down[...]
    for m, x in enumerate((0, 1, nx - 2, nx - 1)):

        def fetch(a, b, q, h):
            rows = slice(8 * h, 8 * h + 8)
            if x - a in hold:
                return ends[a + 1, b + 1, q, hold[x - a], rows, :]
            return sums[a + 1, b + 1, q, x - a, rows, :]

        def put(n, h, tile):
            part[2 * n + h, ROWS * m : ROWS * m + ROWS, :] = tile

        def put_up(n, value):
            up[n, x : x + 1, :] = value

        def put_down(n, value):
            down[n, x : x + 1, :] = value

        gather_layer(fetch, row, put, put_up, put_down)
    for pay in (up, down):
        for n in range(3):
            for x in range(0, nx, ROWS):
                rows = slice(x, x + ROWS)
                pay[n, rows, :] = block_rows(pay[n, rows, :], reflect, turn)
    store_by_parity(lax.rem(lax.axis_index("by"), 2), pay_a, pay_b, up, down)


def turn_kernel(part, out):
    reflect, turn = turns()
    for n in range(part.shape[0]):
        for m in range(4):
            rows = slice(ROWS * m, ROWS * m + ROWS)
            out[n, rows, :] = block_rows(part[n, rows, :], reflect, turn)


def leaving(slots, blocks, step):
    here = lax.axis_index("bx") * lax.axis_size("by") + lax.axis_index("by")
    which = jnp.int32(-1)
    for k in range(blocks):
        which = jnp.where(slots[k] // blocks == here + step, k, which)
    return which


def moments_kernel(
    blocks, slots, inner, outer, got_a, got_b, rho_out, vel_out, pay_a, pay_b,
    above, below, made, up, down,
):
    odd = lax.rem(lax.axis_index("by"), 2)
    load_by_parity(odd, got_a, got_b, above, below)
    nx = above.shape[1]
    width = LANES // ROWS
    group = lane_block(width)
    at = {0: 0, 1: 1, nx - 2: 2, nx - 1: 3}
    for x in range(nx):
        for h in (0, 1):
            rows = slice(ROWS * x, ROWS * x + ROWS)
            spot, halo, sign = (0, below, 1.0) if h == 0 else (ROWS - 1, above, -1.0)
            first = x // ROWS * ROWS
            extra = []
            for n in range(3):
                tile = lane_roll(halo[n, first : first + ROWS, :], width * (spot - x % ROWS))
                extra.append(jnp.where(group == spot, tile, 0.0))
            total, cross, along = extra
            values = []
            for n, more in enumerate((total, cross, sign * total, along)):
                if x in at:
                    tile = outer[2 * n + h, ROWS * at[x] : ROWS * at[x] + ROWS, :]
                else:
                    tile = inner[2 * n + h, rows, :]
                values.append(tile + more)
            inv = 1.0 / values[0]
            lanes = slice((2 * x + h) * LANES, (2 * x + h + 1) * LANES)
            for n in range(4):
                tile = values[0] if n == 0 else values[n] * inv
                made[2 * n + h, rows, :] = tile
                if n == 0:
                    rho_out[:, lanes] = tile
                else:
                    vel_out[n - 1, :, lanes] = tile
    for step, pay in ((1, up), (-1, down)):
        which = jnp.maximum(leaving(slots, blocks, step), 0)
        for n in range(8):
            pay[n, :, :] = made[n, pl.ds(which, nx, stride=ROWS), :]
    store_by_parity(odd, pay_a, pay_b, up, down)


def place_kernel(blocks, slots, rho, vel, got_a, got_b, rho_out, vel_out, after, before):
    odd = lax.rem(lax.axis_index("by"), 2)
    load_by_parity(odd, got_a, got_b, after, before)
    row = sublane()
    to_next = row == leaving(slots, blocks, 1)
    to_prev = row == leaving(slots, blocks, -1)
    for x in range(after.shape[1]):
        for h in (0, 1):
            lanes = slice((2 * x + h) * LANES, (2 * x + h + 1) * LANES)
            for n in range(4):
                k = 2 * n + h
                tile = rho[:, lanes] if n == 0 else vel[n - 1, :, lanes]
                tile = jnp.where(to_next, after[k, x : x + 1, :], tile)
                tile = jnp.where(to_prev, before[k, x : x + 1, :], tile)
                if n == 0:
                    rho_out[:, lanes] = tile
                else:
                    vel_out[n - 1, :, lanes] = tile


def swap(value, axis, odd, curve=False):
    count_x, count_y = lax.axis_size("bx"), lax.axis_size("by")
    pairs = []
    if curve:
        pairs = [(j, j + 1) for j in range(odd, count_x * count_y - 1, 2)]
    elif axis == "by":
        for x in range(count_x):
            for y in range(odd, count_y, 2):
                pairs.append((x * count_y + y, x * count_y + (y + 1) % count_y))
    else:
        for y in range(count_y):
            for x in range(odd, count_x, 2):
                pairs.append((x * count_y + y, (x + 1) % count_x * count_y + y))
    pairs = pairs + [(b, a) for a, b in pairs]
    return lax.ppermute(value, ("bx", "by"), pairs)


def call(kernel, outs, specs, scratch, name, work):
    space = {"v": pltpu.VMEM, "s": pltpu.SMEM, "a": pl.ANY}
    return pl.pallas_call(
        kernel,
        out_shape=[jax.ShapeDtypeStruct(s, jnp.float32) for s in outs],
        in_specs=[pl.BlockSpec(memory_space=space[k]) for k in specs],
        out_specs=[pl.BlockSpec(memory_space=pltpu.VMEM)] * len(outs),
        scratch_shapes=[pltpu.VMEM(s, jnp.float32) for s in scratch],
        compiler_params=pltpu.CompilerParams(vmem_limit_bytes=VMEM_BYTES),
        cost_estimate=pl.CostEstimate(
            flops=work * 2000000, bytes_accessed=work * 1000000, transcendentals=0
        ),
        name=name,
    )


def on_device(populations, block_level, new_slot):
    shape = (lax.axis_size("bx"), lax.axis_size("by"))
    blocks = new_slot.shape[0]
    _, nx, ny, nz = populations.shape
    yface, xface, yedge, block = (9, nx, nz), (27, ny, nz), (3, nx, nz), (8, nx, nz)
    edge, table = (27, 4, ny, nz), (5, 3, 3, ny, nz)

    def run(kernel, *args, outs, specs, scratch=(), work=1):
        def body(*refs):
            kernel(*refs)

        return call(body, outs, specs, scratch, kernel.func.__name__[:-7], work)(*args)

    def leveled(kernel):
        return functools.partial(kernel, shape, blocks)

    pay_a, pay_b = run(
        leveled(face_kernel), block_level, populations,
        outs=[yface, yface], specs="sv", scratch=[yface, yface],
    )
    ya, yb = swap(pay_a, "by", 0), swap(pay_b, "by", 1)
    tables, edges = run(
        leveled(edge_kernel), block_level, populations,
        outs=[table, edge], specs="sv", work=2,
    )
    pay_a, pay_b = run(
        leveled(side_kernel), block_level, populations, edges, ya, yb,
        outs=[xface, xface], specs="svvvv", scratch=[yface, yface, xface, xface],
    )
    xa, xb = swap(pay_a, "bx", 0), swap(pay_b, "bx", 1)
    sums, inner, up, down = run(
        leveled(inner_kernel), block_level, populations, edges, tables, ya, yb, pay_a,
        outs=[(3, 3, 2, nx, ny, nz), (8, nx * ROWS, nz), yedge, yedge],
        specs="svvvvva",
        scratch=[yface, yface, populations.shape, (27, ny, nz)],
        work=10,
    )
    part, pay_a, pay_b = run(
        leveled(outer_kernel),
        block_level, populations, edges, tables, ya, yb, xa, xb, sums, up, down,
        outs=[(8, 4 * ROWS, nz), yedge, yedge],
        specs="svvvvvvvvvv",
        scratch=[yface, yface, xface, xface, (27, ny, nz), (3, 3, 2, 4, ny, nz), yedge, yedge],
    )
    ya, yb = swap(pay_a, "by", 0), swap(pay_b, "by", 1)
    (outer,) = run(
        functools.partial(turn_kernel), part, outs=[(8, 4 * ROWS, nz)], specs="v"
    )
    cells = nx * ny * nz // blocks
    whole = [(blocks, cells), (3, blocks, cells)]
    rho, vel, pay_a, pay_b = run(
        functools.partial(moments_kernel, blocks), new_slot, inner, outer, ya, yb,
        outs=whole + [block, block],
        specs="svvvv",
        scratch=[yedge, yedge, (8, nx * ROWS, nz), block, block],
    )
    ma, mb = swap(pay_a, "by", 0, True), swap(pay_b, "by", 1, True)
    return tuple(
        run(
            functools.partial(place_kernel, blocks), new_slot, rho, vel, ma, mb,
            outs=whole, specs="svvvv", scratch=[block, block],
        )
    )


def solution(mesh):
    in_specs = (P(None, "bx", "by", None), P(), P(("bx", "by")))
    out_specs = (P(("bx", "by"), None), P(None, ("bx", "by"), None))
    return jax.shard_map(
        on_device, mesh=mesh, in_specs=in_specs, out_specs=out_specs, check_vma=False
    )
```

time: 54.4 us -> 44.2 us (0.81)
  waiting for transfers between devices: 18.2 us -> 4.93 us
  starting transfers between devices: 19 us -> 21 us
  Pallas kernels: 13.6 us -> 14.3 us
    ppermute x8, waiting for transfers between devices: 18.2 us -> 4.93 us  [swap(): return lax.ppermute(value, ('bx', 'by'), pairs)]
    ppermute x8, starting transfers between devices: 19 us -> 21 us  [swap(): return lax.ppermute(value, ('bx', 'by'), pairs)]
    pallas_call x5 -> x8, Pallas kernels: 13.6 us -> 14.3 us  [run(): call(body, outs, specs, scratch, kernel.func.__name__[:-7], work)(*args)]
  transfers between devices with their start and end apart: 8 -> 8, of which waited for: 4 -> 4; matrix products, arithmetic and copies ran while one was open for 0% -> 0% of each run, Pallas kernels for 0% -> 21%
where the time goes in v3:
time: 44.2 us; the launch traced here: 43.6 us
  starting transfers between devices  21 us (48%)
  Pallas kernels  14.3 us (32%)
  waiting for transfers between devices  4.93 us (11%)
  local copies, waits for them, and re-layouts  2.68 us (6%)
  between operations  0.74 us (2%)
    ppermute x8, starting transfers between devices, swap(): return lax.ppermute(value, ('bx', 'by'), pairs)  21 us
    pallas_call x8, Pallas kernels, run(): call(body, outs, specs, scratch, kernel.func.__name__[:-7], work)(*args)  14.3 us
    ppermute x8, waiting for transfers between devices, swap(): return lax.ppermute(value, ('bx', 'by'), pairs)  4.93 us
    unnamed x6, local copies, waits for them, and re-layouts  2.68 us
  transfers between devices with their start and end apart: 8, of which 4 were waited for; matrix products, arithmetic and copies ran while one was open for 0% of the time, Pallas kernels for 21%

profile of v3, /device:TPU:16, one launch (start us, length us, event | category | flops | bytes accessed | tf_op | source)
XLA Modules:
  0.0 43.6 jit_solution(18148821997674313444)
XLA Ops:
  0.6 2.0 %copy-done = f32[27,16,16,128]{3,2,1,0:T(8,128)S(1)} copy-done((f32[27,16,16,128]{3,2,1,0:T(8,128)S(1)}, f32[27,16,16,128]{3,2,1,0:T(8,128)}, u32[]{:S(2)}) %copy-start) | copy-done | bytes 3538968
  2.6 0.7 %copy-done.1 = s32[1024]{0:T(1024)S(1)} copy-done((s32[1024]{0:T(1024)S(1)}, s32[1024]{0:T(1024)}, u32[]{:S(2)}) %copy-start.1) | copy-done | bytes 4120
  3.3 0.9 %face.1 = (f32[9,16,128]{2,1,0:T(8,128)S(1)}, f32[9,16,128]{2,1,0:T(8,128)S(1)}) custom-call(s32[1024]{0:T(1024)S(1)} %copy-done.1, f32[27,16,16,128]{3,2,1,0:T(8,128)S(1)} %copy-done), custom_call_target="tpu_custom_call" | custom-call | flops 2000000 | bytes 1000000 | tf_op jit(solution)/shard_map/face/pallas_call | solution.py:635
  4.2 0.1 collective-permute-start
  4.3 4.2 %collective-permute-start.1 = (f32[9,16,128]{2,1,0:T(8,128)S(1)}, f32[9,16,128]{2,1,0:T(8,128)S(1)}, u32[]{:S(2)}, u32[]{:S(2)}) collective-permute-start(f32[9,16,128]{2,1,0:T(8,128)S(1)} %get-tuple-element.22), channel_id=1, source_target_pairs={{1,2},{3,4},{5,6},{7,8},{9,10},{11,12},{13,14},{15,0},{17,18},{19,... | collective-permute-start | bytes 221192 | tf_op jit(solution)/shard_map/ppermute | solution.py:605
  8.6 1.1 %edge.1 = (f32[5,3,3,16,128]{4,3,2,1,0:T(8,128)S(1)}, f32[27,4,16,128]{3,2,1,0:T(8,128)S(1)}) custom-call(s32[1024]{0:T(1024)S(1)} %copy-done.1, f32[27,16,16,128]{3,2,1,0:T(8,128)S(1)} %copy-done), custom_call_target="tpu_custom_call" | custom-call | flops 4000000 | bytes 2000000 | tf_op jit(solution)/shard_map/edge/pallas_call | solution.py:635
  9.7 0.9 %collective-permute-done.1.refs_4_.refs_5_ = f32[9,16,128]{2,1,0:T(8,128)S(1)} collective-permute-done((f32[9,16,128]{2,1,0:T(8,128)S(1)}, f32[9,16,128]{2,1,0:T(8,128)S(1)}, u32[]{:S(2)}, u32[]{:S(2)}) %collective-permute-start.1) | collective-permute-done | bytes 73760 | tf_op jit(solution)/shard_map/ppermute | solution.py:605
  10.6 0.8 %side.1 = (f32[27,16,128]{2,1,0:T(8,128)S(1)}, f32[27,16,128]{2,1,0:T(8,128)S(1)}) custom-call(s32[1024]{0:T(1024)S(1)} %copy-done.1, f32[27,16,16,128]{3,2,1,0:T(8,128)S(1)} %copy-done, f32[27,4,16,128]{3,2,1,0:T(8,128)S(1)} %get-tuple-element.19.refs_2_, f32[9,16,128]{2,1,0:T(8,128)S(1)} %collective-permute-done.refs_3_.refs_4_, ...), custom_call_target="tpu_custom_call" | custom-call | flops 2000000 | bytes 1000000 | tf_op jit(solution)/shard_map/side/pallas_call | solution.py:635
  11.4 3.6 %collective-permute-start.3 = (f32[27,16,128]{2,1,0:T(8,128)S(1)}, f32[27,16,128]{2,1,0:T(8,128)S(1)}, u32[]{:S(2)}, u32[]{:S(2)}) collective-permute-start(f32[27,16,128]{2,1,0:T(8,128)S(1)} %get-tuple-element.25), channel_id=1, source_target_pairs={{16,32},{48,64},{80,96},{112,0},{17,33},{49,65},{81,97},{113,1},{1... | collective-permute-start | bytes 663560 | tf_op jit(solution)/shard_map/ppermute | solution.py:605
  15.0 0.8 %collective-permute-start.2 = (f32[27,16,128]{2,1,0:T(8,128)S(1)}, f32[27,16,128]{2,1,0:T(8,128)S(1)}, u32[]{:S(2)}, u32[]{:S(2)}) collective-permute-start(f32[27,16,128]{2,1,0:T(8,128)S(1)} %get-tuple-element.23.refs_6_), channel_id=1, source_target_pairs={{0,16},{32,48},{64,80},{96,112},{1,17},{33,49},{65,81},{97,113},{2... | collective-permute-start | bytes 663560 | tf_op jit(solution)/shard_map/ppermute | solution.py:605
  15.7 7.8 %inner.1 = (f32[3,3,2,16,16,128]{5,4,3,2,1,0:T(8,128)S(1)}, f32[8,128,128]{2,1,0:T(8,128)S(1)}, f32[3,16,128]{2,1,0:T(8,128)S(1)}, f32[3,16,128]{2,1,0:T(8,128)S(1)}) custom-call(s32[1024]{0:T(1024)S(1)} %copy-done.1, f32[27,16,16,128]{3,2,1,0:T(8,128)S(1)} %copy-done, f32[27,4,16,128]{3,2,1,0:T(8,128)S(1)} %get-tuple-element.19.refs_2_, ...), custom_call_target="tpu_custom_call" | custom-call | flops 20000000 | bytes 10000000 | tf_op jit(solution)/shard_map/inner/pallas_call | solution.py:635
  23.6 0.0 collective-permute-done.3.refs_7_
  23.6 0.6 %collective-permute-done.2.refs_6_ = f32[27,16,128]{2,1,0:T(8,128)S(1)} collective-permute-done((f32[27,16,128]{2,1,0:T(8,128)S(1)}, f32[27,16,128]{2,1,0:T(8,128)S(1)}, u32[]{:S(2)}, u32[]{:S(2)}) %collective-permute-start.2) | collective-permute-done | bytes 221216 | tf_op jit(solution)/shard_map/ppermute | solution.py:605
  24.2 1.2 %outer.1 = (f32[8,32,128]{2,1,0:T(8,128)S(1)}, f32[3,16,128]{2,1,0:T(8,128)S(1)}, f32[3,16,128]{2,1,0:T(8,128)S(1)}) custom-call(s32[1024]{0:T(1024)S(1)} %copy-done.1, f32[27,16,16,128]{3,2,1,0:T(8,128)S(1)} %copy-done, f32[27,4,16,128]{3,2,1,0:T(8,128)S(1)} %get-tuple-element.19.refs_2_, f32[5,3,3,16,128]{4,3,2,1,0:T(8,128)S(1)} %get-tuple-element.20.refs_3_, ...), custom_call_target="tpu_custom_call" | custom-call | flops 2000000 | bytes 1000000 | tf_op jit(solution)/shard_map/outer/pallas_call | solution.py:635
  25.4 0.1 collective-permute-start.4
  25.5 4.4 %collective-permute-start.5 = (f32[3,16,128]{2,1,0:T(8,128)S(1)}, f32[3,16,128]{2,1,0:T(8,128)S(1)}, u32[]{:S(2)}, u32[]{:S(2)}) collective-permute-start(f32[3,16,128]{2,1,0:T(8,128)S(1)} %get-tuple-element.31), channel_id=1, source_target_pairs={{1,2},{3,4},{5,6},{7,8},{9,10},{11,12},{13,14},{15,0},{17,18},{19,... | collective-permute-start | bytes 73736 | tf_op jit(solution)/shard_map/ppermute | solution.py:605
  29.9 0.2 turn.1.refs_2_
  30.1 0.0 collective-permute-done.4.refs_3_
  30.1 1.3 %collective-permute-done.5.refs_4_ = f32[3,16,128]{2,1,0:T(8,128)S(1)} collective-permute-done((f32[3,16,128]{2,1,0:T(8,128)S(1)}, f32[3,16,128]{2,1,0:T(8,128)S(1)}, u32[]{:S(2)}, u32[]{:S(2)}) %collective-permute-start.5) | collective-permute-done | bytes 24608 | tf_op jit(solution)/shard_map/ppermute | solution.py:605
  31.5 0.8 %moments.1 = (f32[8,4096]{1,0:T(8,128)S(1)}, f32[3,8,4096]{2,1,0:T(8,128)S(1)}, f32[8,16,128]{2,1,0:T(8,128)S(1)}, f32[8,16,128]{2,1,0:T(8,128)S(1)}) custom-call(s32[8]{0:T(128)S(1)} %copy-done.2, f32[8,128,128]{2,1,0:T(8,128)S(1)} %get-tuple-element.24.refs_1_, f32[8,32,128]{2,1,0:T(8,128)S(1)} %turn.1.refs_2_, ...), custom_call_target="tpu_custom_call" | custom-call | flops 2000000 | bytes 1000000 | tf_op jit(solution)/shard_map/moments/pallas_call | solution.py:635
  32.3 0.1 collective-permute-start.6
  32.4 7.8 %collective-permute-start.7 = (f32[8,16,128]{2,1,0:T(8,128)S(1)}, f32[8,16,128]{2,1,0:T(8,128)S(1)}, u32[]{:S(2)}, u32[]{:S(2)}) collective-permute-start(f32[8,16,128]{2,1,0:T(8,128)S(1)} %get-tuple-element.35), channel_id=1, source_target_pairs={{1,2},{3,4},{5,6},{7,8},{9,10},{11,12},{13,14},{15,16},{17,18},{19... | collective-permute-start | bytes 196616 | tf_op jit(solution)/shard_map/ppermute | solution.py:605
  40.1 2.0 %collective-permute-done.7.refs_4_ = f32[8,16,128]{2,1,0:T(8,128)S(1)} collective-permute-done((f32[8,16,128]{2,1,0:T(8,128)S(1)}, f32[8,16,128]{2,1,0:T(8,128)S(1)}, u32[]{:S(2)}, u32[]{:S(2)}) %collective-permute-start.7) | collective-permute-done | bytes 65568 | tf_op jit(solution)/shard_map/ppermute | solution.py:605
  42.2 1.5 %place.1 = (f32[8,4096]{1,0:T(8,128)}, f32[3,8,4096]{2,1,0:T(8,128)}) custom-call(s32[8]{0:T(128)S(1)} %copy-done.2, f32[8,4096]{1,0:T(8,128)S(1)} %get-tuple-element.32.refs_1_, f32[3,8,4096]{2,1,0:T(8,128)S(1)} %get-tuple-element.33.refs_2_, f32[8,16,128]{2,1,0:T(8,128)S(1)} %collective-permute-done.6.refs_3_, f32[8,16,128]{2,1,0:T(8,128)S(1)} %collective-permute-done.7.refs_4_), custom_call_target="tpu_custom_call" | custom-call | flops 2000000 | bytes 1000000 | tf_op jit(solution)/shard_map/place/pallas_call | solution.py:635
  (6 shorter events, 0.0 us)
Async XLA Ops:
  0.6 2.0 %copy-start = (f32[27,16,16,128]{3,2,1,0:T(8,128)S(1)}, f32[27,16,16,128]{3,2,1,0:T(8,128)}, u32[]{:S(2)}) copy-start(f32[27,16,16,128]{3,2,1,0:T(8,128)} %refs_1_.9) | copy-start | bytes 10616836
  2.6 0.7 %copy-start.1 = (s32[1024]{0:T(1024)S(1)}, s32[1024]{0:T(1024)}, u32[]{:S(2)}) copy-start(s32[1024]{0:T(1024)} %refs_0_.11) | copy-start | bytes 12292
  4.2 5.4 %collective-permute-start = (f32[9,16,128]{2,1,0:T(8,128)S(1)}, f32[9,16,128]{2,1,0:T(8,128)S(1)}, u32[]{:S(2)}, u32[]{:S(2)}) collective-permute-start(f32[9,16,128]{2,1,0:T(8,128)S(1)} %get-tuple-element.21), channel_id=1, source_target_pairs={{0,1},{2,3},{4,5},{6,7},{8,9},{10,11},{12,13},{14,15},{16,17},{18,... | collective-permute-start | bytes 221192 | tf_op jit(solution)/shard_map/ppermute | solution.py:605
  4.3 6.2 %collective-permute-start.1 = (f32[9,16,128]{2,1,0:T(8,128)S(1)}, f32[9,16,128]{2,1,0:T(8,128)S(1)}, u32[]{:S(2)}, u32[]{:S(2)}) collective-permute-start(f32[9,16,128]{2,1,0:T(8,128)S(1)} %get-tuple-element.22), channel_id=1, source_target_pairs={{1,2},{3,4},{5,6},{7,8},{9,10},{11,12},{13,14},{15,0},{17,18},{19,... | collective-permute-start | bytes 221192 | tf_op jit(solution)/shard_map/ppermute | solution.py:605
  11.4 12.2 %collective-permute-start.3 = (f32[27,16,128]{2,1,0:T(8,128)S(1)}, f32[27,16,128]{2,1,0:T(8,128)S(1)}, u32[]{:S(2)}, u32[]{:S(2)}) collective-permute-start(f32[27,16,128]{2,1,0:T(8,128)S(1)} %get-tuple-element.25), channel_id=1, source_target_pairs={{16,32},{48,64},{80,96},{112,0},{17,33},{49,65},{81,97},{113,1},{1... | collective-permute-start | bytes 663560 | tf_op jit(solution)/shard_map/ppermute | solution.py:605
  15.0 9.2 %collective-permute-start.2 = (f32[27,16,128]{2,1,0:T(8,128)S(1)}, f32[27,16,128]{2,1,0:T(8,128)S(1)}, u32[]{:S(2)}, u32[]{:S(2)}) collective-permute-start(f32[27,16,128]{2,1,0:T(8,128)S(1)} %get-tuple-element.23.refs_6_), channel_id=1, source_target_pairs={{0,16},{32,48},{64,80},{96,112},{1,17},{33,49},{65,81},{97,113},{2... | collective-permute-start | bytes 663560 | tf_op jit(solution)/shard_map/ppermute | solution.py:605
  24.2 7.3 %copy-start.2 = (s32[8]{0:T(128)S(1)}, s32[8]{0:T(128)}, u32[]{:S(2)}) copy-start(s32[8]{0:T(128)} %refs_0_.13) | copy-start | bytes 100
  25.4 4.7 %collective-permute-start.4 = (f32[3,16,128]{2,1,0:T(8,128)S(1)}, f32[3,16,128]{2,1,0:T(8,128)S(1)}, u32[]{:S(2)}, u32[]{:S(2)}) collective-permute-start(f32[3,16,128]{2,1,0:T(8,128)S(1)} %get-tuple-element.30), channel_id=1, source_target_pairs={{0,1},{2,3},{4,5},{6,7},{8,9},{10,11},{12,13},{14,15},{16,17},{18,... | collective-permute-start | bytes 73736 | tf_op jit(solution)/shard_map/ppermute | solution.py:605
  25.5 6.0 %collective-permute-start.5 = (f32[3,16,128]{2,1,0:T(8,128)S(1)}, f32[3,16,128]{2,1,0:T(8,128)S(1)}, u32[]{:S(2)}, u32[]{:S(2)}) collective-permute-start(f32[3,16,128]{2,1,0:T(8,128)S(1)} %get-tuple-element.31), channel_id=1, source_target_pairs={{1,2},{3,4},{5,6},{7,8},{9,10},{11,12},{13,14},{15,0},{17,18},{19,... | collective-permute-start | bytes 73736 | tf_op jit(solution)/shard_map/ppermute | solution.py:605
  32.3 7.9 %collective-permute-start.6 = (f32[8,16,128]{2,1,0:T(8,128)S(1)}, f32[8,16,128]{2,1,0:T(8,128)S(1)}, u32[]{:S(2)}, u32[]{:S(2)}) collective-permute-start(f32[8,16,128]{2,1,0:T(8,128)S(1)} %get-tuple-element.34), channel_id=1, source_target_pairs={{0,1},{2,3},{4,5},{6,7},{8,9},{10,11},{12,13},{14,15},{16,17},{18,... | collective-permute-start | bytes 196616 | tf_op jit(solution)/shard_map/ppermute | solution.py:605
  32.4 9.8 %collective-permute-start.7 = (f32[8,16,128]{2,1,0:T(8,128)S(1)}, f32[8,16,128]{2,1,0:T(8,128)S(1)}, u32[]{:S(2)}, u32[]{:S(2)}) collective-permute-start(f32[8,16,128]{2,1,0:T(8,128)S(1)} %get-tuple-element.35), channel_id=1, source_target_pairs={{1,2},{3,4},{5,6},{7,8},{9,10},{11,12},{13,14},{15,16},{17,18},{19... | collective-permute-start | bytes 196616 | tf_op jit(solution)/shard_map/ppermute | solution.py:605

commit v4 on v3

--- a/solution.py
+++ b/solution.py
@@ -18,6 +18,7 @@
 ROWS = 8
 LANES = 128
 VMEM_BYTES = 16 * 1024 * 1024
+FACE_BYTES = 53 * 1024 * 1024
 
 
 def comp(a, b, e):
@@ -137,23 +138,19 @@
     return jnp.where(lane_roll(there_rows, -e) != here, scale, 1.0)
 
 
-def fill_factors(levels, shape, blocks, table):
-    lev = {
-        (dx, dy): column_level(levels, shape, blocks, dx, dy)
-        for dx in (-1, 0, 1)
-        for dy in (-1, 0, 1)
-    }
+def fill_factors(marks, table):
     row = sublane()
     for k, (own, dx) in enumerate(((0, -1), (0, 0), (0, 1), (-1, 0), (1, 0))):
-        here = lev[own, 0]
+        here = marks[own + 1, 1, :, :]
+        near = [marks[dx + 1, b, :, :] for b in range(3)]
         for e in (-1, 0, 1):
-            plain = level_factor(here, lev[dx, 0], e)
+            plain = level_factor(here, near[1], e)
             for b in (-1, 0, 1):
                 low, high = plain, plain
                 if b == -1:
-                    low = jnp.where(row == 0, level_factor(here, lev[dx, -1], e), plain)
+                    low = jnp.where(row == 0, level_factor(here, near[0], e), plain)
                 if b == 1:
-                    high = jnp.where(row == ROWS - 1, level_factor(here, lev[dx, 1], e), plain)
+                    high = jnp.where(row == ROWS - 1, level_factor(here, near[2], e), plain)
                 table[k, b + 1, e + 1, 0:8, :] = low
                 table[k, b + 1, e + 1, 8:16, :] = high
 
@@ -176,18 +173,31 @@
         second[...] = up[...]
 
 
-def face_kernel(shape, blocks, levels, f, pay_a, pay_b, up, down):
+def face_kernel(
+    shape, blocks, levels, f, marks, pay_a, pay_b, level, high, low, sems, up, down
+):
     _, nx, ny, nz = f.shape
-    flat = f.reshape(27 * nx * ny, nz)
-    here = column_level(levels, shape, blocks, 0, 0)
+    copies = [
+        pltpu.make_async_copy(levels, level, sems.at[0]),
+        pltpu.make_async_copy(f.at[:, :, ny - 1, :], high, sems.at[1]),
+        pltpu.make_async_copy(f.at[:, :, 0, :], low, sems.at[2]),
+    ]
+    for copy in copies:
+        copy.start()
+    copies[0].wait()
+    for dx in (-1, 0, 1):
+        for dy in (-1, 0, 1):
+            marks[dx + 1, dy + 1, :, :] = column_level(level, shape, blocks, dx, dy)
+    here = marks[1, 1, :, :]
     row = sublane()
-    for b, y, pay in ((1, ny - 1, up), (-1, 0, down)):
-        near = [column_level(levels, shape, blocks, dx, b) for dx in (-1, 0, 1)]
+    for b, rows, pay, copy in ((1, high, up, copies[1]), (-1, low, down, copies[2])):
+        near = [marks[dx, b + 1, :, :] for dx in range(3)]
         plain = {e: level_factor(here, near[1], e) for e in (-1, 0, 1)}
+        copy.wait()
         for x in range(0, nx, ROWS):
 
             def get(c):
-                return flat[pl.ds((comp(*c) * nx + x) * ny + y, ROWS, stride=ny), :]
+                return rows[comp(*c), x : x + ROWS, :]
 
             def factor(c):
                 if c[0] == -1 and x == 0:
@@ -220,37 +230,55 @@
         collide(sums_of(get), get, fine, False, factor, lambda c, value: put(c, rows, value))
 
 
-def edge_kernel(shape, blocks, levels, f, table, out):
-    fill_factors(levels, shape, blocks, table)
-    fine = column_level(levels, shape, blocks, 0, 0) == 1
+def first_kernel(marks, f, table, out, calm):
+    fill_factors(marks, table)
+    fine = marks[1, 1, :, :] == 1
     nx = f.shape[1]
-    for k, x in enumerate((0, 1, nx - 2, nx - 1)):
-
+    for n, (x, a) in enumerate(((0, -1), (nx - 1, 1))):
+        for h in (0, 1):
+            rows = slice(8 * h, 8 * h + 8)
+
+            def get(c):
+                return f[comp(*c), x, rows, :]
+
+            def put(c, value):
+                calm[n, face(c[1], c[2]), rows, :] = value
+
+            collide(
+                sums_of(get), get, fine, True,
+                lambda c: table[1 + c[0], c[1] + 1, c[2] + 1, rows, :],
+                put, [c for c in DIRS if c[0] == a],
+            )
+
+    def layer(x, carry):
         def near(a):
-            return 1 + a if (x, a) in ((0, -1), (nx - 1, 1)) else 1
+            return 1 if a == 0 else jnp.where(x == (0 if a < 0 else nx - 1), 1 + a, 1)
 
         def put(c, rows, value):
-            out[comp(*c), k, rows, :] = value
+            out[comp(*c), x, rows, :] = value
 
         first_collide(f, table, fine, x, near, put)
-
-
-def shifted_read(g, above, below, row, c, k, x, h):
+        return carry
+
+    lax.fori_loop(0, nx, layer, 0)
+
+
+def shifted_read(g, above, below, row, c, x, h):
     a, b, e = c
     i = comp(a, b, e)
     if b == 0:
-        tile = g[i, k, 8 * h : 8 * h + 8, :]
+        tile = g[i, x, 8 * h : 8 * h + 8, :]
     elif b == 1:
         if h == 1:
-            tile = g[i, k, 7:15, :]
+            tile = g[i, x, 7:15, :]
         else:
-            tile = pltpu.roll(g[i, k, 0:8, :], 1, 0)
+            tile = pltpu.roll(g[i, x, 0:8, :], 1, 0)
             tile = jnp.where(row == 0, below[face(a, e), pl.ds(x, 1), :], tile)
     else:
         if h == 0:
-            tile = g[i, k, 1:9, :]
+            tile = g[i, x, 1:9, :]
         else:
-            tile = pltpu.roll(g[i, k, 8:16, :], 7, 0)
+            tile = pltpu.roll(g[i, x, 8:16, :], 7, 0)
             tile = jnp.where(row == 7, above[face(a, e), pl.ds(x, 1), :], tile)
     return lane_roll(tile, e)
 
@@ -267,45 +295,34 @@
         below[...] = first[...]
 
 
-def side_kernel(
-    shape, blocks, levels, f, g, got_a, got_b, pay_a, pay_b, above, below, up, down
-):
+def side_kernel(marks, f, g, calm, got_a, got_b, pay_a, pay_b, above, below, up, down):
     load_by_parity(lax.rem(lax.axis_index("by"), 2), got_a, got_b, above, below)
-    fine = column_level(levels, shape, blocks, 0, 0) == 1
+    fine = marks[1, 1, :, :] == 1
     row = sublane()
     nx = f.shape[1]
-    for ad, x, inner, k, near, pay in ((1, nx - 1, nx - 2, 3, 2, up), (-1, 0, 1, 0, 1, down)):
+    for n, (ad, x, pay) in enumerate(((-1, 0, down), (1, nx - 1, up))):
         for h in (0, 1):
             rows = slice(8 * h, 8 * h + 8)
 
-            def old(c):
-                return f[comp(*c), x, rows, :]
-
             def flat(b, e):
-                moved = shifted_read(g, above, below, row, (0, b, e), k, x, h)
-                return jnp.where(fine, moved, old((0, b, e)))
+                return shifted_read(g, above, below, row, (0, b, e), x, h)
 
             for b in (-1, 0, 1):
                 for e in (-1, 0, 1):
-                    c = (ad, b, e)
-                    pay[face(b, e), rows, :] = shifted_read(g, above, below, row, c, k, x, h)
-                    moved = shifted_read(g, above, below, row, c, near, inner, h)
-                    pay[9 + face(b, e), rows, :] = jnp.where(fine, moved, old(c))
-            middle = group_sums(flat)
-            back = group_sums(lambda b, e: old((-ad, b, e)))
-            back = [jnp.where(fine, 0.0, s) for s in back]
-            parts = [middle[0], middle[1], middle[2] + back[2], middle[3]]
-            parts += [middle[4] + back[4], middle[5] + back[5], back[0], back[1], back[3]]
-            for n, part in enumerate(parts):
-                pay[18 + n, rows, :] = part
+                    c, j = (ad, b, e), face(b, e)
+                    pay[j, rows, :] = shifted_read(g, above, below, row, c, x, h)
+                    moved = shifted_read(g, above, below, row, c, x - ad, h)
+                    pay[9 + j, rows, :] = jnp.where(fine, moved, calm[n, j, rows, :])
+            for m, part in enumerate(group_sums(flat)):
+                pay[18 + m, rows, :] = part
     store_by_parity(lax.rem(lax.axis_index("bx"), 2), pay_a, pay_b, up, down)
 
 
-def second_collide(groups, get, fine, factor, put, dirs):
+def second_collide(groups, get, fine, factor, put, dirs, known=None):
     made = {}
 
     def keep(c, value):
-        made[c] = value
+        made[c] = value if known is None else jnp.where(fine, value, known(c))
 
     collide(groups, get, fine, True, factor, keep, dirs)
     for a in (-1, 0, 1):
@@ -351,33 +368,32 @@
     return jnp.take_along_axis(tile, turn, axis=1)
 
 
+def leaving(slots, blocks, step):
+    here = lax.axis_index("bx") * lax.axis_size("by") + lax.axis_index("by")
+    which = jnp.int32(-1)
+    for k in range(blocks):
+        which = jnp.where(slots[k] // blocks == here + step, k, which)
+    return which
+
+
 def inner_kernel(
-    shape, blocks, levels, f, edges, table, ya, yb, tie, sums, made, up, down,
-    above, below, g, state,
+    blocks, slots, marks, f, g, table, ya, yb, tie, sums, made, up, down, moves,
+    above, below, state,
 ):
     load_by_parity(lax.rem(lax.axis_index("by"), 2), ya, yb, above, below)
-    fine = column_level(levels, shape, blocks, 0, 0) == 1
+    for n, step in enumerate((1, -1)):
+        moves[n, :, :] = jnp.full((ROWS, LANES), leaving(slots, blocks, step), jnp.int32)
+    fine = marks[1, 1, :, :] == 1
     row = sublane()
     reflect, turn = turns()
     nx = f.shape[1]
-    for k, x in enumerate((0, 1, nx - 2, nx - 1)):
-        g[:, x, :, :] = edges[:, k, :, :]
-
-    def first(x, carry):
-        def put(c, rows, value):
-            g[comp(*c), x, rows, :] = value
-
-        first_collide(f, table, fine, x, lambda a: 1, put)
-        return carry
-
-    lax.fori_loop(2, nx - 2, first, 0)
 
     def second(x, carry):
         for h in (0, 1):
             rows = slice(8 * h, 8 * h + 8)
 
             def moved(c):
-                tile = shifted_read(g, above, below, row, c, x - c[0], x - c[0], h)
+                tile = shifted_read(g, above, below, row, c, x - c[0], h)
                 tile = jnp.where(fine, tile, f[comp(*c), x, rows, :])
                 state[comp(*c), rows, :] = tile
                 return tile
@@ -418,17 +434,16 @@
 
 
 def outer_kernel(
-    shape, blocks, levels, f, g, table, ya, yb, xa, xb, sums, in_up, in_down,
+    marks, f, g, table, ya, yb, xa, xb, sums, in_up, in_down,
     part, pay_a, pay_b, above, below, right, left, state, ends, up, down,
 ):
     load_by_parity(lax.rem(lax.axis_index("by"), 2), ya, yb, above, below)
     load_by_parity(lax.rem(lax.axis_index("bx"), 2), xa, xb, right, left)
-    fine = {dx: column_level(levels, shape, blocks, dx, 0) == 1 for dx in (-1, 0, 1)}
+    fine = {dx: marks[dx + 1, 1, :, :] == 1 for dx in (-1, 0, 1)}
     row = sublane()
     reflect, turn = turns()
     nx = f.shape[1]
     hold = {-1: 0, 0: 1, nx - 1: 2, nx: 3}
-    at = {0: 0, 1: 1, nx - 2: 2, nx - 1: 3}
     for side, x, k, pay in ((-1, 0, 3, left), (1, nx - 1, 4, right)):
         for h in (0, 1):
             rows = slice(8 * h, 8 * h + 8)
@@ -441,7 +456,7 @@
                 return put
 
             def read(c, x):
-                return shifted_read(g, above, below, row, c, at[x], x, h)
+                return shifted_read(g, above, below, row, c, x, h)
 
             def moved(c):
                 a, b, e = c
@@ -461,18 +476,14 @@
                 keep(hold[x]),
                 [c for c in DIRS if c[0] != side],
             )
-            got = [pay[18 + n, rows, :] for n in range(9)]
-            own = group_sums(lambda b, e: read((side, b, e), x))
-            own = [jnp.where(fine[side], s, 0.0) for s in own]
-            outer = (own[0] + got[6], own[1] + got[7], own[2], own[3] + got[8], own[4], own[5])
 
             def toward(c):
                 return pay[9 + face(c[1], c[2]), rows, :]
 
             second_collide(
                 {
-                    side: outer,
-                    0: tuple(got[:6]),
+                    side: group_sums(lambda b, e: read((side, b, e), x)),
+                    0: tuple(pay[18 + n, rows, :] for n in range(6)),
                     -side: group_sums(lambda b, e: toward((-side, b, e))),
                 },
                 toward,
@@ -480,6 +491,7 @@
                 lambda c: table[k, c[1] + 1, c[2] + 1, rows, :],
                 keep(hold[x + side]),
                 [c for c in DIRS if c[0] == -side],
+                toward,
             )
     up[...] = in_up[...]
     down[...] = in_down[...]
@@ -517,16 +529,8 @@
             out[n, rows, :] = block_rows(part[n, rows, :], reflect, turn)
 
 
-def leaving(slots, blocks, step):
-    here = lax.axis_index("bx") * lax.axis_size("by") + lax.axis_index("by")
-    which = jnp.int32(-1)
-    for k in range(blocks):
-        which = jnp.where(slots[k] // blocks == here + step, k, which)
-    return which
-
-
 def moments_kernel(
-    blocks, slots, inner, outer, got_a, got_b, rho_out, vel_out, pay_a, pay_b,
+    moves, inner, outer, got_a, got_b, rho_out, vel_out, pay_a, pay_b,
     above, below, made, up, down,
 ):
     odd = lax.rem(lax.axis_index("by"), 2)
@@ -561,19 +565,19 @@
                     rho_out[:, lanes] = tile
                 else:
                     vel_out[n - 1, :, lanes] = tile
-    for step, pay in ((1, up), (-1, down)):
-        which = jnp.maximum(leaving(slots, blocks, step), 0)
+    for k, pay in enumerate((up, down)):
+        which = jnp.maximum(jnp.max(moves[k, :, :]), 0)
         for n in range(8):
             pay[n, :, :] = made[n, pl.ds(which, nx, stride=ROWS), :]
     store_by_parity(odd, pay_a, pay_b, up, down)
 
 
-def place_kernel(blocks, slots, rho, vel, got_a, got_b, rho_out, vel_out, after, before):
+def place_kernel(moves, rho, vel, got_a, got_b, rho_out, vel_out, after, before):
     odd = lax.rem(lax.axis_index("by"), 2)
     load_by_parity(odd, got_a, got_b, after, before)
     row = sublane()
-    to_next = row == leaving(slots, blocks, 1)
-    to_prev = row == leaving(slots, blocks, -1)
+    to_next = row == moves[0, :, :]
+    to_prev = row == moves[1, :, :]
     for x in range(after.shape[1]):
         for h in (0, 1):
             lanes = slice((2 * x + h) * LANES, (2 * x + h + 1) * LANES)
@@ -605,15 +609,15 @@
     return lax.ppermute(value, ("bx", "by"), pairs)
 
 
-def call(kernel, outs, specs, scratch, name, work):
-    space = {"v": pltpu.VMEM, "s": pltpu.SMEM, "a": pl.ANY}
+def call(kernel, outs, specs, scratch, name, work, limit):
+    space = {"v": pltpu.VMEM, "s": pltpu.SMEM, "h": pltpu.HBM, "a": pl.ANY}
     return pl.pallas_call(
         kernel,
-        out_shape=[jax.ShapeDtypeStruct(s, jnp.float32) for s in outs],
+        out_shape=outs,
         in_specs=[pl.BlockSpec(memory_space=space[k]) for k in specs],
         out_specs=[pl.BlockSpec(memory_space=pltpu.VMEM)] * len(outs),
-        scratch_shapes=[pltpu.VMEM(s, jnp.float32) for s in scratch],
-        compiler_params=pltpu.CompilerParams(vmem_limit_bytes=VMEM_BYTES),
+        scratch_shapes=scratch,
+        compiler_params=pltpu.CompilerParams(vmem_limit_bytes=limit),
         cost_estimate=pl.CostEstimate(
             flops=work * 2000000, bytes_accessed=work * 1000000, transcendentals=0
         ),
@@ -625,63 +629,82 @@
     shape = (lax.axis_size("bx"), lax.axis_size("by"))
     blocks = new_slot.shape[0]
     _, nx, ny, nz = populations.shape
-    yface, xface, yedge, block = (9, nx, nz), (27, ny, nz), (3, nx, nz), (8, nx, nz)
-    edge, table = (27, 4, ny, nz), (5, 3, 3, ny, nz)
-
-    def run(kernel, *args, outs, specs, scratch=(), work=1):
+    yface, xface, yedge, block = (9, nx, nz), (24, ny, nz), (3, nx, nz), (8, nx, nz)
+    tile = (ROWS, nz)
+
+    def real(*dims):
+        return jax.ShapeDtypeStruct(dims, jnp.float32)
+
+    def whole(*dims):
+        return jax.ShapeDtypeStruct(dims, jnp.int32)
+
+    def room(*shapes):
+        return [pltpu.VMEM(dims, jnp.float32) for dims in shapes]
+
+    def run(kernel, *args, outs, specs, scratch=(), work=1, limit=VMEM_BYTES):
         def body(*refs):
             kernel(*refs)
 
-        return call(body, outs, specs, scratch, kernel.func.__name__[:-7], work)(*args)
-
-    def leveled(kernel):
-        return functools.partial(kernel, shape, blocks)
-
+        return call(body, outs, specs, scratch, kernel.func.__name__[:-7], work, limit)(*args)
+
+    marks, pay_a, pay_b = run(
+        functools.partial(face_kernel, shape, blocks), block_level, populations,
+        outs=[whole(3, 3, *tile), real(*yface), real(*yface)],
+        specs="hh",
+        scratch=[pltpu.SMEM(block_level.shape, jnp.int32)]
+        + room((27, nx, nz), (27, nx, nz))
+        + [pltpu.SemaphoreType.DMA((3,))]
+        + room(yface, yface),
+        limit=FACE_BYTES,
+    )
+    ya, yb = swap(pay_a, "by", 0), swap(pay_b, "by", 1)
+    table, g, calm = run(
+        functools.partial(first_kernel), marks, populations,
+        outs=[real(5, 3, 3, ny, nz), real(*populations.shape), real(2, 9, ny, nz)],
+        specs="vv", work=3,
+    )
     pay_a, pay_b = run(
-        leveled(face_kernel), block_level, populations,
-        outs=[yface, yface], specs="sv", scratch=[yface, yface],
-    )
-    ya, yb = swap(pay_a, "by", 0), swap(pay_b, "by", 1)
-    tables, edges = run(
-        leveled(edge_kernel), block_level, populations,
-        outs=[table, edge], specs="sv", work=2,
-    )
-    pay_a, pay_b = run(
-        leveled(side_kernel), block_level, populations, edges, ya, yb,
-        outs=[xface, xface], specs="svvvv", scratch=[yface, yface, xface, xface],
+        functools.partial(side_kernel), marks, populations, g, calm, ya, yb,
+        outs=[real(*xface)] * 2, specs="vvvvvv", scratch=room(yface, yface, xface, xface),
     )
     xa, xb = swap(pay_a, "bx", 0), swap(pay_b, "bx", 1)
-    sums, inner, up, down = run(
-        leveled(inner_kernel), block_level, populations, edges, tables, ya, yb, pay_a,
-        outs=[(3, 3, 2, nx, ny, nz), (8, nx * ROWS, nz), yedge, yedge],
-        specs="svvvvva",
-        scratch=[yface, yface, populations.shape, (27, ny, nz)],
+    sums, inner, up, down, moves = run(
+        functools.partial(inner_kernel, blocks),
+        new_slot, marks, populations, g, table, ya, yb, pay_a,
+        outs=[
+            real(3, 3, 2, nx, ny, nz), real(8, nx * ROWS, nz), real(*yedge), real(*yedge),
+            whole(2, *tile),
+        ],
+        specs="svvvvvva",
+        scratch=room(yface, yface, (27, ny, nz)),
         work=10,
     )
     part, pay_a, pay_b = run(
-        leveled(outer_kernel),
-        block_level, populations, edges, tables, ya, yb, xa, xb, sums, up, down,
-        outs=[(8, 4 * ROWS, nz), yedge, yedge],
-        specs="svvvvvvvvvv",
-        scratch=[yface, yface, xface, xface, (27, ny, nz), (3, 3, 2, 4, ny, nz), yedge, yedge],
+        functools.partial(outer_kernel),
+        marks, populations, g, table, ya, yb, xa, xb, sums, up, down,
+        outs=[real(8, 4 * ROWS, nz), real(*yedge), real(*yedge)],
+        specs="vvvvvvvvvvv",
+        scratch=room(
+            yface, yface, xface, xface, (27, ny, nz), (3, 3, 2, 4, ny, nz), yedge, yedge
+        ),
     )
     ya, yb = swap(pay_a, "by", 0), swap(pay_b, "by", 1)
     (outer,) = run(
-        functools.partial(turn_kernel), part, outs=[(8, 4 * ROWS, nz)], specs="v"
+        functools.partial(turn_kernel), part, outs=[real(8, 4 * ROWS, nz)], specs="v"
     )
     cells = nx * ny * nz // blocks
-    whole = [(blocks, cells), (3, blocks, cells)]
+    results = [real(blocks, cells), real(3, blocks, cells)]
     rho, vel, pay_a, pay_b = run(
-        functools.partial(moments_kernel, blocks), new_slot, inner, outer, ya, yb,
-        outs=whole + [block, block],
-        specs="svvvv",
-        scratch=[yedge, yedge, (8, nx * ROWS, nz), block, block],
+        functools.partial(moments_kernel), moves, inner, outer, ya, yb,
+        outs=results + [real(*block), real(*block)],
+        specs="vvvvv",
+        scratch=room(yedge, yedge, (8, nx * ROWS, nz), block, block),
     )
     ma, mb = swap(pay_a, "by", 0, True), swap(pay_b, "by", 1, True)
     return tuple(
         run(
-            functools.partial(place_kernel, blocks), new_slot, rho, vel, ma, mb,
-            outs=whole, specs="svvvv", scratch=[block, block],
+            functools.partial(place_kernel), moves, rho, vel, ma, mb,
+            outs=results, specs="vvvvv", scratch=room(block, block),
         )
     )
 

time: 44.2 us -> 39.3 us (0.89)
  Pallas kernels: 14.3 us -> 12 us
  local copies, waits for them, and re-layouts: 2.68 us -> 0.84 us
    pallas_call x8, Pallas kernels: 14.3 us -> 12 us  [run(): call(body, outs, specs, scratch, kernel.func.__name__[:-7], work, limit)]
    unnamed x6, local copies, waits for them, and re-layouts: 2.68 us -> 0.84 us
  transfers between devices with their start and end apart: 8 -> 8, of which waited for: 4 -> 3; matrix products, arithmetic and copies ran while one was open for 0% -> 0% of each run, Pallas kernels for 21% -> 22%
where the time goes in v4:
time: 39.3 us; the launch traced here: 38.9 us
  starting transfers between devices  20.7 us (53%)
  Pallas kernels  12 us (31%)
  waiting for transfers between devices  4.5 us (11%)
  local copies, waits for them, and re-layouts  0.84 us (2%)
  between operations  0.76 us (2%)
    ppermute x8, starting transfers between devices, swap(): return lax.ppermute(value, ('bx', 'by'), pairs)  20.7 us
    pallas_call x8, Pallas kernels, run(): call(body, outs, specs, scratch, kernel.func.__name__[:-7], work, limit)  12 us
    ppermute x8, waiting for transfers between devices, swap(): return lax.ppermute(value, ('bx', 'by'), pairs)  4.5 us
    unnamed x6, local copies, waits for them, and re-layouts  0.84 us
  transfers between devices with their start and end apart: 8, of which 3 were waited for; matrix products, arithmetic and copies ran while one was open for 0% of the time, Pallas kernels for 22%

profile of v4, /device:TPU:16, one launch (start us, length us, event | category | flops | bytes accessed | tf_op | source)
XLA Modules:
  0.0 38.9 jit_solution(7358065065185427987)
XLA Ops:
  0.6 0.8 %copy-done.1 = s32[1024]{0:T(1024)S(1)} copy-done((s32[1024]{0:T(1024)S(1)}, s32[1024]{0:T(1024)}, u32[]{:S(2)}) %copy-start.1) | copy-done | bytes 4120
  1.5 1.4 %face.1 = (s32[3,3,8,128]{3,2,1,0:T(8,128)S(1)}, f32[9,16,128]{2,1,0:T(8,128)S(1)}, f32[9,16,128]{2,1,0:T(8,128)S(1)}) custom-call(s32[1024]{0:T(1024)S(1)} %copy-done.1, f32[27,16,16,128]{3,2,1,0:T(8,128)} %refs_1_.7), custom_call_target="tpu_custom_call" | custom-call | flops 2000000 | bytes 1000000 | tf_op jit(solution)/shard_map/face/pallas_call | solution.py:648
  2.8 0.1 collective-permute-start
  2.9 4.2 %collective-permute-start.1 = (f32[9,16,128]{2,1,0:T(8,128)S(1)}, f32[9,16,128]{2,1,0:T(8,128)S(1)}, u32[]{:S(2)}, u32[]{:S(2)}) collective-permute-start(f32[9,16,128]{2,1,0:T(8,128)S(1)} %get-tuple-element.26), channel_id=1, source_target_pairs={{1,2},{3,4},{5,6},{7,8},{9,10},{11,12},{13,14},{15,0},{17,18},{19,... | collective-permute-start | bytes 221192 | tf_op jit(solution)/shard_map/ppermute | solution.py:609
  7.2 2.3 %first.1 = (f32[5,3,3,16,128]{4,3,2,1,0:T(8,128)S(1)}, f32[27,16,16,128]{3,2,1,0:T(8,128)S(1)}, f32[2,9,16,128]{3,2,1,0:T(8,128)S(1)}) custom-call(s32[3,3,8,128]{3,2,1,0:T(8,128)S(1)} %get-tuple-element.22.refs_0_.refs_1_, f32[27,16,16,128]{3,2,1,0:T(8,128)S(1)} %copy-done), custom_call_target="tpu_custom_call" | custom-call | flops 6000000 | bytes 3000000 | tf_op jit(solution)/shard_map/first/pallas_call | solution.py:648
  9.5 0.0 collective-permute-done.refs_4_.refs_5_
  9.5 0.0 collective-permute-done.1.refs_5_.refs_6_
  9.5 0.0 copy-start.2
  9.5 0.2 side.1
  9.7 3.5 %collective-permute-start.3 = (f32[24,16,128]{2,1,0:T(8,128)S(1)}, f32[24,16,128]{2,1,0:T(8,128)S(1)}, u32[]{:S(2)}, u32[]{:S(2)}) collective-permute-start(f32[24,16,128]{2,1,0:T(8,128)S(1)} %get-tuple-element.31), channel_id=1, source_target_pairs={{16,32},{48,64},{80,96},{112,0},{17,33},{49,65},{81,97},{113,1},{1... | collective-permute-start | bytes 589832 | tf_op jit(solution)/shard_map/ppermute | solution.py:609
  13.3 0.8 %collective-permute-start.2 = (f32[24,16,128]{2,1,0:T(8,128)S(1)}, f32[24,16,128]{2,1,0:T(8,128)S(1)}, u32[]{:S(2)}, u32[]{:S(2)}) collective-permute-start(f32[24,16,128]{2,1,0:T(8,128)S(1)} %get-tuple-element.28.refs_7_), channel_id=1, source_target_pairs={{0,16},{32,48},{64,80},{96,112},{1,17},{33,49},{65,81},{97,113},{2... | collective-permute-start | bytes 589832 | tf_op jit(solution)/shard_map/ppermute | solution.py:609
  14.0 6.2 %inner.1 = (f32[3,3,2,16,16,128]{5,4,3,2,1,0:T(8,128)S(1)}, f32[8,128,128]{2,1,0:T(8,128)S(1)}, f32[3,16,128]{2,1,0:T(8,128)S(1)}, f32[3,16,128]{2,1,0:T(8,128)S(1)}, s32[2,8,128]{2,1,0:T(8,128)S(1)}) custom-call(s32[8]{0:T(128)S(1)} %copy-done.2, s32[3,3,8,128]{3,2,1,0:T(8,128)S(1)} %get-tuple-element.22.refs_0_.refs_1_, f32[27,16,16,128]{3,2,1,0:T(8,128)S(1)} %copy-done, ...), custom_call_target="tpu_custom_call" | custom-call | flops 20000000 | bytes 10000000 | tf_op jit(solution)/shard_map/inner/pallas_call | solution.py:648
  20.3 0.0 collective-permute-done.3.refs_7_
  20.3 1.1 %collective-permute-done.2.refs_6_ = f32[24,16,128]{2,1,0:T(8,128)S(1)} collective-permute-done((f32[24,16,128]{2,1,0:T(8,128)S(1)}, f32[24,16,128]{2,1,0:T(8,128)S(1)}, u32[]{:S(2)}, u32[]{:S(2)}) %collective-permute-start.2) | collective-permute-done | bytes 196640 | tf_op jit(solution)/shard_map/ppermute | solution.py:609
  21.4 0.6 %outer.1 = (f32[8,32,128]{2,1,0:T(8,128)S(1)}, f32[3,16,128]{2,1,0:T(8,128)S(1)}, f32[3,16,128]{2,1,0:T(8,128)S(1)}) custom-call(s32[3,3,8,128]{3,2,1,0:T(8,128)S(1)} %get-tuple-element.22.refs_0_.refs_1_, f32[27,16,16,128]{3,2,1,0:T(8,128)S(1)} %copy-done, f32[27,16,16,128]{3,2,1,0:T(8,128)S(1)} %get-tuple-element.23.refs_2_.refs_3_, ...), custom_call_target="tpu_custom_call" | custom-call | flops 2000000 | bytes 1000000 | tf_op jit(solution)/shard_map/outer/pallas_call | solution.py:648
  22.0 0.1 collective-permute-start.4
  22.1 4.2 %collective-permute-start.5 = (f32[3,16,128]{2,1,0:T(8,128)S(1)}, f32[3,16,128]{2,1,0:T(8,128)S(1)}, u32[]{:S(2)}, u32[]{:S(2)}) collective-permute-start(f32[3,16,128]{2,1,0:T(8,128)S(1)} %get-tuple-element.37), channel_id=1, source_target_pairs={{1,2},{3,4},{5,6},{7,8},{9,10},{11,12},{13,14},{15,0},{17,18},{19,... | collective-permute-start | bytes 73736 | tf_op jit(solution)/shard_map/ppermute | solution.py:609
  26.3 0.2 turn.1.refs_2_
  26.5 1.3 %collective-permute-done.5.refs_4_ = f32[3,16,128]{2,1,0:T(8,128)S(1)} collective-permute-done((f32[3,16,128]{2,1,0:T(8,128)S(1)}, f32[3,16,128]{2,1,0:T(8,128)S(1)}, u32[]{:S(2)}, u32[]{:S(2)}) %collective-permute-start.5) | collective-permute-done | bytes 24608 | tf_op jit(solution)/shard_map/ppermute | solution.py:609
  27.8 0.3 moments.1
  28.1 0.1 collective-permute-start.6
  28.2 7.8 %collective-permute-start.7 = (f32[8,16,128]{2,1,0:T(8,128)S(1)}, f32[8,16,128]{2,1,0:T(8,128)S(1)}, u32[]{:S(2)}, u32[]{:S(2)}) collective-permute-start(f32[8,16,128]{2,1,0:T(8,128)S(1)} %get-tuple-element.41), channel_id=1, source_target_pairs={{1,2},{3,4},{5,6},{7,8},{9,10},{11,12},{13,14},{15,16},{17,18},{19... | collective-permute-start | bytes 196616 | tf_op jit(solution)/shard_map/ppermute | solution.py:609
  35.9 2.0 %collective-permute-done.7.refs_4_ = f32[8,16,128]{2,1,0:T(8,128)S(1)} collective-permute-done((f32[8,16,128]{2,1,0:T(8,128)S(1)}, f32[8,16,128]{2,1,0:T(8,128)S(1)}, u32[]{:S(2)}, u32[]{:S(2)}) %collective-permute-start.7) | collective-permute-done | bytes 65568 | tf_op jit(solution)/shard_map/ppermute | solution.py:609
  38.0 0.9 %place.1 = (f32[8,4096]{1,0:T(8,128)}, f32[3,8,4096]{2,1,0:T(8,128)}) custom-call(s32[2,8,128]{2,1,0:T(8,128)S(1)} %get-tuple-element.29.refs_0_, f32[8,4096]{1,0:T(8,128)S(1)} %get-tuple-element.38.refs_1_, f32[3,8,4096]{2,1,0:T(8,128)S(1)} %get-tuple-element.39.refs_2_, f32[8,16,128]{2,1,0:T(8,128)S(1)} %collective-permute-done.6.refs_3_, ...), custom_call_target="tpu_custom_call" | custom-call | flops 2000000 | bytes 1000000 | tf_op jit(solution)/shard_map/place/pallas_call | solution.py:648
  (6 shorter events, 0.0 us)
Async XLA Ops:
  0.6 6.5 %copy-start = (f32[27,16,16,128]{3,2,1,0:T(8,128)S(1)}, f32[27,16,16,128]{3,2,1,0:T(8,128)}, u32[]{:S(2)}) copy-start(f32[27,16,16,128]{3,2,1,0:T(8,128)} %refs_1_.7) | copy-start | bytes 10616836
  0.6 0.8 %copy-start.1 = (s32[1024]{0:T(1024)S(1)}, s32[1024]{0:T(1024)}, u32[]{:S(2)}) copy-start(s32[1024]{0:T(1024)} %refs_0_.2) | copy-start | bytes 12292
  2.8 6.6 %collective-permute-start = (f32[9,16,128]{2,1,0:T(8,128)S(1)}, f32[9,16,128]{2,1,0:T(8,128)S(1)}, u32[]{:S(2)}, u32[]{:S(2)}) collective-permute-start(f32[9,16,128]{2,1,0:T(8,128)S(1)} %get-tuple-element.25), channel_id=1, source_target_pairs={{0,1},{2,3},{4,5},{6,7},{8,9},{10,11},{12,13},{14,15},{16,17},{18,... | collective-permute-start | bytes 221192 | tf_op jit(solution)/shard_map/ppermute | solution.py:609
  2.9 6.5 %collective-permute-start.1 = (f32[9,16,128]{2,1,0:T(8,128)S(1)}, f32[9,16,128]{2,1,0:T(8,128)S(1)}, u32[]{:S(2)}, u32[]{:S(2)}) collective-permute-start(f32[9,16,128]{2,1,0:T(8,128)S(1)} %get-tuple-element.26), channel_id=1, source_target_pairs={{1,2},{3,4},{5,6},{7,8},{9,10},{11,12},{13,14},{15,0},{17,18},{19,... | collective-permute-start | bytes 221192 | tf_op jit(solution)/shard_map/ppermute | solution.py:609
  9.5 4.5 %copy-start.2 = (s32[8]{0:T(128)S(1)}, s32[8]{0:T(128)}, u32[]{:S(2)}) copy-start(s32[8]{0:T(128)} %refs_0_.3) | copy-start | bytes 100
  9.7 10.6 %collective-permute-start.3 = (f32[24,16,128]{2,1,0:T(8,128)S(1)}, f32[24,16,128]{2,1,0:T(8,128)S(1)}, u32[]{:S(2)}, u32[]{:S(2)}) collective-permute-start(f32[24,16,128]{2,1,0:T(8,128)S(1)} %get-tuple-element.31), channel_id=1, source_target_pairs={{16,32},{48,64},{80,96},{112,0},{17,33},{49,65},{81,97},{113,1},{1... | collective-permute-start | bytes 589832 | tf_op jit(solution)/shard_map/ppermute | solution.py:609
  13.3 8.1 %collective-permute-start.2 = (f32[24,16,128]{2,1,0:T(8,128)S(1)}, f32[24,16,128]{2,1,0:T(8,128)S(1)}, u32[]{:S(2)}, u32[]{:S(2)}) collective-permute-start(f32[24,16,128]{2,1,0:T(8,128)S(1)} %get-tuple-element.28.refs_7_), channel_id=1, source_target_pairs={{0,16},{32,48},{64,80},{96,112},{1,17},{33,49},{65,81},{97,113},{2... | collective-permute-start | bytes 589832 | tf_op jit(solution)/shard_map/ppermute | solution.py:609
  22.0 4.5 %collective-permute-start.4 = (f32[3,16,128]{2,1,0:T(8,128)S(1)}, f32[3,16,128]{2,1,0:T(8,128)S(1)}, u32[]{:S(2)}, u32[]{:S(2)}) collective-permute-start(f32[3,16,128]{2,1,0:T(8,128)S(1)} %get-tuple-element.36), channel_id=1, source_target_pairs={{0,1},{2,3},{4,5},{6,7},{8,9},{10,11},{12,13},{14,15},{16,17},{18,... | collective-permute-start | bytes 73736 | tf_op jit(solution)/shard_map/ppermute | solution.py:609
  22.1 5.7 %collective-permute-start.5 = (f32[3,16,128]{2,1,0:T(8,128)S(1)}, f32[3,16,128]{2,1,0:T(8,128)S(1)}, u32[]{:S(2)}, u32[]{:S(2)}) collective-permute-start(f32[3,16,128]{2,1,0:T(8,128)S(1)} %get-tuple-element.37), channel_id=1, source_target_pairs={{1,2},{3,4},{5,6},{7,8},{9,10},{11,12},{13,14},{15,0},{17,18},{19,... | collective-permute-start | bytes 73736 | tf_op jit(solution)/shard_map/ppermute | solution.py:609
  28.1 7.9 %collective-permute-start.6 = (f32[8,16,128]{2,1,0:T(8,128)S(1)}, f32[8,16,128]{2,1,0:T(8,128)S(1)}, u32[]{:S(2)}, u32[]{:S(2)}) collective-permute-start(f32[8,16,128]{2,1,0:T(8,128)S(1)} %get-tuple-element.40), channel_id=1, source_target_pairs={{0,1},{2,3},{4,5},{6,7},{8,9},{10,11},{12,13},{14,15},{16,17},{18,... | collective-permute-start | bytes 196616 | tf_op jit(solution)/shard_map/ppermute | solution.py:609
  28.2 9.8 %collective-permute-start.7 = (f32[8,16,128]{2,1,0:T(8,128)S(1)}, f32[8,16,128]{2,1,0:T(8,128)S(1)}, u32[]{:S(2)}, u32[]{:S(2)}) collective-permute-start(f32[8,16,128]{2,1,0:T(8,128)S(1)} %get-tuple-element.41), channel_id=1, source_target_pairs={{1,2},{3,4},{5,6},{7,8},{9,10},{11,12},{13,14},{15,16},{17,18},{19... | collective-permute-start | bytes 196616 | tf_op jit(solution)/shard_map/ppermute | solution.py:609

commit v5 on v4

--- a/solution.py
+++ b/solution.py
@@ -164,12 +164,14 @@
 def store_by_parity(odd, first, second, up, down):
     @pl.when(odd == 0)
     def _():
-        first[...] = up[...]
+        if first is not None:
+            first[...] = up[...]
         second[...] = down[...]
 
     @pl.when(odd == 1)
     def _():
-        first[...] = down[...]
+        if first is not None:
+            first[...] = down[...]
         second[...] = up[...]
 
 
@@ -370,10 +372,12 @@
 
 def leaving(slots, blocks, step):
     here = lax.axis_index("bx") * lax.axis_size("by") + lax.axis_index("by")
-    which = jnp.int32(-1)
+    which, theirs = jnp.int32(-1), jnp.int32(0)
     for k in range(blocks):
-        which = jnp.where(slots[k] // blocks == here + step, k, which)
-    return which
+        goes = slots[k] // blocks == here + step
+        which = jnp.where(goes, k, which)
+        theirs = jnp.where(goes, lax.rem(slots[k], blocks), theirs)
+    return which, theirs
 
 
 def inner_kernel(
@@ -382,7 +386,9 @@
 ):
     load_by_parity(lax.rem(lax.axis_index("by"), 2), ya, yb, above, below)
     for n, step in enumerate((1, -1)):
-        moves[n, :, :] = jnp.full((ROWS, LANES), leaving(slots, blocks, step), jnp.int32)
+        which, theirs = leaving(slots, blocks, step)
+        moves[n, :, :] = jnp.full((ROWS, LANES), which, jnp.int32)
+        moves[2 + n, :, :] = jnp.full((ROWS, LANES), theirs, jnp.int32)
     fine = marks[1, 1, :, :] == 1
     row = sublane()
     reflect, turn = turns()
@@ -435,7 +441,7 @@
 
 def outer_kernel(
     marks, f, g, table, ya, yb, xa, xb, sums, in_up, in_down,
-    part, pay_a, pay_b, above, below, right, left, state, ends, up, down,
+    part, pay, away, above, below, right, left, state, ends, up, down,
 ):
     load_by_parity(lax.rem(lax.axis_index("by"), 2), ya, yb, above, below)
     load_by_parity(lax.rem(lax.axis_index("bx"), 2), xa, xb, right, left)
@@ -444,7 +450,7 @@
     reflect, turn = turns()
     nx = f.shape[1]
     hold = {-1: 0, 0: 1, nx - 1: 2, nx: 3}
-    for side, x, k, pay in ((-1, 0, 3, left), (1, nx - 1, 4, right)):
+    for side, x, k, got in ((-1, 0, 3, left), (1, nx - 1, 4, right)):
         for h in (0, 1):
             rows = slice(8 * h, 8 * h + 8)
 
@@ -461,7 +467,7 @@
             def moved(c):
                 a, b, e = c
                 if a == -side:
-                    tile = pay[face(b, e), rows, :]
+                    tile = got[face(b, e), rows, :]
                 else:
                     tile = read(c, x - a)
                 tile = jnp.where(fine[0], tile, f[comp(*c), x, rows, :])
@@ -478,12 +484,12 @@
             )
 
             def toward(c):
-                return pay[9 + face(c[1], c[2]), rows, :]
+                return got[9 + face(c[1], c[2]), rows, :]
 
             second_collide(
                 {
                     side: group_sums(lambda b, e: read((side, b, e), x)),
-                    0: tuple(pay[18 + n, rows, :] for n in range(6)),
+                    0: tuple(got[18 + n, rows, :] for n in range(6)),
                     -side: group_sums(lambda b, e: toward((-side, b, e))),
                 },
                 toward,
@@ -513,12 +519,14 @@
             down[n, x : x + 1, :] = value
 
         gather_layer(fetch, row, put, put_up, put_down)
-    for pay in (up, down):
+    for edge in (up, down):
         for n in range(3):
             for x in range(0, nx, ROWS):
                 rows = slice(x, x + ROWS)
-                pay[n, rows, :] = block_rows(pay[n, rows, :], reflect, turn)
-    store_by_parity(lax.rem(lax.axis_index("by"), 2), pay_a, pay_b, up, down)
+                edge[n, rows, :] = block_rows(edge[n, rows, :], reflect, turn)
+    odd = lax.rem(lax.axis_index("by"), 2)
+    store_by_parity(odd, pay.at[pl.ds(0, 3)], pay.at[pl.ds(3, 3)], up, down)
+    store_by_parity(odd, None, away, up, down)
 
 
 def turn_kernel(part, out):
@@ -529,75 +537,134 @@
             out[n, rows, :] = block_rows(part[n, rows, :], reflect, turn)
 
 
-def moments_kernel(
-    moves, inner, outer, got_a, got_b, rho_out, vel_out, pay_a, pay_b,
-    above, below, made, up, down,
-):
+def add_crossed(made, crossed, top):
+    nx = crossed.shape[1]
+    width = LANES // ROWS
+    spot = top * (ROWS - 1)
+    sign = jnp.where(top == 1, -1.0, 1.0)
+    mask = lane_block(width) == spot
+    for x in range(nx):
+        rows = slice(ROWS * x, ROWS * x + ROWS)
+        first = x // ROWS * ROWS
+        shift = lax.rem(width * (spot - x % ROWS) + LANES, LANES)
+        total, cross, along = (
+            jnp.where(mask, pltpu.roll(crossed[n, first : first + ROWS, :], shift, 1), 0.0)
+            for n in range(3)
+        )
+        for n, more in enumerate((total, cross, sign * total, along)):
+            made[2 * n + top, rows, :] += more
+
+
+def pack_block(made, pay, start, which):
+    for n in range(8):
+        pay[start + n, :, :] = made[n, pl.ds(which, pay.shape[1], stride=ROWS), :]
+
+
+def number(tile):
+    return jnp.maximum(jnp.max(tile), 0)
+
+
+def pack_kernel(moves, inner, outer, got, made, block, pay_w):
+    iy = lax.axis_index("by")
+    odd = lax.rem(iy, 2)
+    nx = got.shape[1]
+    low, high = ROWS * 2, ROWS * (nx - 2)
+    made[:, 0:low, :] = outer[:, 0:low, :]
+    made[:, low:high, :] = inner[:, low:high, :]
+    made[:, high:, :] = outer[:, low:, :]
+    add_crossed(made, got, 1 - odd)
+    pack_block(made, block, 0, number(moves[1 - odd, :, :]))
+    end = jnp.logical_or(iy == 0, iy == lax.axis_size("by") - 1)
+
+    @pl.when(end)
+    def _():
+        pay_w[0:8, :, :] = block[...]
+
+    @pl.when(jnp.logical_not(end))
+    def _():
+        pay_w[0:3, :, :] = got[3:6, :, :]
+
+
+def join_kernel(first, second, out):
+    out[0 : first.shape[0], :, :] = first[...]
+    out[first.shape[0] :, :, :] = second[...]
+
+
+def moments_kernel(moves, part, got_b, got_w, rho_out, vel_out, pay_a, made):
     odd = lax.rem(lax.axis_index("by"), 2)
-    load_by_parity(odd, got_a, got_b, above, below)
-    nx = above.shape[1]
+    nx = got_b.shape[1]
+    made[...] = part[...]
+    add_crossed(made, got_b, odd)
+    for x in range(nx):
+        rows = slice(ROWS * x, ROWS * x + ROWS)
+        for h in (0, 1):
+            rho = made[h, rows, :]
+            inv = 1.0 / rho
+            lanes = slice((2 * x + h) * LANES, (2 * x + h + 1) * LANES)
+            rho_out[:, lanes] = rho
+            for n in range(1, 4):
+                tile = made[2 * n + h, rows, :] * inv
+                made[2 * n + h, rows, :] = tile
+                vel_out[n - 1, :, lanes] = tile
+    pack_block(made, pay_a, 0, number(moves[odd, :, :]))
+    pay_a[8:11, :, :] = got_w[0:3, :, :]
+
+
+def place_kernel(moves, rho, vel, away, got_a, got_b, got_w, rho_out, vel_out, block, crossed):
+    iy = lax.axis_index("by")
+    odd = lax.rem(iy, 2)
+    end = jnp.logical_or(iy == 0, iy == lax.axis_size("by") - 1)
+
+    @pl.when(end)
+    def _():
+        block[...] = got_w[0:8, :, :]
+        crossed[...] = got_a[8:11, :, :]
+
+    @pl.when(jnp.logical_not(end))
+    def _():
+        block[...] = got_b[3:11, :, :]
+        crossed[...] = away[...]
+
+    row = sublane()
     width = LANES // ROWS
-    group = lane_block(width)
-    at = {0: 0, 1: 1, nx - 2: 2, nx - 1: 3}
-    for x in range(nx):
+    top = 1 - odd
+    sign = jnp.where(top == 1, -1.0, 1.0)
+    mask = lane_block(width) == top * (ROWS - 1)
+    spread = row * width + (lane_block(1) & (width - 1))
+    theirs = number(moves[3 - odd, :, :])
+    for first in range(0, block.shape[1], ROWS):
+        rows = slice(first, first + ROWS)
+        extra = []
+        for n in range(3):
+            line = jnp.broadcast_to(crossed[n, pl.ds(first + theirs, 1), :], (ROWS, LANES))
+            extra.append(jnp.where(mask, jnp.take_along_axis(line, spread, axis=1), 0.0))
+        total, cross, along = extra
+        for n, more in enumerate((total, cross, sign * total, along)):
+            block[2 * n + top, rows, :] += more
         for h in (0, 1):
-            rows = slice(ROWS * x, ROWS * x + ROWS)
-            spot, halo, sign = (0, below, 1.0) if h == 0 else (ROWS - 1, above, -1.0)
-            first = x // ROWS * ROWS
-            extra = []
-            for n in range(3):
-                tile = lane_roll(halo[n, first : first + ROWS, :], width * (spot - x % ROWS))
-                extra.append(jnp.where(group == spot, tile, 0.0))
-            total, cross, along = extra
-            values = []
-            for n, more in enumerate((total, cross, sign * total, along)):
-                if x in at:
-                    tile = outer[2 * n + h, ROWS * at[x] : ROWS * at[x] + ROWS, :]
-                else:
-                    tile = inner[2 * n + h, rows, :]
-                values.append(tile + more)
-            inv = 1.0 / values[0]
-            lanes = slice((2 * x + h) * LANES, (2 * x + h + 1) * LANES)
-            for n in range(4):
-                tile = values[0] if n == 0 else values[n] * inv
-                made[2 * n + h, rows, :] = tile
-                if n == 0:
-                    rho_out[:, lanes] = tile
-                else:
-                    vel_out[n - 1, :, lanes] = tile
-    for k, pay in enumerate((up, down)):
-        which = jnp.maximum(jnp.max(moves[k, :, :]), 0)
-        for n in range(8):
-            pay[n, :, :] = made[n, pl.ds(which, nx, stride=ROWS), :]
-    store_by_parity(odd, pay_a, pay_b, up, down)
-
-
-def place_kernel(moves, rho, vel, got_a, got_b, rho_out, vel_out, after, before):
-    odd = lax.rem(lax.axis_index("by"), 2)
-    load_by_parity(odd, got_a, got_b, after, before)
-    row = sublane()
-    to_next = row == moves[0, :, :]
-    to_prev = row == moves[1, :, :]
-    for x in range(after.shape[1]):
+            inv = 1.0 / block[h, rows, :]
+            for n in range(1, 4):
+                block[2 * n + h, rows, :] *= inv
+    near = row == moves[odd, :, :]
+    far = row == moves[1 - odd, :, :]
+    for x in range(block.shape[1]):
         for h in (0, 1):
             lanes = slice((2 * x + h) * LANES, (2 * x + h + 1) * LANES)
             for n in range(4):
                 k = 2 * n + h
                 tile = rho[:, lanes] if n == 0 else vel[n - 1, :, lanes]
-                tile = jnp.where(to_next, after[k, x : x + 1, :], tile)
-                tile = jnp.where(to_prev, before[k, x : x + 1, :], tile)
+                tile = jnp.where(near, got_a[k, x : x + 1, :], tile)
+                tile = jnp.where(far, block[k, x : x + 1, :], tile)
                 if n == 0:
                     rho_out[:, lanes] = tile
                 else:
                     vel_out[n - 1, :, lanes] = tile
 
 
-def swap(value, axis, odd, curve=False):
+def swap(value, axis, odd):
     count_x, count_y = lax.axis_size("bx"), lax.axis_size("by")
     pairs = []
-    if curve:
-        pairs = [(j, j + 1) for j in range(odd, count_x * count_y - 1, 2)]
-    elif axis == "by":
+    if axis == "by":
         for x in range(count_x):
             for y in range(odd, count_y, 2):
                 pairs.append((x * count_y + y, x * count_y + (y + 1) % count_y))
@@ -606,6 +673,20 @@
             for x in range(odd, count_x, 2):
                 pairs.append((x * count_y + y, (x + 1) % count_x * count_y + y))
     pairs = pairs + [(b, a) for a, b in pairs]
+    return lax.ppermute(value, ("bx", "by"), pairs)
+
+
+def swap_ends(value):
+    count_x, count_y = lax.axis_size("bx"), lax.axis_size("by")
+    pairs = []
+    for x in range(count_x):
+        here, after = x * count_y, (x + 1) * count_y
+        if x + 1 < count_x:
+            pairs += [(after - 1, after), (after, after - 1)]
+            pairs += [(here + 1, after + 1), (after + count_y - 2, after - 2)]
+        pairs += [(here + y, here + (y ^ 1)) for y in range(2, count_y - 2)]
+    pairs += [(0, 1), (after - 1, after - 2)]
+    pairs += [(after - count_y + 1, after - 1), (count_y - 2, 0)]
     return lax.ppermute(value, ("bx", "by"), pairs)
 
 
@@ -629,7 +710,7 @@
     shape = (lax.axis_size("bx"), lax.axis_size("by"))
     blocks = new_slot.shape[0]
     _, nx, ny, nz = populations.shape
-    yface, xface, yedge, block = (9, nx, nz), (24, ny, nz), (3, nx, nz), (8, nx, nz)
+    yface, xface, yedge = (9, nx, nz), (24, ny, nz), (3, nx, nz)
     tile = (ROWS, nz)
 
     def real(*dims):
@@ -673,38 +754,47 @@
         new_slot, marks, populations, g, table, ya, yb, pay_a,
         outs=[
             real(3, 3, 2, nx, ny, nz), real(8, nx * ROWS, nz), real(*yedge), real(*yedge),
-            whole(2, *tile),
+            whole(4, *tile),
         ],
         specs="svvvvvva",
         scratch=room(yface, yface, (27, ny, nz)),
         work=10,
     )
-    part, pay_a, pay_b = run(
+    part, pay_a, away = run(
         functools.partial(outer_kernel),
         marks, populations, g, table, ya, yb, xa, xb, sums, up, down,
-        outs=[real(8, 4 * ROWS, nz), real(*yedge), real(*yedge)],
+        outs=[real(8, 4 * ROWS, nz), real(6, nx, nz), real(*yedge)],
         specs="vvvvvvvvvvv",
         scratch=room(
             yface, yface, xface, xface, (27, ny, nz), (3, 3, 2, 4, ny, nz), yedge, yedge
         ),
     )
-    ya, yb = swap(pay_a, "by", 0), swap(pay_b, "by", 1)
+    got_a = swap(pay_a, "by", 0)
     (outer,) = run(
         functools.partial(turn_kernel), part, outs=[real(8, 4 * ROWS, nz)], specs="v"
     )
+    part, block, pay_w = run(
+        functools.partial(pack_kernel), moves, inner, outer, got_a,
+        outs=[real(8, nx * ROWS, nz), real(8, nx, nz), real(12, nx, nz)], specs="vvvv",
+    )
+    got_w = swap_ends(pay_w)
+    (pay_b,) = run(
+        functools.partial(join_kernel), away, block, outs=[real(11, nx, nz)], specs="vv"
+    )
+    got_b = swap(pay_b, "by", 1)
     cells = nx * ny * nz // blocks
     results = [real(blocks, cells), real(3, blocks, cells)]
-    rho, vel, pay_a, pay_b = run(
-        functools.partial(moments_kernel), moves, inner, outer, ya, yb,
-        outs=results + [real(*block), real(*block)],
-        specs="vvvvv",
-        scratch=room(yedge, yedge, (8, nx * ROWS, nz), block, block),
-    )
-    ma, mb = swap(pay_a, "by", 0, True), swap(pay_b, "by", 1, True)
+    rho, vel, pay_a = run(
+        functools.partial(moments_kernel), moves, part, got_b, got_w,
+        outs=results + [real(11, nx, nz)],
+        specs="vvvv",
+        scratch=room((8, nx * ROWS, nz)),
+    )
+    got_a = swap(pay_a, "by", 0)
     return tuple(
         run(
-            functools.partial(place_kernel), moves, rho, vel, ma, mb,
-            outs=results, specs="vvvvv", scratch=room(block, block),
+            functools.partial(place_kernel), moves, rho, vel, away, got_a, got_b, got_w,
+            outs=results, specs="vvvvvvv", scratch=room((8, nx, nz), yedge),
         )
     )
 

time: 39.3 us -> 39.1 us (level)
  starting transfers between devices: 20.7 us -> 14.7 us
  waiting for transfers between devices: 4.5 us -> 9.5 us
  Pallas kernels: 12 us -> 12.6 us
    ppermute x8 -> x7, starting transfers between devices: 20.7 us -> 8.8 us  [swap(): return lax.ppermute(value, ('bx', 'by'), pairs)]
    ppermute x0 -> x1, starting transfers between devices: none -> 5.92 us  [swap_ends(): return lax.ppermute(value, ('bx', 'by'), pairs)]
    ppermute x8 -> x7, waiting for transfers between devices: 4.5 us -> 9.49 us  [swap(): return lax.ppermute(value, ('bx', 'by'), pairs)]
    pallas_call x8 -> x10, Pallas kernels: 12 us -> 12.6 us  [run(): call(body, outs, specs, scratch, kernel.func.__name__[:-7], work, limit)]
  transfers between devices with their start and end apart: 8 -> 8, of which waited for: 3 -> 4; matrix products, arithmetic and copies ran while one was open for 0% -> 0% of each run, Pallas kernels for 22% -> 23%
where the time goes in v5:
time: 39.1 us; the launch traced here: 38.4 us
  starting transfers between devices  14.7 us (38%)
  Pallas kernels  12.6 us (32%)
  waiting for transfers between devices  9.5 us (24%)
  local copies, waits for them, and re-layouts  0.84 us (2%)
  between operations  0.75 us (2%)
    pallas_call x10, Pallas kernels, run(): call(body, outs, specs, scratch, kernel.func.__name__[:-7], work, limit)  12.6 us
    ppermute x7, waiting for transfers between devices, swap(): return lax.ppermute(value, ('bx', 'by'), pairs)  9.49 us
    ppermute x7, starting transfers between devices, swap(): return lax.ppermute(value, ('bx', 'by'), pairs)  8.8 us
    ppermute x1, starting transfers between devices, swap_ends(): return lax.ppermute(value, ('bx', 'by'), pairs)  5.92 us
    unnamed x6, local copies, waits for them, and re-layouts  0.84 us
  transfers between devices with their start and end apart: 8, of which 4 were waited for; matrix products, arithmetic and copies ran while one was open for 0% of the time, Pallas kernels for 23%

profile of v5, /device:TPU:16, one launch (start us, length us, event | category | flops | bytes accessed | tf_op | source)
XLA Modules:
  0.0 38.4 jit_solution(8923990638863393100)
XLA Ops:
  0.6 0.8 %copy-done.1 = s32[1024]{0:T(1024)S(1)} copy-done((s32[1024]{0:T(1024)S(1)}, s32[1024]{0:T(1024)}, u32[]{:S(2)}) %copy-start.1) | copy-done | bytes 4120
  1.5 1.4 %face.1 = (s32[3,3,8,128]{3,2,1,0:T(8,128)S(1)}, f32[9,16,128]{2,1,0:T(8,128)S(1)}, f32[9,16,128]{2,1,0:T(8,128)S(1)}) custom-call(s32[1024]{0:T(1024)S(1)} %copy-done.1, f32[27,16,16,128]{3,2,1,0:T(8,128)} %refs_1_.7), custom_call_target="tpu_custom_call" | custom-call | flops 2000000 | bytes 1000000 | tf_op jit(solution)/shard_map/face/pallas_call | solution.py:729
  2.8 0.1 collective-permute-start
  2.9 4.2 %collective-permute-start.1 = (f32[9,16,128]{2,1,0:T(8,128)S(1)}, f32[9,16,128]{2,1,0:T(8,128)S(1)}, u32[]{:S(2)}, u32[]{:S(2)}) collective-permute-start(f32[9,16,128]{2,1,0:T(8,128)S(1)} %get-tuple-element.28), channel_id=1, source_target_pairs={{1,2},{3,4},{5,6},{7,8},{9,10},{11,12},{13,14},{15,0},{17,18},{19,... | collective-permute-start | bytes 221192 | tf_op jit(solution)/shard_map/ppermute | solution.py:676
  7.2 2.3 %first.1 = (f32[5,3,3,16,128]{4,3,2,1,0:T(8,128)S(1)}, f32[27,16,16,128]{3,2,1,0:T(8,128)S(1)}, f32[2,9,16,128]{3,2,1,0:T(8,128)S(1)}) custom-call(s32[3,3,8,128]{3,2,1,0:T(8,128)S(1)} %get-tuple-element.24.refs_0_.refs_1_, f32[27,16,16,128]{3,2,1,0:T(8,128)S(1)} %copy-done), custom_call_target="tpu_custom_call" | custom-call | flops 6000000 | bytes 3000000 | tf_op jit(solution)/shard_map/first/pallas_call | solution.py:729
  9.5 0.0 collective-permute-done.refs_4_.refs_5_
  9.5 0.0 collective-permute-done.1.refs_5_.refs_6_
  9.5 0.0 copy-start.2
  9.5 0.2 side.1
  9.7 3.5 %collective-permute-start.3 = (f32[24,16,128]{2,1,0:T(8,128)S(1)}, f32[24,16,128]{2,1,0:T(8,128)S(1)}, u32[]{:S(2)}, u32[]{:S(2)}) collective-permute-start(f32[24,16,128]{2,1,0:T(8,128)S(1)} %get-tuple-element.33), channel_id=1, source_target_pairs={{16,32},{48,64},{80,96},{112,0},{17,33},{49,65},{81,97},{113,1},{1... | collective-permute-start | bytes 589832 | tf_op jit(solution)/shard_map/ppermute | solution.py:676
  13.3 0.8 %collective-permute-start.2 = (f32[24,16,128]{2,1,0:T(8,128)S(1)}, f32[24,16,128]{2,1,0:T(8,128)S(1)}, u32[]{:S(2)}, u32[]{:S(2)}) collective-permute-start(f32[24,16,128]{2,1,0:T(8,128)S(1)} %get-tuple-element.30.refs_7_), channel_id=1, source_target_pairs={{0,16},{32,48},{64,80},{96,112},{1,17},{33,49},{65,81},{97,113},{2... | collective-permute-start | bytes 589832 | tf_op jit(solution)/shard_map/ppermute | solution.py:676
  14.0 6.2 %inner.1 = (f32[3,3,2,16,16,128]{5,4,3,2,1,0:T(8,128)S(1)}, f32[8,128,128]{2,1,0:T(8,128)S(1)}, f32[3,16,128]{2,1,0:T(8,128)S(1)}, f32[3,16,128]{2,1,0:T(8,128)S(1)}, s32[4,8,128]{2,1,0:T(8,128)S(1)}) custom-call(s32[8]{0:T(128)S(1)} %copy-done.2, s32[3,3,8,128]{3,2,1,0:T(8,128)S(1)} %get-tuple-element.24.refs_0_.refs_1_, f32[27,16,16,128]{3,2,1,0:T(8,128)S(1)} %copy-done, ...), custom_call_target="tpu_custom_call" | custom-call | flops 20000000 | bytes 10000000 | tf_op jit(solution)/shard_map/inner/pallas_call | solution.py:729
  20.3 1.1 %collective-permute-done.2.refs_6_ = f32[24,16,128]{2,1,0:T(8,128)S(1)} collective-permute-done((f32[24,16,128]{2,1,0:T(8,128)S(1)}, f32[24,16,128]{2,1,0:T(8,128)S(1)}, u32[]{:S(2)}, u32[]{:S(2)}) %collective-permute-start.2) | collective-permute-done | bytes 196640 | tf_op jit(solution)/shard_map/ppermute | solution.py:676
  21.4 0.6 %outer.1 = (f32[8,32,128]{2,1,0:T(8,128)S(1)}, f32[6,16,128]{2,1,0:T(8,128)S(1)}, f32[3,16,128]{2,1,0:T(8,128)S(1)}) custom-call(s32[3,3,8,128]{3,2,1,0:T(8,128)S(1)} %get-tuple-element.24.refs_0_.refs_1_, f32[27,16,16,128]{3,2,1,0:T(8,128)S(1)} %copy-done, f32[27,16,16,128]{3,2,1,0:T(8,128)S(1)} %get-tuple-element.25.refs_2_.refs_3_, ...), custom_call_target="tpu_custom_call" | custom-call | flops 2000000 | bytes 1000000 | tf_op jit(solution)/shard_map/outer/pallas_call | solution.py:729
  22.0 0.1 collective-permute-start.4
  22.1 0.2 turn.1.refs_2_
  22.3 1.0 %collective-permute-done.4.refs_3_ = f32[6,16,128]{2,1,0:T(8,128)S(1)} collective-permute-done((f32[6,16,128]{2,1,0:T(8,128)S(1)}, f32[6,16,128]{2,1,0:T(8,128)S(1)}, u32[]{:S(2)}, u32[]{:S(2)}) %collective-permute-start.4) | collective-permute-done | bytes 49184 | tf_op jit(solution)/shard_map/ppermute | solution.py:676
  23.3 0.2 pack.1
  23.6 5.9 %collective-permute-start.6 = (f32[12,16,128]{2,1,0:T(8,128)S(1)}, f32[12,16,128]{2,1,0:T(8,128)S(1)}, u32[]{:S(2)}, u32[]{:S(2)}) collective-permute-start(f32[12,16,128]{2,1,0:T(8,128)S(1)} %get-tuple-element.42), channel_id=1, source_target_pairs={{15,16},{16,15},{1,17},{30,14},{2,3},{3,2},{4,5},{5,4},{6,7},{7,6}... | collective-permute-start | bytes 294920 | tf_op jit(solution)/shard_map/ppermute | solution.py:690
  29.5 6.1 %collective-permute-done.5.refs_2_.refs_5_ = f32[11,16,128]{2,1,0:T(8,128)S(1)} collective-permute-done((f32[11,16,128]{2,1,0:T(8,128)S(1)}, f32[11,16,128]{2,1,0:T(8,128)S(1)}, u32[]{:S(2)}, u32[]{:S(2)}) %collective-permute-start.5) | collective-permute-done | bytes 90144 | tf_op jit(solution)/shard_map/ppermute | solution.py:676
  35.5 0.3 moments.1
  35.9 0.1 collective-permute-start.7
  36.0 1.3 %collective-permute-done.7.refs_4_ = f32[11,16,128]{2,1,0:T(8,128)S(1)} collective-permute-done((f32[11,16,128]{2,1,0:T(8,128)S(1)}, f32[11,16,128]{2,1,0:T(8,128)S(1)}, u32[]{:S(2)}, u32[]{:S(2)}) %collective-permute-start.7) | collective-permute-done | bytes 90144 | tf_op jit(solution)/shard_map/ppermute | solution.py:676
  37.2 1.1 %place.1 = (f32[8,4096]{1,0:T(8,128)}, f32[3,8,4096]{2,1,0:T(8,128)}) custom-call(s32[4,8,128]{2,1,0:T(8,128)S(1)} %get-tuple-element.31.refs_0_, f32[8,4096]{1,0:T(8,128)S(1)} %get-tuple-element.43.refs_1_, f32[3,8,4096]{2,1,0:T(8,128)S(1)} %get-tuple-element.44.refs_2_, f32[3,16,128]{2,1,0:T(8,128)S(1)} %get-tuple-element.40.refs_0_.refs_3_, ...), custom_call_target="tpu_custom_call" | custom-call | flops 2000000 | bytes 1000000 | tf_op jit(solution)/shard_map/place/pallas_call | solution.py:729
  (8 shorter events, 0.0 us)
Async XLA Ops:
  0.6 6.5 %copy-start = (f32[27,16,16,128]{3,2,1,0:T(8,128)S(1)}, f32[27,16,16,128]{3,2,1,0:T(8,128)}, u32[]{:S(2)}) copy-start(f32[27,16,16,128]{3,2,1,0:T(8,128)} %refs_1_.7) | copy-start | bytes 10616836
  0.6 0.8 %copy-start.1 = (s32[1024]{0:T(1024)S(1)}, s32[1024]{0:T(1024)}, u32[]{:S(2)}) copy-start(s32[1024]{0:T(1024)} %refs_0_.2) | copy-start | bytes 12292
  2.8 6.6 %collective-permute-start = (f32[9,16,128]{2,1,0:T(8,128)S(1)}, f32[9,16,128]{2,1,0:T(8,128)S(1)}, u32[]{:S(2)}, u32[]{:S(2)}) collective-permute-start(f32[9,16,128]{2,1,0:T(8,128)S(1)} %get-tuple-element.27), channel_id=1, source_target_pairs={{0,1},{2,3},{4,5},{6,7},{8,9},{10,11},{12,13},{14,15},{16,17},{18,... | collective-permute-start | bytes 221192 | tf_op jit(solution)/shard_map/ppermute | solution.py:676
  2.9 6.5 %collective-permute-start.1 = (f32[9,16,128]{2,1,0:T(8,128)S(1)}, f32[9,16,128]{2,1,0:T(8,128)S(1)}, u32[]{:S(2)}, u32[]{:S(2)}) collective-permute-start(f32[9,16,128]{2,1,0:T(8,128)S(1)} %get-tuple-element.28), channel_id=1, source_target_pairs={{1,2},{3,4},{5,6},{7,8},{9,10},{11,12},{13,14},{15,0},{17,18},{19,... | collective-permute-start | bytes 221192 | tf_op jit(solution)/shard_map/ppermute | solution.py:676
  9.5 4.5 %copy-start.2 = (s32[8]{0:T(128)S(1)}, s32[8]{0:T(128)}, u32[]{:S(2)}) copy-start(s32[8]{0:T(128)} %refs_0_.3) | copy-start | bytes 100
  9.7 10.6 %collective-permute-start.3 = (f32[24,16,128]{2,1,0:T(8,128)S(1)}, f32[24,16,128]{2,1,0:T(8,128)S(1)}, u32[]{:S(2)}, u32[]{:S(2)}) collective-permute-start(f32[24,16,128]{2,1,0:T(8,128)S(1)} %get-tuple-element.33), channel_id=1, source_target_pairs={{16,32},{48,64},{80,96},{112,0},{17,33},{49,65},{81,97},{113,1},{1... | collective-permute-start | bytes 589832 | tf_op jit(solution)/shard_map/ppermute | solution.py:676
  13.3 8.1 %collective-permute-start.2 = (f32[24,16,128]{2,1,0:T(8,128)S(1)}, f32[24,16,128]{2,1,0:T(8,128)S(1)}, u32[]{:S(2)}, u32[]{:S(2)}) collective-permute-start(f32[24,16,128]{2,1,0:T(8,128)S(1)} %get-tuple-element.30.refs_7_), channel_id=1, source_target_pairs={{0,16},{32,48},{64,80},{96,112},{1,17},{33,49},{65,81},{97,113},{2... | collective-permute-start | bytes 589832 | tf_op jit(solution)/shard_map/ppermute | solution.py:676
  22.0 1.3 %collective-permute-start.4 = (f32[6,16,128]{2,1,0:T(8,128)S(1)}, f32[6,16,128]{2,1,0:T(8,128)S(1)}, u32[]{:S(2)}, u32[]{:S(2)}) collective-permute-start(f32[6,16,128]{2,1,0:T(8,128)S(1)} %get-tuple-element.38), channel_id=1, source_target_pairs={{0,1},{2,3},{4,5},{6,7},{8,9},{10,11},{12,13},{14,15},{16,17},{18,... | collective-permute-start | bytes 147464 | tf_op jit(solution)/shard_map/ppermute | solution.py:676
  23.6 12.0 %collective-permute-start.6 = (f32[12,16,128]{2,1,0:T(8,128)S(1)}, f32[12,16,128]{2,1,0:T(8,128)S(1)}, u32[]{:S(2)}, u32[]{:S(2)}) collective-permute-start(f32[12,16,128]{2,1,0:T(8,128)S(1)} %get-tuple-element.42), channel_id=1, source_target_pairs={{15,16},{16,15},{1,17},{30,14},{2,3},{3,2},{4,5},{5,4},{6,7},{7,6}... | collective-permute-start | bytes 294920 | tf_op jit(solution)/shard_map/ppermute | solution.py:690
  29.5 6.1 %collective-permute-start.5 = (f32[11,16,128]{2,1,0:T(8,128)S(1)}, f32[11,16,128]{2,1,0:T(8,128)S(1)}, u32[]{:S(2)}, u32[]{:S(2)}) collective-permute-start(f32[11,16,128]{2,1,0:T(8,128)S(1)} %join.1), channel_id=1, source_target_pairs={{1,2},{3,4},{5,6},{7,8},{9,10},{11,12},{13,14},{15,0},{17,18},{19,... | collective-permute-start | bytes 270344 | tf_op jit(solution)/shard_map/ppermute | solution.py:676
  35.9 1.4 %collective-permute-start.7 = (f32[11,16,128]{2,1,0:T(8,128)S(1)}, f32[11,16,128]{2,1,0:T(8,128)S(1)}, u32[]{:S(2)}, u32[]{:S(2)}) collective-permute-start(f32[11,16,128]{2,1,0:T(8,128)S(1)} %get-tuple-element.45), channel_id=1, source_target_pairs={{0,1},{2,3},{4,5},{6,7},{8,9},{10,11},{12,13},{14,15},{16,17},{18,... | collective-permute-start | bytes 270344 | tf_op jit(solution)/shard_map/ppermute | solution.py:676

commit v6 on v5

--- a/solution.py
+++ b/solution.py
@@ -46,11 +46,9 @@
     ix = lax.rem(lax.axis_index("bx") + (dx + count_x), count_x)
     iy = lax.rem(lax.axis_index("by") + (dy + count_y), count_y)
     base = (ix * count_y + iy) * blocks
-    block = lane_block(LANES // blocks)
-    value = jnp.full((ROWS, LANES), levels[base], jnp.int32)
-    for k in range(1, blocks):
-        value = jnp.where(block == k, levels[base + k], value)
-    return value
+    line = jnp.broadcast_to(levels[pl.ds(base // LANES, 1), :], (ROWS, LANES))
+    line = pltpu.roll(line, lax.rem(LANES - lax.rem(base, LANES), LANES), 1)
+    return jnp.take_along_axis(line, lane_block(LANES // blocks), axis=1)
 
 
 def lane_roll(tile, by):
@@ -175,27 +173,28 @@
         second[...] = up[...]
 
 
-def face_kernel(
-    shape, blocks, levels, f, marks, pay_a, pay_b, level, high, low, sems, up, down
-):
-    _, nx, ny, nz = f.shape
+def fetch_kernel(f, high, low, sems):
+    ny = f.shape[2]
     copies = [
-        pltpu.make_async_copy(levels, level, sems.at[0]),
-        pltpu.make_async_copy(f.at[:, :, ny - 1, :], high, sems.at[1]),
-        pltpu.make_async_copy(f.at[:, :, 0, :], low, sems.at[2]),
+        pltpu.make_async_copy(f.at[:, :, ny - 1, :], high, sems.at[0]),
+        pltpu.make_async_copy(f.at[:, :, 0, :], low, sems.at[1]),
     ]
     for copy in copies:
         copy.start()
-    copies[0].wait()
+    for copy in copies:
+        copy.wait()
+
+
+def face_kernel(shape, blocks, levels, high, low, marks, pay_a, pay_b, up, down):
+    nx = high.shape[1]
     for dx in (-1, 0, 1):
         for dy in (-1, 0, 1):
-            marks[dx + 1, dy + 1, :, :] = column_level(level, shape, blocks, dx, dy)
+            marks[dx + 1, dy + 1, :, :] = column_level(levels, shape, blocks, dx, dy)
     here = marks[1, 1, :, :]
     row = sublane()
-    for b, rows, pay, copy in ((1, high, up, copies[1]), (-1, low, down, copies[2])):
+    for b, rows, pay in ((1, high, up), (-1, low, down)):
         near = [marks[dx, b + 1, :, :] for dx in range(3)]
         plain = {e: level_factor(here, near[1], e) for e in (-1, 0, 1)}
-        copy.wait()
         for x in range(0, nx, ROWS):
 
             def get(c):
@@ -610,7 +609,7 @@
     pay_a[8:11, :, :] = got_w[0:3, :, :]
 
 
-def place_kernel(moves, rho, vel, away, got_a, got_b, got_w, rho_out, vel_out, block, crossed):
+def place_kernel(moves, rho, vel, away, got_a, got_b, got_w, rho_out, vel_out, block, crossed, made, sems):
     iy = lax.axis_index("by")
     odd = lax.rem(iy, 2)
     end = jnp.logical_or(iy == 0, iy == lax.axis_size("by") - 1)
@@ -647,18 +646,20 @@
                 block[2 * n + h, rows, :] *= inv
     near = row == moves[odd, :, :]
     far = row == moves[1 - odd, :, :]
-    for x in range(block.shape[1]):
-        for h in (0, 1):
-            lanes = slice((2 * x + h) * LANES, (2 * x + h + 1) * LANES)
-            for n in range(4):
+    copies = []
+    for n in range(4):
+        for x in range(block.shape[1]):
+            for h in (0, 1):
+                lanes = slice((2 * x + h) * LANES, (2 * x + h + 1) * LANES)
                 k = 2 * n + h
                 tile = rho[:, lanes] if n == 0 else vel[n - 1, :, lanes]
                 tile = jnp.where(near, got_a[k, x : x + 1, :], tile)
-                tile = jnp.where(far, block[k, x : x + 1, :], tile)
-                if n == 0:
-                    rho_out[:, lanes] = tile
-                else:
-                    vel_out[n - 1, :, lanes] = tile
+                made[n, :, lanes] = jnp.where(far, block[k, x : x + 1, :], tile)
+        target = rho_out if n == 0 else vel_out.at[n - 1]
+        copies.append(pltpu.make_async_copy(made.at[n], target, sems.at[n]))
+        copies[n].start()
+    for copy in copies:
+        copy.wait()
 
 
 def swap(value, axis, odd):
@@ -690,13 +691,13 @@
     return lax.ppermute(value, ("bx", "by"), pairs)
 
 
-def call(kernel, outs, specs, scratch, name, work, limit):
+def call(kernel, outs, specs, scratch, name, work, limit, kept):
     space = {"v": pltpu.VMEM, "s": pltpu.SMEM, "h": pltpu.HBM, "a": pl.ANY}
     return pl.pallas_call(
         kernel,
         out_shape=outs,
         in_specs=[pl.BlockSpec(memory_space=space[k]) for k in specs],
-        out_specs=[pl.BlockSpec(memory_space=pltpu.VMEM)] * len(outs),
+        out_specs=[pl.BlockSpec(memory_space=pltpu.VMEM if kept else pl.ANY)] * len(outs),
         scratch_shapes=scratch,
         compiler_params=pltpu.CompilerParams(vmem_limit_bytes=limit),
         cost_estimate=pl.CostEstimate(
@@ -722,21 +723,22 @@
     def room(*shapes):
         return [pltpu.VMEM(dims, jnp.float32) for dims in shapes]
 
-    def run(kernel, *args, outs, specs, scratch=(), work=1, limit=VMEM_BYTES):
+    def run(kernel, *args, outs, specs, scratch=(), work=1, limit=VMEM_BYTES, kept=True):
         def body(*refs):
             kernel(*refs)
 
-        return call(body, outs, specs, scratch, kernel.func.__name__[:-7], work, limit)(*args)
-
+        return call(body, outs, specs, scratch, kernel.func.__name__[:-7], work, limit, kept)(*args)
+
+    high, low = run(
+        functools.partial(fetch_kernel), populations,
+        outs=[real(27, nx, nz)] * 2, specs="h", scratch=[pltpu.SemaphoreType.DMA((2,))],
+        limit=FACE_BYTES,
+    )
     marks, pay_a, pay_b = run(
-        functools.partial(face_kernel, shape, blocks), block_level, populations,
+        functools.partial(face_kernel, shape, blocks),
+        block_level.reshape(block_level.shape[0] // nz, nz), high, low,
         outs=[whole(3, 3, *tile), real(*yface), real(*yface)],
-        specs="hh",
-        scratch=[pltpu.SMEM(block_level.shape, jnp.int32)]
-        + room((27, nx, nz), (27, nx, nz))
-        + [pltpu.SemaphoreType.DMA((3,))]
-        + room(yface, yface),
-        limit=FACE_BYTES,
+        specs="vvv", scratch=room(yface, yface),
     )
     ya, yb = swap(pay_a, "by", 0), swap(pay_b, "by", 1)
     table, g, calm = run(
@@ -794,7 +796,8 @@
     return tuple(
         run(
             functools.partial(place_kernel), moves, rho, vel, away, got_a, got_b, got_w,
-            outs=results, specs="vvvvvvv", scratch=room((8, nx, nz), yedge),
+            outs=results, specs="vvvvvvv", kept=False,
+            scratch=room((8, nx, nz), yedge, (4, blocks, cells)) + [pltpu.SemaphoreType.DMA((4,))],
         )
     )
 

time: 39.1 us -> 38.4 us (0.982)
  local copies, waits for them, and re-layouts: 0.84 us -> 0.01 us
    unnamed x6, local copies, waits for them, and re-layouts: 0.84 us -> 0.01 us
    pallas_call x10 -> x11, Pallas kernels: 12.6 us -> 12.7 us  [run(): call(body, outs, specs, scratch, kernel.func.__name__[:-7], work, limit,...]
where the time goes in v6:
time: 38.4 us; the launch traced here: 37.7 us
  starting transfers between devices  14.7 us (38%)
  Pallas kernels  12.7 us (33%)
  waiting for transfers between devices  9.5 us (25%)
  between operations  0.77 us (2%)
    pallas_call x11, Pallas kernels, run(): call(body, outs, specs, scratch, kernel.func.__name__[:-7], work, limit,...  12.7 us
    ppermute x7, waiting for transfers between devices, swap(): return lax.ppermute(value, ('bx', 'by'), pairs)  9.5 us
    ppermute x7, starting transfers between devices, swap(): return lax.ppermute(value, ('bx', 'by'), pairs)  8.8 us
    ppermute x1, starting transfers between devices, swap_ends(): return lax.ppermute(value, ('bx', 'by'), pairs)  5.92 us
  transfers between devices with their start and end apart: 8, of which 4 were waited for; matrix products, arithmetic and copies ran while one was open for 0% of the time, Pallas kernels for 23%

profile of v6, /device:TPU:16, one launch (start us, length us, event | category | flops | bytes accessed | tf_op | source)
XLA Modules:
  0.0 37.7 jit_solution(2903759112293825939)
XLA Ops:
  0.6 1.2 %fetch.1 = (f32[27,16,128]{2,1,0:T(8,128)S(1)}, f32[27,16,128]{2,1,0:T(8,128)S(1)}) custom-call(f32[27,16,16,128]{3,2,1,0:T(8,128)} %refs_1_.5), custom_call_target="tpu_custom_call" | custom-call | flops 2000000 | bytes 1000000 | tf_op jit(solution)/shard_map/fetch/pallas_call | solution.py:730
  1.9 0.3 face.1
  2.2 0.1 collective-permute-start
  2.3 4.2 %collective-permute-start.1 = (f32[9,16,128]{2,1,0:T(8,128)S(1)}, f32[9,16,128]{2,1,0:T(8,128)S(1)}, u32[]{:S(2)}, u32[]{:S(2)}) collective-permute-start(f32[9,16,128]{2,1,0:T(8,128)S(1)} %get-tuple-element.32), channel_id=1, source_target_pairs={{1,2},{3,4},{5,6},{7,8},{9,10},{11,12},{13,14},{15,0},{17,18},{19,... | collective-permute-start | bytes 221192 | tf_op jit(solution)/shard_map/ppermute | solution.py:677
  6.5 2.3 %first.1 = (f32[5,3,3,16,128]{4,3,2,1,0:T(8,128)S(1)}, f32[27,16,16,128]{3,2,1,0:T(8,128)S(1)}, f32[2,9,16,128]{3,2,1,0:T(8,128)S(1)}) custom-call(s32[3,3,8,128]{3,2,1,0:T(8,128)S(1)} %get-tuple-element.28.refs_0_.refs_1_, f32[27,16,16,128]{3,2,1,0:T(8,128)S(1)} %copy-done), custom_call_target="tpu_custom_call" | custom-call | flops 6000000 | bytes 3000000 | tf_op jit(solution)/shard_map/first/pallas_call | solution.py:730
  8.8 0.0 collective-permute-done.refs_4_.refs_5_
  8.8 0.0 copy-start.2
  8.9 0.2 side.1
  9.0 3.6 %collective-permute-start.3 = (f32[24,16,128]{2,1,0:T(8,128)S(1)}, f32[24,16,128]{2,1,0:T(8,128)S(1)}, u32[]{:S(2)}, u32[]{:S(2)}) collective-permute-start(f32[24,16,128]{2,1,0:T(8,128)S(1)} %get-tuple-element.37), channel_id=1, source_target_pairs={{16,32},{48,64},{80,96},{112,0},{17,33},{49,65},{81,97},{113,1},{1... | collective-permute-start | bytes 589832 | tf_op jit(solution)/shard_map/ppermute | solution.py:677
  12.6 0.8 %collective-permute-start.2 = (f32[24,16,128]{2,1,0:T(8,128)S(1)}, f32[24,16,128]{2,1,0:T(8,128)S(1)}, u32[]{:S(2)}, u32[]{:S(2)}) collective-permute-start(f32[24,16,128]{2,1,0:T(8,128)S(1)} %get-tuple-element.34.refs_7_), channel_id=1, source_target_pairs={{0,16},{32,48},{64,80},{96,112},{1,17},{33,49},{65,81},{97,113},{2... | collective-permute-start | bytes 589832 | tf_op jit(solution)/shard_map/ppermute | solution.py:677
  13.4 6.2 %inner.1 = (f32[3,3,2,16,16,128]{5,4,3,2,1,0:T(8,128)S(1)}, f32[8,128,128]{2,1,0:T(8,128)S(1)}, f32[3,16,128]{2,1,0:T(8,128)S(1)}, f32[3,16,128]{2,1,0:T(8,128)S(1)}, s32[4,8,128]{2,1,0:T(8,128)S(1)}) custom-call(s32[8]{0:T(128)S(1)} %copy-done.2, s32[3,3,8,128]{3,2,1,0:T(8,128)S(1)} %get-tuple-element.28.refs_0_.refs_1_, f32[27,16,16,128]{3,2,1,0:T(8,128)S(1)} %copy-done, ...), custom_call_target="tpu_custom_call" | custom-call | flops 20000000 | bytes 10000000 | tf_op jit(solution)/shard_map/inner/pallas_call | solution.py:730
  19.6 0.0 collective-permute-done.3.refs_7_
  19.6 1.1 %collective-permute-done.2.refs_6_ = f32[24,16,128]{2,1,0:T(8,128)S(1)} collective-permute-done((f32[24,16,128]{2,1,0:T(8,128)S(1)}, f32[24,16,128]{2,1,0:T(8,128)S(1)}, u32[]{:S(2)}, u32[]{:S(2)}) %collective-permute-start.2) | collective-permute-done | bytes 196640 | tf_op jit(solution)/shard_map/ppermute | solution.py:677
  20.7 0.6 %outer.1 = (f32[8,32,128]{2,1,0:T(8,128)S(1)}, f32[6,16,128]{2,1,0:T(8,128)S(1)}, f32[3,16,128]{2,1,0:T(8,128)S(1)}) custom-call(s32[3,3,8,128]{3,2,1,0:T(8,128)S(1)} %get-tuple-element.28.refs_0_.refs_1_, f32[27,16,16,128]{3,2,1,0:T(8,128)S(1)} %copy-done, f32[27,16,16,128]{3,2,1,0:T(8,128)S(1)} %get-tuple-element.29.refs_2_.refs_3_, ...), custom_call_target="tpu_custom_call" | custom-call | flops 2000000 | bytes 1000000 | tf_op jit(solution)/shard_map/outer/pallas_call | solution.py:730
  21.3 0.1 collective-permute-start.4
  21.4 0.2 turn.1.refs_2_
  21.6 1.0 %collective-permute-done.4.refs_3_ = f32[6,16,128]{2,1,0:T(8,128)S(1)} collective-permute-done((f32[6,16,128]{2,1,0:T(8,128)S(1)}, f32[6,16,128]{2,1,0:T(8,128)S(1)}, u32[]{:S(2)}, u32[]{:S(2)}) %collective-permute-start.4) | collective-permute-done | bytes 49184 | tf_op jit(solution)/shard_map/ppermute | solution.py:677
  22.6 0.2 pack.1
  22.9 5.9 %collective-permute-start.6 = (f32[12,16,128]{2,1,0:T(8,128)S(1)}, f32[12,16,128]{2,1,0:T(8,128)S(1)}, u32[]{:S(2)}, u32[]{:S(2)}) collective-permute-start(f32[12,16,128]{2,1,0:T(8,128)S(1)} %get-tuple-element.46), channel_id=1, source_target_pairs={{15,16},{16,15},{1,17},{30,14},{2,3},{3,2},{4,5},{5,4},{6,7},{7,6}... | collective-permute-start | bytes 294920 | tf_op jit(solution)/shard_map/ppermute | solution.py:691
  28.8 6.1 %collective-permute-done.5.refs_2_.refs_5_ = f32[11,16,128]{2,1,0:T(8,128)S(1)} collective-permute-done((f32[11,16,128]{2,1,0:T(8,128)S(1)}, f32[11,16,128]{2,1,0:T(8,128)S(1)}, u32[]{:S(2)}, u32[]{:S(2)}) %collective-permute-start.5) | collective-permute-done | bytes 90144 | tf_op jit(solution)/shard_map/ppermute | solution.py:677
  34.9 0.3 moments.1
  35.2 0.1 collective-permute-start.7
  35.3 1.3 %collective-permute-done.7.refs_4_ = f32[11,16,128]{2,1,0:T(8,128)S(1)} collective-permute-done((f32[11,16,128]{2,1,0:T(8,128)S(1)}, f32[11,16,128]{2,1,0:T(8,128)S(1)}, u32[]{:S(2)}, u32[]{:S(2)}) %collective-permute-start.7) | collective-permute-done | bytes 90144 | tf_op jit(solution)/shard_map/ppermute | solution.py:677
  36.6 1.1 %place.1 = (f32[8,4096]{1,0:T(8,128)}, f32[3,8,4096]{2,1,0:T(8,128)}) custom-call(s32[4,8,128]{2,1,0:T(8,128)S(1)} %get-tuple-element.35.refs_0_, f32[8,4096]{1,0:T(8,128)S(1)} %get-tuple-element.47.refs_1_, f32[3,8,4096]{2,1,0:T(8,128)S(1)} %get-tuple-element.48.refs_2_, f32[3,16,128]{2,1,0:T(8,128)S(1)} %get-tuple-element.44.refs_0_.refs_3_, ...), custom_call_target="tpu_custom_call" | custom-call | flops 2000000 | bytes 1000000 | tf_op jit(solution)/shard_map/place/pallas_call | solution.py:730
  (9 shorter events, 0.0 us)
Async XLA Ops:
  0.6 5.9 %copy-start = (f32[27,16,16,128]{3,2,1,0:T(8,128)S(1)}, f32[27,16,16,128]{3,2,1,0:T(8,128)}, u32[]{:S(2)}) copy-start(f32[27,16,16,128]{3,2,1,0:T(8,128)} %refs_1_.5) | copy-start | bytes 10616836
  0.6 1.3 %copy-start.1 = (s32[1024]{0:T(1024)S(1)}, s32[1024]{0:T(1024)}, u32[]{:S(2)}) copy-start(s32[1024]{0:T(1024)} %param.4) | copy-start | bytes 12292
  2.2 6.6 %collective-permute-start = (f32[9,16,128]{2,1,0:T(8,128)S(1)}, f32[9,16,128]{2,1,0:T(8,128)S(1)}, u32[]{:S(2)}, u32[]{:S(2)}) collective-permute-start(f32[9,16,128]{2,1,0:T(8,128)S(1)} %get-tuple-element.31), channel_id=1, source_target_pairs={{0,1},{2,3},{4,5},{6,7},{8,9},{10,11},{12,13},{14,15},{16,17},{18,... | collective-permute-start | bytes 221192 | tf_op jit(solution)/shard_map/ppermute | solution.py:677
  2.3 6.5 %collective-permute-start.1 = (f32[9,16,128]{2,1,0:T(8,128)S(1)}, f32[9,16,128]{2,1,0:T(8,128)S(1)}, u32[]{:S(2)}, u32[]{:S(2)}) collective-permute-start(f32[9,16,128]{2,1,0:T(8,128)S(1)} %get-tuple-element.32), channel_id=1, source_target_pairs={{1,2},{3,4},{5,6},{7,8},{9,10},{11,12},{13,14},{15,0},{17,18},{19,... | collective-permute-start | bytes 221192 | tf_op jit(solution)/shard_map/ppermute | solution.py:677
  8.8 4.5 %copy-start.2 = (s32[8]{0:T(128)S(1)}, s32[8]{0:T(128)}, u32[]{:S(2)}) copy-start(s32[8]{0:T(128)} %refs_0_.3) | copy-start | bytes 100
  9.0 10.6 %collective-permute-start.3 = (f32[24,16,128]{2,1,0:T(8,128)S(1)}, f32[24,16,128]{2,1,0:T(8,128)S(1)}, u32[]{:S(2)}, u32[]{:S(2)}) collective-permute-start(f32[24,16,128]{2,1,0:T(8,128)S(1)} %get-tuple-element.37), channel_id=1, source_target_pairs={{16,32},{48,64},{80,96},{112,0},{17,33},{49,65},{81,97},{113,1},{1... | collective-permute-start | bytes 589832 | tf_op jit(solution)/shard_map/ppermute | solution.py:677
  12.6 8.1 %collective-permute-start.2 = (f32[24,16,128]{2,1,0:T(8,128)S(1)}, f32[24,16,128]{2,1,0:T(8,128)S(1)}, u32[]{:S(2)}, u32[]{:S(2)}) collective-permute-start(f32[24,16,128]{2,1,0:T(8,128)S(1)} %get-tuple-element.34.refs_7_), channel_id=1, source_target_pairs={{0,16},{32,48},{64,80},{96,112},{1,17},{33,49},{65,81},{97,113},{2... | collective-permute-start | bytes 589832 | tf_op jit(solution)/shard_map/ppermute | solution.py:677
  21.3 1.3 %collective-permute-start.4 = (f32[6,16,128]{2,1,0:T(8,128)S(1)}, f32[6,16,128]{2,1,0:T(8,128)S(1)}, u32[]{:S(2)}, u32[]{:S(2)}) collective-permute-start(f32[6,16,128]{2,1,0:T(8,128)S(1)} %get-tuple-element.42), channel_id=1, source_target_pairs={{0,1},{2,3},{4,5},{6,7},{8,9},{10,11},{12,13},{14,15},{16,17},{18,... | collective-permute-start | bytes 147464 | tf_op jit(solution)/shard_map/ppermute | solution.py:677
  22.9 12.0 %collective-permute-start.6 = (f32[12,16,128]{2,1,0:T(8,128)S(1)}, f32[12,16,128]{2,1,0:T(8,128)S(1)}, u32[]{:S(2)}, u32[]{:S(2)}) collective-permute-start(f32[12,16,128]{2,1,0:T(8,128)S(1)} %get-tuple-element.46), channel_id=1, source_target_pairs={{15,16},{16,15},{1,17},{30,14},{2,3},{3,2},{4,5},{5,4},{6,7},{7,6}... | collective-permute-start | bytes 294920 | tf_op jit(solution)/shard_map/ppermute | solution.py:691
  28.8 6.1 %collective-permute-start.5 = (f32[11,16,128]{2,1,0:T(8,128)S(1)}, f32[11,16,128]{2,1,0:T(8,128)S(1)}, u32[]{:S(2)}, u32[]{:S(2)}) collective-permute-start(f32[11,16,128]{2,1,0:T(8,128)S(1)} %join.1), channel_id=1, source_target_pairs={{1,2},{3,4},{5,6},{7,8},{9,10},{11,12},{13,14},{15,0},{17,18},{19,... | collective-permute-start | bytes 270344 | tf_op jit(solution)/shard_map/ppermute | solution.py:677
  35.2 1.4 %collective-permute-start.7 = (f32[11,16,128]{2,1,0:T(8,128)S(1)}, f32[11,16,128]{2,1,0:T(8,128)S(1)}, u32[]{:S(2)}, u32[]{:S(2)}) collective-permute-start(f32[11,16,128]{2,1,0:T(8,128)S(1)} %get-tuple-element.49), channel_id=1, source_target_pairs={{0,1},{2,3},{4,5},{6,7},{8,9},{10,11},{12,13},{14,15},{16,17},{18,... | collective-permute-start | bytes 270344 | tf_op jit(solution)/shard_map/ppermute | solution.py:677

commit v7 on v6

--- a/solution.py
+++ b/solution.py
@@ -316,7 +316,7 @@
                     pay[9 + j, rows, :] = jnp.where(fine, moved, calm[n, j, rows, :])
             for m, part in enumerate(group_sums(flat)):
                 pay[18 + m, rows, :] = part
-    store_by_parity(lax.rem(lax.axis_index("bx"), 2), pay_a, pay_b, up, down)
+    store_by_parity(lax.rem(lax.axis_index("bx"), 2), pay_a.at[pl.ds(0, 24)], pay_b, up, down)
 
 
 def second_collide(groups, get, fine, factor, put, dirs, known=None):
@@ -443,7 +443,7 @@
     part, pay, away, above, below, right, left, state, ends, up, down,
 ):
     load_by_parity(lax.rem(lax.axis_index("by"), 2), ya, yb, above, below)
-    load_by_parity(lax.rem(lax.axis_index("bx"), 2), xa, xb, right, left)
+    load_by_parity(lax.rem(lax.axis_index("bx"), 2), xa.at[pl.ds(0, 24)], xb, right, left)
     fine = {dx: marks[dx + 1, 1, :, :] == 1 for dx in (-1, 0, 1)}
     row = sublane()
     reflect, turn = turns()
@@ -748,7 +748,7 @@
     )
     pay_a, pay_b = run(
         functools.partial(side_kernel), marks, populations, g, calm, ya, yb,
-        outs=[real(*xface)] * 2, specs="vvvvvv", scratch=room(yface, yface, xface, xface),
+        outs=[real(25, ny, nz), real(*xface)], specs="vvvvvv", scratch=room(yface, yface, xface, xface),
     )
     xa, xb = swap(pay_a, "bx", 0), swap(pay_b, "bx", 1)
     sums, inner, up, down, moves = run(

time: 38.4 us -> 37.5 us (0.977)
  starting transfers between devices: 14.7 us -> 13 us
  waiting for transfers between devices: 9.5 us -> 10.2 us
    ppermute x1, starting transfers between devices: 5.92 us -> 4.88 us  [swap_ends(): return lax.ppermute(value, ('bx', 'by'), pairs)]
    ppermute x7, waiting for transfers between devices: 9.5 us -> 10.2 us  [swap(): return lax.ppermute(value, ('bx', 'by'), pairs)]
    ppermute x7, starting transfers between devices: 8.8 us -> 8.14 us  [swap(): return lax.ppermute(value, ('bx', 'by'), pairs)]
  transfers between devices with their start and end apart: 8 -> 8, of which waited for: 4 -> 4; matrix products, arithmetic and copies ran while one was open for 0% -> 0% of each run, Pallas kernels for 23% -> 24%
where the time goes in v7:
time: 37.5 us; the launch traced here: 36.7 us
  starting transfers between devices  13 us (35%)
  Pallas kernels  12.7 us (34%)
  waiting for transfers between devices  10.2 us (27%)
  between operations  0.77 us (2%)
    pallas_call x11, Pallas kernels, run(): call(body, outs, specs, scratch, kernel.func.__name__[:-7], work, limit,...  12.7 us
    ppermute x7, waiting for transfers between devices, swap(): return lax.ppermute(value, ('bx', 'by'), pairs)  10.2 us
    ppermute x7, starting transfers between devices, swap(): return lax.ppermute(value, ('bx', 'by'), pairs)  8.14 us
    ppermute x1, starting transfers between devices, swap_ends(): return lax.ppermute(value, ('bx', 'by'), pairs)  4.88 us
  transfers between devices with their start and end apart: 8, of which 4 were waited for; matrix products, arithmetic and copies ran while one was open for 0% of the time, Pallas kernels for 24%

profile of v7, /device:TPU:16, one launch (start us, length us, event | category | flops | bytes accessed | tf_op | source)
XLA Modules:
  0.0 36.7 jit_solution(5180557566173366851)
XLA Ops:
  0.6 1.2 %fetch.1 = (f32[27,16,128]{2,1,0:T(8,128)S(1)}, f32[27,16,128]{2,1,0:T(8,128)S(1)}) custom-call(f32[27,16,16,128]{3,2,1,0:T(8,128)} %refs_1_.5), custom_call_target="tpu_custom_call" | custom-call | flops 2000000 | bytes 1000000 | tf_op jit(solution)/shard_map/fetch/pallas_call | solution.py:730
  1.9 0.3 face.1
  2.2 0.1 collective-permute-start
  2.3 4.2 %collective-permute-start.1 = (f32[9,16,128]{2,1,0:T(8,128)S(1)}, f32[9,16,128]{2,1,0:T(8,128)S(1)}, u32[]{:S(2)}, u32[]{:S(2)}) collective-permute-start(f32[9,16,128]{2,1,0:T(8,128)S(1)} %get-tuple-element.32), channel_id=1, source_target_pairs={{1,2},{3,4},{5,6},{7,8},{9,10},{11,12},{13,14},{15,0},{17,18},{19,... | collective-permute-start | bytes 221192 | tf_op jit(solution)/shard_map/ppermute | solution.py:677
  6.5 2.3 %first.1 = (f32[5,3,3,16,128]{4,3,2,1,0:T(8,128)S(1)}, f32[27,16,16,128]{3,2,1,0:T(8,128)S(1)}, f32[2,9,16,128]{3,2,1,0:T(8,128)S(1)}) custom-call(s32[3,3,8,128]{3,2,1,0:T(8,128)S(1)} %get-tuple-element.28.refs_0_.refs_1_, f32[27,16,16,128]{3,2,1,0:T(8,128)S(1)} %copy-done), custom_call_target="tpu_custom_call" | custom-call | flops 6000000 | bytes 3000000 | tf_op jit(solution)/shard_map/first/pallas_call | solution.py:730
  8.8 0.0 collective-permute-done.refs_4_.refs_5_
  8.8 0.0 copy-start.2
  8.9 0.2 side.1
  9.0 3.7 %collective-permute-start.2 = (f32[25,16,128]{2,1,0:T(8,128)S(1)}, f32[25,16,128]{2,1,0:T(8,128)S(1)}, u32[]{:S(2)}, u32[]{:S(2)}) collective-permute-start(f32[25,16,128]{2,1,0:T(8,128)S(1)} %get-tuple-element.34.refs_7_), channel_id=1, source_target_pairs={{0,16},{32,48},{64,80},{96,112},{1,17},{33,49},{65,81},{97,113},{2... | collective-permute-start | bytes 614408 | tf_op jit(solution)/shard_map/ppermute | solution.py:677
  12.7 0.0 collective-permute-start.3
  12.7 6.2 %inner.1 = (f32[3,3,2,16,16,128]{5,4,3,2,1,0:T(8,128)S(1)}, f32[8,128,128]{2,1,0:T(8,128)S(1)}, f32[3,16,128]{2,1,0:T(8,128)S(1)}, f32[3,16,128]{2,1,0:T(8,128)S(1)}, s32[4,8,128]{2,1,0:T(8,128)S(1)}) custom-call(s32[8]{0:T(128)S(1)} %copy-done.2, s32[3,3,8,128]{3,2,1,0:T(8,128)S(1)} %get-tuple-element.28.refs_0_.refs_1_, f32[27,16,16,128]{3,2,1,0:T(8,128)S(1)} %copy-done, ...), custom_call_target="tpu_custom_call" | custom-call | flops 20000000 | bytes 10000000 | tf_op jit(solution)/shard_map/inner/pallas_call | solution.py:730
  18.9 1.8 %collective-permute-done.3.refs_7_ = f32[24,16,128]{2,1,0:T(8,128)S(1)} collective-permute-done((f32[24,16,128]{2,1,0:T(8,128)S(1)}, f32[24,16,128]{2,1,0:T(8,128)S(1)}, u32[]{:S(2)}, u32[]{:S(2)}) %collective-permute-start.3) | collective-permute-done | bytes 196640 | tf_op jit(solution)/shard_map/ppermute | solution.py:677
  20.8 0.0 collective-permute-done.2.refs_6_
  20.8 0.6 %outer.1 = (f32[8,32,128]{2,1,0:T(8,128)S(1)}, f32[6,16,128]{2,1,0:T(8,128)S(1)}, f32[3,16,128]{2,1,0:T(8,128)S(1)}) custom-call(s32[3,3,8,128]{3,2,1,0:T(8,128)S(1)} %get-tuple-element.28.refs_0_.refs_1_, f32[27,16,16,128]{3,2,1,0:T(8,128)S(1)} %copy-done, f32[27,16,16,128]{3,2,1,0:T(8,128)S(1)} %get-tuple-element.29.refs_2_.refs_3_, ...), custom_call_target="tpu_custom_call" | custom-call | flops 2000000 | bytes 1000000 | tf_op jit(solution)/shard_map/outer/pallas_call | solution.py:730
  21.4 0.1 collective-permute-start.4
  21.5 0.2 turn.1.refs_2_
  21.7 1.0 %collective-permute-done.4.refs_3_ = f32[6,16,128]{2,1,0:T(8,128)S(1)} collective-permute-done((f32[6,16,128]{2,1,0:T(8,128)S(1)}, f32[6,16,128]{2,1,0:T(8,128)S(1)}, u32[]{:S(2)}, u32[]{:S(2)}) %collective-permute-start.4) | collective-permute-done | bytes 49184 | tf_op jit(solution)/shard_map/ppermute | solution.py:677
  22.7 0.2 pack.1
  23.0 4.9 %collective-permute-start.6 = (f32[12,16,128]{2,1,0:T(8,128)S(1)}, f32[12,16,128]{2,1,0:T(8,128)S(1)}, u32[]{:S(2)}, u32[]{:S(2)}) collective-permute-start(f32[12,16,128]{2,1,0:T(8,128)S(1)} %get-tuple-element.46), channel_id=1, source_target_pairs={{15,16},{16,15},{1,17},{30,14},{2,3},{3,2},{4,5},{5,4},{6,7},{7,6}... | collective-permute-start | bytes 294920 | tf_op jit(solution)/shard_map/ppermute | solution.py:691
  27.9 6.1 %collective-permute-done.5.refs_2_.refs_5_ = f32[11,16,128]{2,1,0:T(8,128)S(1)} collective-permute-done((f32[11,16,128]{2,1,0:T(8,128)S(1)}, f32[11,16,128]{2,1,0:T(8,128)S(1)}, u32[]{:S(2)}, u32[]{:S(2)}) %collective-permute-start.5) | collective-permute-done | bytes 90144 | tf_op jit(solution)/shard_map/ppermute | solution.py:677
  33.9 0.3 moments.1
  34.2 0.1 collective-permute-start.7
  34.3 1.3 %collective-permute-done.7.refs_4_ = f32[11,16,128]{2,1,0:T(8,128)S(1)} collective-permute-done((f32[11,16,128]{2,1,0:T(8,128)S(1)}, f32[11,16,128]{2,1,0:T(8,128)S(1)}, u32[]{:S(2)}, u32[]{:S(2)}) %collective-permute-start.7) | collective-permute-done | bytes 90144 | tf_op jit(solution)/shard_map/ppermute | solution.py:677
  35.6 1.1 %place.1 = (f32[8,4096]{1,0:T(8,128)}, f32[3,8,4096]{2,1,0:T(8,128)}) custom-call(s32[4,8,128]{2,1,0:T(8,128)S(1)} %get-tuple-element.35.refs_0_, f32[8,4096]{1,0:T(8,128)S(1)} %get-tuple-element.47.refs_1_, f32[3,8,4096]{2,1,0:T(8,128)S(1)} %get-tuple-element.48.refs_2_, f32[3,16,128]{2,1,0:T(8,128)S(1)} %get-tuple-element.44.refs_0_.refs_3_, ...), custom_call_target="tpu_custom_call" | custom-call | flops 2000000 | bytes 1000000 | tf_op jit(solution)/shard_map/place/pallas_call | solution.py:730
  (9 shorter events, 0.0 us)
Async XLA Ops:
  0.6 5.9 %copy-start = (f32[27,16,16,128]{3,2,1,0:T(8,128)S(1)}, f32[27,16,16,128]{3,2,1,0:T(8,128)}, u32[]{:S(2)}) copy-start(f32[27,16,16,128]{3,2,1,0:T(8,128)} %refs_1_.5) | copy-start | bytes 10616836
  0.6 1.3 %copy-start.1 = (s32[1024]{0:T(1024)S(1)}, s32[1024]{0:T(1024)}, u32[]{:S(2)}) copy-start(s32[1024]{0:T(1024)} %param.4) | copy-start | bytes 12292
  2.2 6.6 %collective-permute-start = (f32[9,16,128]{2,1,0:T(8,128)S(1)}, f32[9,16,128]{2,1,0:T(8,128)S(1)}, u32[]{:S(2)}, u32[]{:S(2)}) collective-permute-start(f32[9,16,128]{2,1,0:T(8,128)S(1)} %get-tuple-element.31), channel_id=1, source_target_pairs={{0,1},{2,3},{4,5},{6,7},{8,9},{10,11},{12,13},{14,15},{16,17},{18,... | collective-permute-start | bytes 221192 | tf_op jit(solution)/shard_map/ppermute | solution.py:677
  2.3 6.5 %collective-permute-start.1 = (f32[9,16,128]{2,1,0:T(8,128)S(1)}, f32[9,16,128]{2,1,0:T(8,128)S(1)}, u32[]{:S(2)}, u32[]{:S(2)}) collective-permute-start(f32[9,16,128]{2,1,0:T(8,128)S(1)} %get-tuple-element.32), channel_id=1, source_target_pairs={{1,2},{3,4},{5,6},{7,8},{9,10},{11,12},{13,14},{15,0},{17,18},{19,... | collective-permute-start | bytes 221192 | tf_op jit(solution)/shard_map/ppermute | solution.py:677
  8.8 3.9 %copy-start.2 = (s32[8]{0:T(128)S(1)}, s32[8]{0:T(128)}, u32[]{:S(2)}) copy-start(s32[8]{0:T(128)} %refs_0_.3) | copy-start | bytes 100
  9.0 11.7 %collective-permute-start.2 = (f32[25,16,128]{2,1,0:T(8,128)S(1)}, f32[25,16,128]{2,1,0:T(8,128)S(1)}, u32[]{:S(2)}, u32[]{:S(2)}) collective-permute-start(f32[25,16,128]{2,1,0:T(8,128)S(1)} %get-tuple-element.34.refs_7_), channel_id=1, source_target_pairs={{0,16},{32,48},{64,80},{96,112},{1,17},{33,49},{65,81},{97,113},{2... | collective-permute-start | bytes 614408 | tf_op jit(solution)/shard_map/ppermute | solution.py:677
  12.7 8.1 %collective-permute-start.3 = (f32[24,16,128]{2,1,0:T(8,128)S(1)}, f32[24,16,128]{2,1,0:T(8,128)S(1)}, u32[]{:S(2)}, u32[]{:S(2)}) collective-permute-start(f32[24,16,128]{2,1,0:T(8,128)S(1)} %get-tuple-element.37), channel_id=1, source_target_pairs={{16,32},{48,64},{80,96},{112,0},{17,33},{49,65},{81,97},{113,1},{1... | collective-permute-start | bytes 589832 | tf_op jit(solution)/shard_map/ppermute | solution.py:677
  21.4 1.3 %collective-permute-start.4 = (f32[6,16,128]{2,1,0:T(8,128)S(1)}, f32[6,16,128]{2,1,0:T(8,128)S(1)}, u32[]{:S(2)}, u32[]{:S(2)}) collective-permute-start(f32[6,16,128]{2,1,0:T(8,128)S(1)} %get-tuple-element.42), channel_id=1, source_target_pairs={{0,1},{2,3},{4,5},{6,7},{8,9},{10,11},{12,13},{14,15},{16,17},{18,... | collective-permute-start | bytes 147464 | tf_op jit(solution)/shard_map/ppermute | solution.py:677
  23.0 11.0 %collective-permute-start.6 = (f32[12,16,128]{2,1,0:T(8,128)S(1)}, f32[12,16,128]{2,1,0:T(8,128)S(1)}, u32[]{:S(2)}, u32[]{:S(2)}) collective-permute-start(f32[12,16,128]{2,1,0:T(8,128)S(1)} %get-tuple-element.46), channel_id=1, source_target_pairs={{15,16},{16,15},{1,17},{30,14},{2,3},{3,2},{4,5},{5,4},{6,7},{7,6}... | collective-permute-start | bytes 294920 | tf_op jit(solution)/shard_map/ppermute | solution.py:691
  27.8 6.1 %collective-permute-start.5 = (f32[11,16,128]{2,1,0:T(8,128)S(1)}, f32[11,16,128]{2,1,0:T(8,128)S(1)}, u32[]{:S(2)}, u32[]{:S(2)}) collective-permute-start(f32[11,16,128]{2,1,0:T(8,128)S(1)} %join.1), channel_id=1, source_target_pairs={{1,2},{3,4},{5,6},{7,8},{9,10},{11,12},{13,14},{15,0},{17,18},{19,... | collective-permute-start | bytes 270344 | tf_op jit(solution)/shard_map/ppermute | solution.py:677
  34.2 1.4 %collective-permute-start.7 = (f32[11,16,128]{2,1,0:T(8,128)S(1)}, f32[11,16,128]{2,1,0:T(8,128)S(1)}, u32[]{:S(2)}, u32[]{:S(2)}) collective-permute-start(f32[11,16,128]{2,1,0:T(8,128)S(1)} %get-tuple-element.49), channel_id=1, source_target_pairs={{0,1},{2,3},{4,5},{6,7},{8,9},{10,11},{12,13},{14,15},{16,17},{18,... | collective-permute-start | bytes 270344 | tf_op jit(solution)/shard_map/ppermute | solution.py:677

commit v8 on v7

--- a/solution.py
+++ b/solution.py
@@ -566,13 +566,14 @@
 def pack_kernel(moves, inner, outer, got, made, block, pay_w):
     iy = lax.axis_index("by")
     odd = lax.rem(iy, 2)
+    which = number(moves[1 - odd, :, :])
     nx = got.shape[1]
     low, high = ROWS * 2, ROWS * (nx - 2)
     made[:, 0:low, :] = outer[:, 0:low, :]
     made[:, low:high, :] = inner[:, low:high, :]
     made[:, high:, :] = outer[:, low:, :]
     add_crossed(made, got, 1 - odd)
-    pack_block(made, block, 0, number(moves[1 - odd, :, :]))
+    pack_block(made, block, 0, which)
     end = jnp.logical_or(iy == 0, iy == lax.axis_size("by") - 1)
 
     @pl.when(end)
@@ -592,6 +593,7 @@
 def moments_kernel(moves, part, got_b, got_w, rho_out, vel_out, pay_a, made):
     odd = lax.rem(lax.axis_index("by"), 2)
     nx = got_b.shape[1]
+    which = number(moves[odd, :, :])
     made[...] = part[...]
     add_crossed(made, got_b, odd)
     for x in range(nx):
@@ -605,7 +607,7 @@
                 tile = made[2 * n + h, rows, :] * inv
                 made[2 * n + h, rows, :] = tile
                 vel_out[n - 1, :, lanes] = tile
-    pack_block(made, pay_a, 0, number(moves[odd, :, :]))
+    pack_block(made, pay_a, 0, which)
     pay_a[8:11, :, :] = got_w[0:3, :, :]
 
 
@@ -630,12 +632,12 @@
     sign = jnp.where(top == 1, -1.0, 1.0)
     mask = lane_block(width) == top * (ROWS - 1)
     spread = row * width + (lane_block(1) & (width - 1))
-    theirs = number(moves[3 - odd, :, :])
+    theirs = jnp.maximum(moves[3 - odd, :, :], 0)
     for first in range(0, block.shape[1], ROWS):
         rows = slice(first, first + ROWS)
         extra = []
         for n in range(3):
-            line = jnp.broadcast_to(crossed[n, pl.ds(first + theirs, 1), :], (ROWS, LANES))
+            line = jnp.take_along_axis(crossed[n, rows, :], theirs, axis=0)
             extra.append(jnp.where(mask, jnp.take_along_axis(line, spread, axis=1), 0.0))
         total, cross, along = extra
         for n, more in enumerate((total, cross, sign * total, along)):

time: 37.5 us -> 37.3 us (level)
  no operation moved by 1% of the time
where the time goes in v8:
time: 37.3 us; the launch traced here: 36.5 us
  starting transfers between devices  13 us (35%)
  Pallas kernels  12.5 us (34%)
  waiting for transfers between devices  10.2 us (27%)
  between operations  0.77 us (2%)
    pallas_call x11, Pallas kernels, run(): call(body, outs, specs, scratch, kernel.func.__name__[:-7], work, limit,...  12.5 us
    ppermute x7, waiting for transfers between devices, swap(): return lax.ppermute(value, ('bx', 'by'), pairs)  10.2 us
    ppermute x7, starting transfers between devices, swap(): return lax.ppermute(value, ('bx', 'by'), pairs)  8.14 us
    ppermute x1, starting transfers between devices, swap_ends(): return lax.ppermute(value, ('bx', 'by'), pairs)  4.88 us
  transfers between devices with their start and end apart: 8, of which 4 were waited for; matrix products, arithmetic and copies ran while one was open for 0% of the time, Pallas kernels for 24%

profile of v8, /device:TPU:16, one launch (start us, length us, event | category | flops | bytes accessed | tf_op | source)
XLA Modules:
  0.0 36.5 jit_solution(13636705655345948120)
XLA Ops:
  0.6 1.2 %fetch.1 = (f32[27,16,128]{2,1,0:T(8,128)S(1)}, f32[27,16,128]{2,1,0:T(8,128)S(1)}) custom-call(f32[27,16,16,128]{3,2,1,0:T(8,128)} %refs_1_.5), custom_call_target="tpu_custom_call" | custom-call | flops 2000000 | bytes 1000000 | tf_op jit(solution)/shard_map/fetch/pallas_call | solution.py:732
  1.9 0.3 face.1
  2.2 0.1 collective-permute-start
  2.3 4.2 %collective-permute-start.1 = (f32[9,16,128]{2,1,0:T(8,128)S(1)}, f32[9,16,128]{2,1,0:T(8,128)S(1)}, u32[]{:S(2)}, u32[]{:S(2)}) collective-permute-start(f32[9,16,128]{2,1,0:T(8,128)S(1)} %get-tuple-element.32), channel_id=1, source_target_pairs={{1,2},{3,4},{5,6},{7,8},{9,10},{11,12},{13,14},{15,0},{17,18},{19,... | collective-permute-start | bytes 221192 | tf_op jit(solution)/shard_map/ppermute | solution.py:679
  6.5 2.3 %first.1 = (f32[5,3,3,16,128]{4,3,2,1,0:T(8,128)S(1)}, f32[27,16,16,128]{3,2,1,0:T(8,128)S(1)}, f32[2,9,16,128]{3,2,1,0:T(8,128)S(1)}) custom-call(s32[3,3,8,128]{3,2,1,0:T(8,128)S(1)} %get-tuple-element.28.refs_0_.refs_1_, f32[27,16,16,128]{3,2,1,0:T(8,128)S(1)} %copy-done), custom_call_target="tpu_custom_call" | custom-call | flops 6000000 | bytes 3000000 | tf_op jit(solution)/shard_map/first/pallas_call | solution.py:732
  8.8 0.0 collective-permute-done.refs_4_.refs_5_
  8.8 0.0 copy-start.2
  8.9 0.2 side.1
  9.0 3.7 %collective-permute-start.2 = (f32[25,16,128]{2,1,0:T(8,128)S(1)}, f32[25,16,128]{2,1,0:T(8,128)S(1)}, u32[]{:S(2)}, u32[]{:S(2)}) collective-permute-start(f32[25,16,128]{2,1,0:T(8,128)S(1)} %get-tuple-element.34.refs_7_), channel_id=1, source_target_pairs={{0,16},{32,48},{64,80},{96,112},{1,17},{33,49},{65,81},{97,113},{2... | collective-permute-start | bytes 614408 | tf_op jit(solution)/shard_map/ppermute | solution.py:679
  12.7 0.0 collective-permute-start.3
  12.7 6.2 %inner.1 = (f32[3,3,2,16,16,128]{5,4,3,2,1,0:T(8,128)S(1)}, f32[8,128,128]{2,1,0:T(8,128)S(1)}, f32[3,16,128]{2,1,0:T(8,128)S(1)}, f32[3,16,128]{2,1,0:T(8,128)S(1)}, s32[4,8,128]{2,1,0:T(8,128)S(1)}) custom-call(s32[8]{0:T(128)S(1)} %copy-done.2, s32[3,3,8,128]{3,2,1,0:T(8,128)S(1)} %get-tuple-element.28.refs_0_.refs_1_, f32[27,16,16,128]{3,2,1,0:T(8,128)S(1)} %copy-done, ...), custom_call_target="tpu_custom_call" | custom-call | flops 20000000 | bytes 10000000 | tf_op jit(solution)/shard_map/inner/pallas_call | solution.py:732
  18.9 1.8 %collective-permute-done.3.refs_7_ = f32[24,16,128]{2,1,0:T(8,128)S(1)} collective-permute-done((f32[24,16,128]{2,1,0:T(8,128)S(1)}, f32[24,16,128]{2,1,0:T(8,128)S(1)}, u32[]{:S(2)}, u32[]{:S(2)}) %collective-permute-start.3) | collective-permute-done | bytes 196640 | tf_op jit(solution)/shard_map/ppermute | solution.py:679
  20.8 0.0 collective-permute-done.2.refs_6_
  20.8 0.6 %outer.1 = (f32[8,32,128]{2,1,0:T(8,128)S(1)}, f32[6,16,128]{2,1,0:T(8,128)S(1)}, f32[3,16,128]{2,1,0:T(8,128)S(1)}) custom-call(s32[3,3,8,128]{3,2,1,0:T(8,128)S(1)} %get-tuple-element.28.refs_0_.refs_1_, f32[27,16,16,128]{3,2,1,0:T(8,128)S(1)} %copy-done, f32[27,16,16,128]{3,2,1,0:T(8,128)S(1)} %get-tuple-element.29.refs_2_.refs_3_, ...), custom_call_target="tpu_custom_call" | custom-call | flops 2000000 | bytes 1000000 | tf_op jit(solution)/shard_map/outer/pallas_call | solution.py:732
  21.4 0.1 collective-permute-start.4
  21.5 0.2 turn.1.refs_2_
  21.7 1.0 %collective-permute-done.4.refs_3_ = f32[6,16,128]{2,1,0:T(8,128)S(1)} collective-permute-done((f32[6,16,128]{2,1,0:T(8,128)S(1)}, f32[6,16,128]{2,1,0:T(8,128)S(1)}, u32[]{:S(2)}, u32[]{:S(2)}) %collective-permute-start.4) | collective-permute-done | bytes 49184 | tf_op jit(solution)/shard_map/ppermute | solution.py:679
  22.7 0.2 pack.1
  23.0 4.9 %collective-permute-start.6 = (f32[12,16,128]{2,1,0:T(8,128)S(1)}, f32[12,16,128]{2,1,0:T(8,128)S(1)}, u32[]{:S(2)}, u32[]{:S(2)}) collective-permute-start(f32[12,16,128]{2,1,0:T(8,128)S(1)} %get-tuple-element.46), channel_id=1, source_target_pairs={{15,16},{16,15},{1,17},{30,14},{2,3},{3,2},{4,5},{5,4},{6,7},{7,6}... | collective-permute-start | bytes 294920 | tf_op jit(solution)/shard_map/ppermute | solution.py:693
  27.9 6.1 %collective-permute-done.5.refs_2_.refs_5_ = f32[11,16,128]{2,1,0:T(8,128)S(1)} collective-permute-done((f32[11,16,128]{2,1,0:T(8,128)S(1)}, f32[11,16,128]{2,1,0:T(8,128)S(1)}, u32[]{:S(2)}, u32[]{:S(2)}) %collective-permute-start.5) | collective-permute-done | bytes 90144 | tf_op jit(solution)/shard_map/ppermute | solution.py:679
  33.9 0.3 moments.1
  34.2 0.1 collective-permute-start.7
  34.3 1.3 %collective-permute-done.7.refs_4_ = f32[11,16,128]{2,1,0:T(8,128)S(1)} collective-permute-done((f32[11,16,128]{2,1,0:T(8,128)S(1)}, f32[11,16,128]{2,1,0:T(8,128)S(1)}, u32[]{:S(2)}, u32[]{:S(2)}) %collective-permute-start.7) | collective-permute-done | bytes 90144 | tf_op jit(solution)/shard_map/ppermute | solution.py:679
  35.6 0.9 %place.1 = (f32[8,4096]{1,0:T(8,128)}, f32[3,8,4096]{2,1,0:T(8,128)}) custom-call(s32[4,8,128]{2,1,0:T(8,128)S(1)} %get-tuple-element.35.refs_0_, f32[8,4096]{1,0:T(8,128)S(1)} %get-tuple-element.47.refs_1_, f32[3,8,4096]{2,1,0:T(8,128)S(1)} %get-tuple-element.48.refs_2_, f32[3,16,128]{2,1,0:T(8,128)S(1)} %get-tuple-element.44.refs_0_.refs_3_, ...), custom_call_target="tpu_custom_call" | custom-call | flops 2000000 | bytes 1000000 | tf_op jit(solution)/shard_map/place/pallas_call | solution.py:732
  (9 shorter events, 0.0 us)
Async XLA Ops:
  0.6 5.9 %copy-start = (f32[27,16,16,128]{3,2,1,0:T(8,128)S(1)}, f32[27,16,16,128]{3,2,1,0:T(8,128)}, u32[]{:S(2)}) copy-start(f32[27,16,16,128]{3,2,1,0:T(8,128)} %refs_1_.5) | copy-start | bytes 10616836
  0.6 1.3 %copy-start.1 = (s32[1024]{0:T(1024)S(1)}, s32[1024]{0:T(1024)}, u32[]{:S(2)}) copy-start(s32[1024]{0:T(1024)} %param.4) | copy-start | bytes 12292
  2.2 6.6 %collective-permute-start = (f32[9,16,128]{2,1,0:T(8,128)S(1)}, f32[9,16,128]{2,1,0:T(8,128)S(1)}, u32[]{:S(2)}, u32[]{:S(2)}) collective-permute-start(f32[9,16,128]{2,1,0:T(8,128)S(1)} %get-tuple-element.31), channel_id=1, source_target_pairs={{0,1},{2,3},{4,5},{6,7},{8,9},{10,11},{12,13},{14,15},{16,17},{18,... | collective-permute-start | bytes 221192 | tf_op jit(solution)/shard_map/ppermute | solution.py:679
  2.3 6.5 %collective-permute-start.1 = (f32[9,16,128]{2,1,0:T(8,128)S(1)}, f32[9,16,128]{2,1,0:T(8,128)S(1)}, u32[]{:S(2)}, u32[]{:S(2)}) collective-permute-start(f32[9,16,128]{2,1,0:T(8,128)S(1)} %get-tuple-element.32), channel_id=1, source_target_pairs={{1,2},{3,4},{5,6},{7,8},{9,10},{11,12},{13,14},{15,0},{17,18},{19,... | collective-permute-start | bytes 221192 | tf_op jit(solution)/shard_map/ppermute | solution.py:679
  8.8 3.9 %copy-start.2 = (s32[8]{0:T(128)S(1)}, s32[8]{0:T(128)}, u32[]{:S(2)}) copy-start(s32[8]{0:T(128)} %refs_0_.3) | copy-start | bytes 100
  9.0 11.7 %collective-permute-start.2 = (f32[25,16,128]{2,1,0:T(8,128)S(1)}, f32[25,16,128]{2,1,0:T(8,128)S(1)}, u32[]{:S(2)}, u32[]{:S(2)}) collective-permute-start(f32[25,16,128]{2,1,0:T(8,128)S(1)} %get-tuple-element.34.refs_7_), channel_id=1, source_target_pairs={{0,16},{32,48},{64,80},{96,112},{1,17},{33,49},{65,81},{97,113},{2... | collective-permute-start | bytes 614408 | tf_op jit(solution)/shard_map/ppermute | solution.py:679
  12.7 8.1 %collective-permute-start.3 = (f32[24,16,128]{2,1,0:T(8,128)S(1)}, f32[24,16,128]{2,1,0:T(8,128)S(1)}, u32[]{:S(2)}, u32[]{:S(2)}) collective-permute-start(f32[24,16,128]{2,1,0:T(8,128)S(1)} %get-tuple-element.37), channel_id=1, source_target_pairs={{16,32},{48,64},{80,96},{112,0},{17,33},{49,65},{81,97},{113,1},{1... | collective-permute-start | bytes 589832 | tf_op jit(solution)/shard_map/ppermute | solution.py:679
  21.4 1.3 %collective-permute-start.4 = (f32[6,16,128]{2,1,0:T(8,128)S(1)}, f32[6,16,128]{2,1,0:T(8,128)S(1)}, u32[]{:S(2)}, u32[]{:S(2)}) collective-permute-start(f32[6,16,128]{2,1,0:T(8,128)S(1)} %get-tuple-element.42), channel_id=1, source_target_pairs={{0,1},{2,3},{4,5},{6,7},{8,9},{10,11},{12,13},{14,15},{16,17},{18,... | collective-permute-start | bytes 147464 | tf_op jit(solution)/shard_map/ppermute | solution.py:679
  23.0 11.0 %collective-permute-start.6 = (f32[12,16,128]{2,1,0:T(8,128)S(1)}, f32[12,16,128]{2,1,0:T(8,128)S(1)}, u32[]{:S(2)}, u32[]{:S(2)}) collective-permute-start(f32[12,16,128]{2,1,0:T(8,128)S(1)} %get-tuple-element.46), channel_id=1, source_target_pairs={{15,16},{16,15},{1,17},{30,14},{2,3},{3,2},{4,5},{5,4},{6,7},{7,6}... | collective-permute-start | bytes 294920 | tf_op jit(solution)/shard_map/ppermute | solution.py:693
  27.8 6.1 %collective-permute-start.5 = (f32[11,16,128]{2,1,0:T(8,128)S(1)}, f32[11,16,128]{2,1,0:T(8,128)S(1)}, u32[]{:S(2)}, u32[]{:S(2)}) collective-permute-start(f32[11,16,128]{2,1,0:T(8,128)S(1)} %join.1), channel_id=1, source_target_pairs={{1,2},{3,4},{5,6},{7,8},{9,10},{11,12},{13,14},{15,0},{17,18},{19,... | collective-permute-start | bytes 270344 | tf_op jit(solution)/shard_map/ppermute | solution.py:679
  34.2 1.4 %collective-permute-start.7 = (f32[11,16,128]{2,1,0:T(8,128)S(1)}, f32[11,16,128]{2,1,0:T(8,128)S(1)}, u32[]{:S(2)}, u32[]{:S(2)}) collective-permute-start(f32[11,16,128]{2,1,0:T(8,128)S(1)} %get-tuple-element.49), channel_id=1, source_target_pairs={{0,1},{2,3},{4,5},{6,7},{8,9},{10,11},{12,13},{14,15},{16,17},{18,... | collective-permute-start | bytes 270344 | tf_op jit(solution)/shard_map/ppermute | solution.py:679

commit v9 on v8

--- a/solution.py
+++ b/solution.py
@@ -779,7 +779,7 @@
     )
     part, block, pay_w = run(
         functools.partial(pack_kernel), moves, inner, outer, got_a,
-        outs=[real(8, nx * ROWS, nz), real(8, nx, nz), real(12, nx, nz)], specs="vvvv",
+        outs=[real(8, nx * ROWS, nz), real(8, nx, nz), real(8, nx, nz)], specs="vvvv",
     )
     got_w = swap_ends(pay_w)
     (pay_b,) = run(

time: 37.3 us -> 37.3 us (level)
  the two profiles are of different devices: /device:TPU:16 before, /device:TPU:1 now
where the time goes in v9:
time: 37.3 us; the launch traced here: 37.2 us
  starting transfers between devices  21 us (56%)
  Pallas kernels  12.5 us (34%)
  waiting for transfers between devices  2.99 us (8%)
  between operations  0.75 us (2%)
    ppermute x7, starting transfers between devices, swap(): return lax.ppermute(value, ('bx', 'by'), pairs)  18.6 us
    pallas_call x11, Pallas kernels, run(): call(body, outs, specs, scratch, kernel.func.__name__[:-7], work, limit,...  12.5 us
    ppermute x1, starting transfers between devices, swap_ends(): return lax.ppermute(value, ('bx', 'by'), pairs)  2.4 us
    ppermute x7, waiting for transfers between devices, swap(): return lax.ppermute(value, ('bx', 'by'), pairs)  1.65 us
    ppermute x1, waiting for transfers between devices, swap_ends(): return lax.ppermute(value, ('bx', 'by'), pairs)  1.33 us
  transfers between devices with their start and end apart: 8, of which 3 were waited for; matrix products, arithmetic and copies ran while one was open for 0% of the time, Pallas kernels for 23%

profile of v9, /device:TPU:1, one launch (start us, length us, event | category | flops | bytes accessed | tf_op | source)
XLA Modules:
  0.0 37.2 jit_solution(8812615320071699254)
XLA Ops:
  0.6 1.2 %fetch.1 = (f32[27,16,128]{2,1,0:T(8,128)S(1)}, f32[27,16,128]{2,1,0:T(8,128)S(1)}) custom-call(f32[27,16,16,128]{3,2,1,0:T(8,128)} %refs_1_.5), custom_call_target="tpu_custom_call" | custom-call | flops 2000000 | bytes 1000000 | tf_op jit(solution)/shard_map/fetch/pallas_call | solution.py:732
  1.9 0.3 face.1
  2.2 1.5 %collective-permute-start = (f32[9,16,128]{2,1,0:T(8,128)S(1)}, f32[9,16,128]{2,1,0:T(8,128)S(1)}, u32[]{:S(2)}, u32[]{:S(2)}) collective-permute-start(f32[9,16,128]{2,1,0:T(8,128)S(1)} %get-tuple-element.31), channel_id=1, source_target_pairs={{0,1},{2,3},{4,5},{6,7},{8,9},{10,11},{12,13},{14,15},{16,17},{18,... | collective-permute-start | bytes 221192 | tf_op jit(solution)/shard_map/ppermute | solution.py:679
  3.7 1.7 %collective-permute-start.1 = (f32[9,16,128]{2,1,0:T(8,128)S(1)}, f32[9,16,128]{2,1,0:T(8,128)S(1)}, u32[]{:S(2)}, u32[]{:S(2)}) collective-permute-start(f32[9,16,128]{2,1,0:T(8,128)S(1)} %get-tuple-element.32), channel_id=1, source_target_pairs={{1,2},{3,4},{5,6},{7,8},{9,10},{11,12},{13,14},{15,0},{17,18},{19,... | collective-permute-start | bytes 221192 | tf_op jit(solution)/shard_map/ppermute | solution.py:679
  5.4 2.3 %first.1 = (f32[5,3,3,16,128]{4,3,2,1,0:T(8,128)S(1)}, f32[27,16,16,128]{3,2,1,0:T(8,128)S(1)}, f32[2,9,16,128]{3,2,1,0:T(8,128)S(1)}) custom-call(s32[3,3,8,128]{3,2,1,0:T(8,128)S(1)} %get-tuple-element.28.refs_0_.refs_1_, f32[27,16,16,128]{3,2,1,0:T(8,128)S(1)} %copy-done), custom_call_target="tpu_custom_call" | custom-call | flops 6000000 | bytes 3000000 | tf_op jit(solution)/shard_map/first/pallas_call | solution.py:732
  7.7 0.0 collective-permute-done.refs_4_.refs_5_
  7.7 0.0 copy-start.2
  7.7 0.2 side.1
  7.9 3.5 %collective-permute-start.2 = (f32[25,16,128]{2,1,0:T(8,128)S(1)}, f32[25,16,128]{2,1,0:T(8,128)S(1)}, u32[]{:S(2)}, u32[]{:S(2)}) collective-permute-start(f32[25,16,128]{2,1,0:T(8,128)S(1)} %get-tuple-element.34.refs_7_), channel_id=1, source_target_pairs={{0,16},{32,48},{64,80},{96,112},{1,17},{33,49},{65,81},{97,113},{2... | collective-permute-start | bytes 614408 | tf_op jit(solution)/shard_map/ppermute | solution.py:679
  11.4 2.5 %collective-permute-start.3 = (f32[24,16,128]{2,1,0:T(8,128)S(1)}, f32[24,16,128]{2,1,0:T(8,128)S(1)}, u32[]{:S(2)}, u32[]{:S(2)}) collective-permute-start(f32[24,16,128]{2,1,0:T(8,128)S(1)} %get-tuple-element.37), channel_id=1, source_target_pairs={{16,32},{48,64},{80,96},{112,0},{17,33},{49,65},{81,97},{113,1},{1... | collective-permute-start | bytes 589832 | tf_op jit(solution)/shard_map/ppermute | solution.py:679
  14.0 6.2 %inner.1 = (f32[3,3,2,16,16,128]{5,4,3,2,1,0:T(8,128)S(1)}, f32[8,128,128]{2,1,0:T(8,128)S(1)}, f32[3,16,128]{2,1,0:T(8,128)S(1)}, f32[3,16,128]{2,1,0:T(8,128)S(1)}, s32[4,8,128]{2,1,0:T(8,128)S(1)}) custom-call(s32[8]{0:T(128)S(1)} %copy-done.2, s32[3,3,8,128]{3,2,1,0:T(8,128)S(1)} %get-tuple-element.28.refs_0_.refs_1_, f32[27,16,16,128]{3,2,1,0:T(8,128)S(1)} %copy-done, ...), custom_call_target="tpu_custom_call" | custom-call | flops 20000000 | bytes 10000000 | tf_op jit(solution)/shard_map/inner/pallas_call | solution.py:732
  20.2 0.0 collective-permute-done.3.refs_7_
  20.2 0.6 %outer.1 = (f32[8,32,128]{2,1,0:T(8,128)S(1)}, f32[6,16,128]{2,1,0:T(8,128)S(1)}, f32[3,16,128]{2,1,0:T(8,128)S(1)}) custom-call(s32[3,3,8,128]{3,2,1,0:T(8,128)S(1)} %get-tuple-element.28.refs_0_.refs_1_, f32[27,16,16,128]{3,2,1,0:T(8,128)S(1)} %copy-done, f32[27,16,16,128]{3,2,1,0:T(8,128)S(1)} %get-tuple-element.29.refs_2_.refs_3_, ...), custom_call_target="tpu_custom_call" | custom-call | flops 2000000 | bytes 1000000 | tf_op jit(solution)/shard_map/outer/pallas_call | solution.py:732
  20.8 3.4 %collective-permute-start.4 = (f32[6,16,128]{2,1,0:T(8,128)S(1)}, f32[6,16,128]{2,1,0:T(8,128)S(1)}, u32[]{:S(2)}, u32[]{:S(2)}) collective-permute-start(f32[6,16,128]{2,1,0:T(8,128)S(1)} %get-tuple-element.42), channel_id=1, source_target_pairs={{0,1},{2,3},{4,5},{6,7},{8,9},{10,11},{12,13},{14,15},{16,17},{18,... | collective-permute-start | bytes 147464 | tf_op jit(solution)/shard_map/ppermute | solution.py:679
  24.2 0.2 turn.1.refs_2_
  24.4 0.7 %collective-permute-done.4.refs_3_ = f32[6,16,128]{2,1,0:T(8,128)S(1)} collective-permute-done((f32[6,16,128]{2,1,0:T(8,128)S(1)}, f32[6,16,128]{2,1,0:T(8,128)S(1)}, u32[]{:S(2)}, u32[]{:S(2)}) %collective-permute-start.4) | collective-permute-done | bytes 49184 | tf_op jit(solution)/shard_map/ppermute | solution.py:679
  25.1 0.2 pack.1
  25.3 0.7 %collective-permute-start.5 = (f32[11,16,128]{2,1,0:T(8,128)S(1)}, f32[11,16,128]{2,1,0:T(8,128)S(1)}, u32[]{:S(2)}, u32[]{:S(2)}) collective-permute-start(f32[11,16,128]{2,1,0:T(8,128)S(1)} %join.1), channel_id=1, source_target_pairs={{1,2},{3,4},{5,6},{7,8},{9,10},{11,12},{13,14},{15,0},{17,18},{19,... | collective-permute-start | bytes 270344 | tf_op jit(solution)/shard_map/ppermute | solution.py:679
  26.0 2.4 %collective-permute-start.6 = (f32[8,16,128]{2,1,0:T(8,128)S(1)}, f32[8,16,128]{2,1,0:T(8,128)S(1)}, u32[]{:S(2)}, u32[]{:S(2)}) collective-permute-start(f32[8,16,128]{2,1,0:T(8,128)S(1)} %get-tuple-element.46), channel_id=1, source_target_pairs={{15,16},{16,15},{1,17},{30,14},{2,3},{3,2},{4,5},{5,4},{6,7},{7,6}... | collective-permute-start | bytes 196616 | tf_op jit(solution)/shard_map/ppermute | solution.py:693
  28.4 1.3 %collective-permute-done.6.refs_3_.refs_6_ = f32[8,16,128]{2,1,0:T(8,128)S(1)} collective-permute-done((f32[8,16,128]{2,1,0:T(8,128)S(1)}, f32[8,16,128]{2,1,0:T(8,128)S(1)}, u32[]{:S(2)}, u32[]{:S(2)}) %collective-permute-start.6) | collective-permute-done | bytes 65568 | tf_op jit(solution)/shard_map/ppermute | solution.py:693
  29.7 0.3 moments.1
  30.0 5.3 %collective-permute-start.7 = (f32[11,16,128]{2,1,0:T(8,128)S(1)}, f32[11,16,128]{2,1,0:T(8,128)S(1)}, u32[]{:S(2)}, u32[]{:S(2)}) collective-permute-start(f32[11,16,128]{2,1,0:T(8,128)S(1)} %get-tuple-element.49), channel_id=1, source_target_pairs={{0,1},{2,3},{4,5},{6,7},{8,9},{10,11},{12,13},{14,15},{16,17},{18,... | collective-permute-start | bytes 270344 | tf_op jit(solution)/shard_map/ppermute | solution.py:679
  35.4 0.9 %collective-permute-done.7.refs_4_ = f32[11,16,128]{2,1,0:T(8,128)S(1)} collective-permute-done((f32[11,16,128]{2,1,0:T(8,128)S(1)}, f32[11,16,128]{2,1,0:T(8,128)S(1)}, u32[]{:S(2)}, u32[]{:S(2)}) %collective-permute-start.7) | collective-permute-done | bytes 90144 | tf_op jit(solution)/shard_map/ppermute | solution.py:679
  36.3 0.9 %place.1 = (f32[8,4096]{1,0:T(8,128)}, f32[3,8,4096]{2,1,0:T(8,128)}) custom-call(s32[4,8,128]{2,1,0:T(8,128)S(1)} %get-tuple-element.35.refs_0_, f32[8,4096]{1,0:T(8,128)S(1)} %get-tuple-element.47.refs_1_, f32[3,8,4096]{2,1,0:T(8,128)S(1)} %get-tuple-element.48.refs_2_, f32[3,16,128]{2,1,0:T(8,128)S(1)} %get-tuple-element.44.refs_0_.refs_3_, ...), custom_call_target="tpu_custom_call" | custom-call | flops 2000000 | bytes 1000000 | tf_op jit(solution)/shard_map/place/pallas_call | solution.py:732
  (9 shorter events, 0.0 us)
Async XLA Ops:
  0.6 4.8 %copy-start = (f32[27,16,16,128]{3,2,1,0:T(8,128)S(1)}, f32[27,16,16,128]{3,2,1,0:T(8,128)}, u32[]{:S(2)}) copy-start(f32[27,16,16,128]{3,2,1,0:T(8,128)} %refs_1_.5) | copy-start | bytes 10616836
  0.6 1.3 %copy-start.1 = (s32[1024]{0:T(1024)S(1)}, s32[1024]{0:T(1024)}, u32[]{:S(2)}) copy-start(s32[1024]{0:T(1024)} %param.4) | copy-start | bytes 12292
  2.2 5.5 %collective-permute-start = (f32[9,16,128]{2,1,0:T(8,128)S(1)}, f32[9,16,128]{2,1,0:T(8,128)S(1)}, u32[]{:S(2)}, u32[]{:S(2)}) collective-permute-start(f32[9,16,128]{2,1,0:T(8,128)S(1)} %get-tuple-element.31), channel_id=1, source_target_pairs={{0,1},{2,3},{4,5},{6,7},{8,9},{10,11},{12,13},{14,15},{16,17},{18,... | collective-permute-start | bytes 221192 | tf_op jit(solution)/shard_map/ppermute | solution.py:679
  3.7 4.0 %collective-permute-start.1 = (f32[9,16,128]{2,1,0:T(8,128)S(1)}, f32[9,16,128]{2,1,0:T(8,128)S(1)}, u32[]{:S(2)}, u32[]{:S(2)}) collective-permute-start(f32[9,16,128]{2,1,0:T(8,128)S(1)} %get-tuple-element.32), channel_id=1, source_target_pairs={{1,2},{3,4},{5,6},{7,8},{9,10},{11,12},{13,14},{15,0},{17,18},{19,... | collective-permute-start | bytes 221192 | tf_op jit(solution)/shard_map/ppermute | solution.py:679
  7.7 6.2 %copy-start.2 = (s32[8]{0:T(128)S(1)}, s32[8]{0:T(128)}, u32[]{:S(2)}) copy-start(s32[8]{0:T(128)} %refs_0_.3) | copy-start | bytes 100
  7.9 12.3 %collective-permute-start.2 = (f32[25,16,128]{2,1,0:T(8,128)S(1)}, f32[25,16,128]{2,1,0:T(8,128)S(1)}, u32[]{:S(2)}, u32[]{:S(2)}) collective-permute-start(f32[25,16,128]{2,1,0:T(8,128)S(1)} %get-tuple-element.34.refs_7_), channel_id=1, source_target_pairs={{0,16},{32,48},{64,80},{96,112},{1,17},{33,49},{65,81},{97,113},{2... | collective-permute-start | bytes 614408 | tf_op jit(solution)/shard_map/ppermute | solution.py:679
  11.4 8.8 %collective-permute-start.3 = (f32[24,16,128]{2,1,0:T(8,128)S(1)}, f32[24,16,128]{2,1,0:T(8,128)S(1)}, u32[]{:S(2)}, u32[]{:S(2)}) collective-permute-start(f32[24,16,128]{2,1,0:T(8,128)S(1)} %get-tuple-element.37), channel_id=1, source_target_pairs={{16,32},{48,64},{80,96},{112,0},{17,33},{49,65},{81,97},{113,1},{1... | collective-permute-start | bytes 589832 | tf_op jit(solution)/shard_map/ppermute | solution.py:679
  20.8 4.2 %collective-permute-start.4 = (f32[6,16,128]{2,1,0:T(8,128)S(1)}, f32[6,16,128]{2,1,0:T(8,128)S(1)}, u32[]{:S(2)}, u32[]{:S(2)}) collective-permute-start(f32[6,16,128]{2,1,0:T(8,128)S(1)} %get-tuple-element.42), channel_id=1, source_target_pairs={{0,1},{2,3},{4,5},{6,7},{8,9},{10,11},{12,13},{14,15},{16,17},{18,... | collective-permute-start | bytes 147464 | tf_op jit(solution)/shard_map/ppermute | solution.py:679
  25.3 4.4 %collective-permute-start.5 = (f32[11,16,128]{2,1,0:T(8,128)S(1)}, f32[11,16,128]{2,1,0:T(8,128)S(1)}, u32[]{:S(2)}, u32[]{:S(2)}) collective-permute-start(f32[11,16,128]{2,1,0:T(8,128)S(1)} %join.1), channel_id=1, source_target_pairs={{1,2},{3,4},{5,6},{7,8},{9,10},{11,12},{13,14},{15,0},{17,18},{19,... | collective-permute-start | bytes 270344 | tf_op jit(solution)/shard_map/ppermute | solution.py:679
  26.0 3.7 %collective-permute-start.6 = (f32[8,16,128]{2,1,0:T(8,128)S(1)}, f32[8,16,128]{2,1,0:T(8,128)S(1)}, u32[]{:S(2)}, u32[]{:S(2)}) collective-permute-start(f32[8,16,128]{2,1,0:T(8,128)S(1)} %get-tuple-element.46), channel_id=1, source_target_pairs={{15,16},{16,15},{1,17},{30,14},{2,3},{3,2},{4,5},{5,4},{6,7},{7,6}... | collective-permute-start | bytes 196616 | tf_op jit(solution)/shard_map/ppermute | solution.py:693
  30.0 6.3 %collective-permute-start.7 = (f32[11,16,128]{2,1,0:T(8,128)S(1)}, f32[11,16,128]{2,1,0:T(8,128)S(1)}, u32[]{:S(2)}, u32[]{:S(2)}) collective-permute-start(f32[11,16,128]{2,1,0:T(8,128)S(1)} %get-tuple-element.49), channel_id=1, source_target_pairs={{0,1},{2,3},{4,5},{6,7},{8,9},{10,11},{12,13},{14,15},{16,17},{18,... | collective-permute-start | bytes 270344 | tf_op jit(solution)/shard_map/ppermute | solution.py:679
